TPU v7x, 128 devices: a whole 4x4x4 slice. The times are simulated.
128 devices in a mesh: row: 16 (over y, x), col: 8 (over z, core).
Axes of the slice: x: 4, y: 4, z: 4, core: 2. Of those that a mesh axis runs over, the one named last changes fastest.
Arguments:
- features: bfloat16 [131072, 128], P(('col', 'row')), may hold values from -6 to 6
- weight: bfloat16 [128, 128], replicated, may hold values from -0.5 to 0.5
- cotangent: bfloat16 [131072, 128], P(('row', 'col')), may hold values from -0.015625 to 0.015625
- tile_row: int32 [16, 8, 256], P('row', 'col'), may hold values from 0 to 31
- tile_col: int32 [16, 8, 256], P('row', 'col'), may hold values from 0 to 63
- nnz_row: int32 [16, 8, 256, 256], P('row', 'col'), may hold values from 0 to 255
- nnz_col: int32 [16, 8, 256, 256], P('row', 'col'), may hold values from 0 to 255
- edge_value: bfloat16 [16, 8, 256, 256], P('row', 'col'), may hold values from 0.019897461 to 0.19921875
- tile_count: int32 [16, 8, 256], P('row', 'col'), may hold values from 0 to 256, as said below
Outputs:
- node_out: bfloat16 [131072, 128], P(('row', 'col'))
- weight_grad: float32 [128, 128], replicated
Inputs may be any that keep to these rules, and one draw needn't show every extreme that they name: `tile_count`: every device's block has a tile holding 256 live slots.
All inputs are finite; a program needn't handle non-finite values.
Results may differ from a plain program's by a relative error of at most 0.0051.
Values may be sent and summed in bfloat16 or wider, within the bound.
No kernel may reach another device: no remote copies, remote signals or barrier semaphores. Data moves between devices by JAX's collectives and lax.ppermute only.
A program may use at most 192 MiB of HBM per device.

v0:
```python
import jax
import jax.numpy as jnp
from jax import lax
from jax.sharding import PartitionSpec as P


def tile_mats(row_idx, col_idx, value_rows, count_rows):
    group, slots = row_idx.shape
    live = jnp.arange(slots, dtype=jnp.int32)[None, :] < count_rows[:, None]
    values = jnp.where(live, value_rows.astype(jnp.float32), jnp.float32(0.0))
    flat_idx = row_idx * 256 + col_idx
    flat = jnp.zeros((group, 65536), jnp.float32)
    flat = flat.at[jnp.arange(group, dtype=jnp.int32)[:, None], flat_idx].add(values)
    return flat.reshape(group, 256, 256).astype(jnp.bfloat16)


def grouped(array, group):
    return array.reshape((array.shape[0] // group, group) + array.shape[1:])


def build_tiles(nrow, ncol, values, counts):
    total = nrow.shape[0]
    group = min(32, total)

    def one_group(item):
        return tile_mats(item[0], item[1], item[2], item[3])

    built = lax.map(
        one_group,
        (
            grouped(nrow, group),
            grouped(ncol, group),
            grouped(values, group),
            grouped(counts, group),
        ),
    )
    return built.reshape(total, 256, 256)


def forward_block(panel, tiles, rows, cols, row_tiles):
    total = rows.shape[0]
    group = min(32, total)
    width = panel.shape[1]
    blocks = panel.reshape(-1, 256, width)
    targets = jnp.arange(row_tiles, dtype=jnp.int32)

    def forward_step(carry, item):
        row_ids, col_ids, mats = item
        picked = jnp.take(blocks, col_ids, axis=0)
        prod = jnp.einsum("gij,gjf->gif", mats, picked, preferred_element_type=jnp.float32)
        onehot = (row_ids[:, None] == targets[None, :]).astype(jnp.float32)
        return (
            carry + jnp.einsum("gk,gif->kif", onehot, prod, precision=lax.Precision.HIGHEST),
            None,
        )

    init = jnp.zeros((row_tiles, 256, width), jnp.float32)
    items = (grouped(rows, group), grouped(cols, group), grouped(tiles, group))
    out, unused = lax.scan(forward_step, init, items)
    return out.reshape(row_tiles * 256, width)


def backward_block(grads, tiles, rows, cols, col_tiles):
    total = rows.shape[0]
    group = min(32, total)
    width = grads.shape[1]
    blocks = grads.reshape(-1, 256, width)
    targets = jnp.arange(col_tiles, dtype=jnp.int32)

    def backward_step(carry, item):
        row_ids, col_ids, mats = item
        picked = jnp.take(blocks, row_ids, axis=0)
        prod = jnp.einsum("gij,gif->gjf", mats, picked, preferred_element_type=jnp.float32)
        onehot = (col_ids[:, None] == targets[None, :]).astype(jnp.float32)
        return (
            carry + jnp.einsum("gk,gif->kif", onehot, prod, precision=lax.Precision.HIGHEST),
            None,
        )

    init = jnp.zeros((col_tiles, 256, width), jnp.float32)
    items = (grouped(rows, group), grouped(cols, group), grouped(tiles, group))
    out, unused = lax.scan(backward_step, init, items)
    return out.reshape(col_tiles * 256, width)


def silu_slope(pre):
    sig = jax.nn.sigmoid(pre)
    return sig * (1.0 + pre * (1.0 - sig))


def body(features, weight, cotangent, tile_row, tile_col, nnz_row, nnz_col, edge_value, tile_count):
    slot_count = tile_row.shape[2]
    rows = tile_row.reshape(slot_count)
    cols = tile_col.reshape(slot_count)
    nrow = nnz_row.reshape(slot_count, -1)
    ncol = nnz_col.reshape(slot_count, -1)
    values = edge_value.reshape(slot_count, -1)
    counts = tile_count.reshape(slot_count)
    tiles = build_tiles(nrow, ncol, values, counts)
    share = cotangent.shape[0]
    row_len = share * lax.axis_size("col")
    row_tiles = row_len // 256
    local_proj = jnp.dot(features, weight, preferred_element_type=jnp.float32).astype(jnp.bfloat16)
    panel = lax.all_gather(local_proj, "row", axis=0, tiled=True)
    col_tiles = panel.shape[0] // 256
    partial_value = forward_block(panel, tiles, rows, cols, row_tiles)
    pre_share = lax.psum_scatter(partial_value, "col", scatter_dimension=0, tiled=True)
    node_out = jax.nn.silu(pre_share).astype(jnp.bfloat16)
    grad_share = (cotangent.astype(jnp.float32) * silu_slope(pre_share)).astype(jnp.bfloat16)
    grad_rows = lax.all_gather(grad_share, "col", axis=0, tiled=True)
    col_partial = backward_block(grad_rows, tiles, rows, cols, col_tiles)
    col_grad = lax.psum_scatter(col_partial, "row", scatter_dimension=0, tiled=True)
    partial_w = jnp.dot(features.astype(jnp.float32).T, col_grad, precision=lax.Precision.HIGHEST)
    weight_grad = lax.psum(partial_w, ("row", "col"))
    return (node_out, weight_grad)


def solution(mesh):
    placed = (
        P(("col", "row"), None),
        P(),
        P(("row", "col"), None),
        P("row", "col", None),
        P("row", "col", None),
        P("row", "col", None, None),
        P("row", "col", None, None),
        P("row", "col", None, None),
        P("row", "col", None),
    )
    return jax.shard_map(
        body, mesh=mesh, in_specs=placed, out_specs=(P(("row", "col"), None), P()), check_vma=False
    )
```

profile of v0, /device:TPU:0, one launch (start us, length us, event | category | flops | bytes accessed | tf_op | source)
XLA Modules:
  0.0 1196.3 jit_solution(7998629950292407888)
XLA Ops:
  14.6 535.2 %while.32 = (s32[]{:T(128)}, bf16[8,32,256,256]{3,2,1,0:T(8,128)(2,1)}, s32[8,32,256]{2,1,0:T(8,128)}, s32[8,32,256]{2,1,0:T(8,128)}, s32[8,32]{1,0:T(8,128)S(1)...) while((s32[]{:T(128)}, bf16[8,32,256,256]{3,2,1,0:T(8,128)(2,1)}, ...), condition=%wide.region_2.3_spmd, body=%wide.region_0.2_spmd.sunk | while | flops 2293762 | bytes 38306820 | solution.py:28
  17.7 46.9 %scatter_custom_fusion.5 = f32[2097152]{0:T(1024)} fusion(s32[8192]{0:T(1024)S(1)} %bitcast.96, f32[8192]{0:T(1024)S(1)} %bitcast.97, f32[]{:T(128)} %constant.47.clone.2..sunk), kind=kCustom, calls=%fused_computation.5.clone.1 | custom fusion | flops 8192 | bytes 8388612 | tf_op jit(solution)/shard_map/while
  84.6 46.9 %scatter_custom_fusion.5 = f32[2097152]{0:T(1024)} fusion(s32[8192]{0:T(1024)S(1)} %bitcast.96, f32[8192]{0:T(1024)S(1)} %bitcast.97, f32[]{:T(128)} %constant.47.clone.2..sunk), kind=kCustom, calls=%fused_computation.5.clone.1 | custom fusion | flops 8192 | bytes 8388612 | tf_op jit(solution)/shard_map/while
  151.5 46.9 %scatter_custom_fusion.5 = f32[2097152]{0:T(1024)} fusion(s32[8192]{0:T(1024)S(1)} %bitcast.96, f32[8192]{0:T(1024)S(1)} %bitcast.97, f32[]{:T(128)} %constant.47.clone.2..sunk), kind=kCustom, calls=%fused_computation.5.clone.1 | custom fusion | flops 8192 | bytes 8388612 | tf_op jit(solution)/shard_map/while
  218.4 46.9 %scatter_custom_fusion.5 = f32[2097152]{0:T(1024)} fusion(s32[8192]{0:T(1024)S(1)} %bitcast.96, f32[8192]{0:T(1024)S(1)} %bitcast.97, f32[]{:T(128)} %constant.47.clone.2..sunk), kind=kCustom, calls=%fused_computation.5.clone.1 | custom fusion | flops 8192 | bytes 8388612 | tf_op jit(solution)/shard_map/while
  285.3 46.9 %scatter_custom_fusion.5 = f32[2097152]{0:T(1024)} fusion(s32[8192]{0:T(1024)S(1)} %bitcast.96, f32[8192]{0:T(1024)S(1)} %bitcast.97, f32[]{:T(128)} %constant.47.clone.2..sunk), kind=kCustom, calls=%fused_computation.5.clone.1 | custom fusion | flops 8192 | bytes 8388612 | tf_op jit(solution)/shard_map/while
  352.2 46.9 %scatter_custom_fusion.5 = f32[2097152]{0:T(1024)} fusion(s32[8192]{0:T(1024)S(1)} %bitcast.96, f32[8192]{0:T(1024)S(1)} %bitcast.97, f32[]{:T(128)} %constant.47.clone.2..sunk), kind=kCustom, calls=%fused_computation.5.clone.1 | custom fusion | flops 8192 | bytes 8388612 | tf_op jit(solution)/shard_map/while
  419.1 46.9 %scatter_custom_fusion.5 = f32[2097152]{0:T(1024)} fusion(s32[8192]{0:T(1024)S(1)} %bitcast.96, f32[8192]{0:T(1024)S(1)} %bitcast.97, f32[]{:T(128)} %constant.47.clone.2..sunk), kind=kCustom, calls=%fused_computation.5.clone.1 | custom fusion | flops 8192 | bytes 8388612 | tf_op jit(solution)/shard_map/while
  486.0 46.9 %scatter_custom_fusion.5 = f32[2097152]{0:T(1024)} fusion(s32[8192]{0:T(1024)S(1)} %bitcast.96, f32[8192]{0:T(1024)S(1)} %bitcast.97, f32[]{:T(128)} %constant.47.clone.2..sunk), kind=kCustom, calls=%fused_computation.5.clone.1 | custom fusion | flops 8192 | bytes 8388612 | tf_op jit(solution)/shard_map/while
  549.8 150.0 %while.33 = (s32[]{:T(128)}, f32[32,256,128]{2,0,1:T(8,128)}, s32[8,32]{1,0:T(8,128)S(1)}, bf16[8,32,256,256]{3,2,1,0:T(8,128)(2,1)}, s32[8,32]{1,0:T(8,128)S(1)...) while((s32[]{:T(128)}, f32[32,256,128]{2,0,1:T(8,128)}, s32[8,32]{1,0:T(8,128)S(1)}, ...), condition=%wide.region_4.5_spmd.clone, body=%wide.region_3.4_spmd.clone.sunk | while | flops 942672192 | bytes 27268780 | solution.py:59
  706.5 40.8 %reduce-scatter.3.cloned.1.call-done = f32[1024,128]{1,0:T(8,128)} async-done(((f32[8192,128]{1,0:T(8,128)}), f32[1024,128]{1,0:T(8,128)}) %reduce-scatter.3.cloned.1.call-update) | async-done | bytes 524304 | tf_op jit(solution)/shard_map/reduce_scatter | solution.py:107
  749.4 24.3 %all-gather.5.cloned.1.call-done = bf16[8192,128]{1,0:T(8,128)(2,1)} async-done(((bf16[1024,128]{1,0:T(8,128)(2,1)}), bf16[8192,128]{1,0:T(8,128)(2,1)}) %all-gather.5.cloned.1.call-update) | async-done | bytes 2097168 | tf_op jit(solution)/shard_map/all_gather | solution.py:110
  773.7 177.3 %while.34 = (s32[]{:T(128)}, f32[64,256,128]{2,0,1:T(8,128)}, s32[8,32]{1,0:T(8,128)S(1)}, bf16[8,32,256,256]{3,2,1,0:T(8,128)(2,1)}, s32[8,32]{1,0:T(8,128)S(1)...) while((s32[]{:T(128)}, f32[64,256,128]{2,0,1:T(8,128)}, s32[8,32]{1,0:T(8,128)S(1)}, ...), condition=%wide.region_7.8_spmd.clone, body=%wide.region_6.7_spmd.clone.sunk | while | flops 1347423488 | bytes 35657384 | solution.py:82
  781.7 11.9 select_add_fusion.5
  801.8 14.4 %select_add_fusion.5 = f32[64,256,128]{2,0,1:T(8,128)} fusion(f32[64,256,128]{2,0,1:T(8,128)} %get-tuple-element.373, pred[]{:T(512)S(6)} %compare.15, f32[32,256,128]{2,1,0:T(8,128)} %fusion.78, s32[32]{0:T(128)S(1)} %fusion.79), kind=kOutput, calls=%fused_computation.40.clone.1 | convolution fusion | flops 809502720 | bytes 20971648 | tf_op jit(solution)/shard_map/while/body/eval_jaxpr/gk,gif->kif/dot_general | solution.py:76
  824.2 14.4 %select_add_fusion.5 = f32[64,256,128]{2,0,1:T(8,128)} fusion(f32[64,256,128]{2,0,1:T(8,128)} %get-tuple-element.373, pred[]{:T(512)S(6)} %compare.15, f32[32,256,128]{2,1,0:T(8,128)} %fusion.78, s32[32]{0:T(128)S(1)} %fusion.79), kind=kOutput, calls=%fused_computation.40.clone.1 | convolution fusion | flops 809502720 | bytes 20971648 | tf_op jit(solution)/shard_map/while/body/eval_jaxpr/gk,gif->kif/dot_general | solution.py:76
  846.7 14.4 %select_add_fusion.5 = f32[64,256,128]{2,0,1:T(8,128)} fusion(f32[64,256,128]{2,0,1:T(8,128)} %get-tuple-element.373, pred[]{:T(512)S(6)} %compare.15, f32[32,256,128]{2,1,0:T(8,128)} %fusion.78, s32[32]{0:T(128)S(1)} %fusion.79), kind=kOutput, calls=%fused_computation.40.clone.1 | convolution fusion | flops 809502720 | bytes 20971648 | tf_op jit(solution)/shard_map/while/body/eval_jaxpr/gk,gif->kif/dot_general | solution.py:76
  869.2 14.4 %select_add_fusion.5 = f32[64,256,128]{2,0,1:T(8,128)} fusion(f32[64,256,128]{2,0,1:T(8,128)} %get-tuple-element.373, pred[]{:T(512)S(6)} %compare.15, f32[32,256,128]{2,1,0:T(8,128)} %fusion.78, s32[32]{0:T(128)S(1)} %fusion.79), kind=kOutput, calls=%fused_computation.40.clone.1 | convolution fusion | flops 809502720 | bytes 20971648 | tf_op jit(solution)/shard_map/while/body/eval_jaxpr/gk,gif->kif/dot_general | solution.py:76
  891.7 14.4 %select_add_fusion.5 = f32[64,256,128]{2,0,1:T(8,128)} fusion(f32[64,256,128]{2,0,1:T(8,128)} %get-tuple-element.373, pred[]{:T(512)S(6)} %compare.15, f32[32,256,128]{2,1,0:T(8,128)} %fusion.78, s32[32]{0:T(128)S(1)} %fusion.79), kind=kOutput, calls=%fused_computation.40.clone.1 | convolution fusion | flops 809502720 | bytes 20971648 | tf_op jit(solution)/shard_map/while/body/eval_jaxpr/gk,gif->kif/dot_general | solution.py:76
  914.1 14.4 %select_add_fusion.5 = f32[64,256,128]{2,0,1:T(8,128)} fusion(f32[64,256,128]{2,0,1:T(8,128)} %get-tuple-element.373, pred[]{:T(512)S(6)} %compare.15, f32[32,256,128]{2,1,0:T(8,128)} %fusion.78, s32[32]{0:T(128)S(1)} %fusion.79), kind=kOutput, calls=%fused_computation.40.clone.1 | convolution fusion | flops 809502720 | bytes 20971648 | tf_op jit(solution)/shard_map/while/body/eval_jaxpr/gk,gif->kif/dot_general | solution.py:76
  936.6 14.4 %select_add_fusion.5 = f32[64,256,128]{2,0,1:T(8,128)} fusion(f32[64,256,128]{2,0,1:T(8,128)} %get-tuple-element.373, pred[]{:T(512)S(6)} %compare.15, f32[32,256,128]{2,1,0:T(8,128)} %fusion.78, s32[32]{0:T(128)S(1)} %fusion.79), kind=kOutput, calls=%fused_computation.40.clone.1 | convolution fusion | flops 809502720 | bytes 20971648 | tf_op jit(solution)/shard_map/while/body/eval_jaxpr/gk,gif->kif/dot_general | solution.py:76
  951.0 11.5 copy.14
  962.6 85.7 %reduce-scatter.5.cloned.1.call-done = f32[1024,128]{1,0:T(8,128)} async-done(((f32[16384,128]{1,0:T(8,128)}), f32[1024,128]{1,0:T(8,128)}) %reduce-scatter.5.cloned.1.call-update) | async-done | bytes 524304 | tf_op jit(solution)/shard_map/reduce_scatter | solution.py:112
  1050.6 137.6 %all-reduce.2.cloned.1.call-done = f32[128,128]{0,1:T(8,128)} async-done(((f32[128,128]{0,1:T(8,128)}), f32[128,128]{0,1:T(8,128)}) %all-reduce.2.cloned.1.call-update) | async-done | bytes 65552 | tf_op jit(solution)/shard_map/psum | solution.py:114
  (230 shorter events, 394.0 us)
Async XLA Ops:
  7.2 1.0 copy-start
  7.2 542.6 %all-gather.3.cloned.1.call-start = ((), (), s32[]{:S(2)}) async-start(), calls=%async_computation.2 | async-start | bytes 4456448 | tf_op jit(solution)/shard_map/all_gather | solution.py:104
  9.8 737.4 %reduce-scatter.3.cloned.1.call-start = ((), (), s32[]{:S(2)}) async-start(), calls=%async_computation.3 | async-start | bytes 4718592 | tf_op jit(solution)/shard_map/reduce_scatter | solution.py:107
  706.4 40.8 %copy-start.1 = (bf16[1024,128]{1,0:T(8,128)(2,1)S(1)}, bf16[1024,128]{1,0:T(8,128)(2,1)}, u32[]{:S(2)}) copy-start(bf16[1024,128]{1,0:T(8,128)(2,1)} %param.17) | copy-start | bytes 786436
  706.4 67.3 %all-gather.5.cloned.1.call-start = ((), (), s32[]{:S(2)}) async-start(), calls=%async_computation.4 | async-start | bytes 2359296 | tf_op jit(solution)/shard_map/all_gather | solution.py:110
  749.4 298.9 %reduce-scatter.5.cloned.1.call-start = ((), (), s32[]{:S(2)}) async-start(), calls=%async_computation.5 | async-start | bytes 8912896 | tf_op jit(solution)/shard_map/reduce_scatter | solution.py:112
  962.5 225.7 %all-reduce.2.cloned.1.call-start = ((), (), s32[]{:S(2)}) async-start(), calls=%async_computation.6 | async-start | bytes 131072 | tf_op jit(solution)/shard_map/psum | solution.py:114
Sparse Core Ops, SparseCore 0:
  10.7 53.8 all-gather.2
  706.5 40.6 reduce-scatter.2
  749.5 24.1 all-gather.4
  962.6 85.6 reduce-scatter.4
  1053.5 134.6 all-reduce.1
where the time goes:
time: 1200 us
  other arithmetic  447 us (37%)
  waiting for transfers between devices  288 us (24%)
  matrix products  285 us (24%)
  local copies, waits for them, and re-layouts  161 us (13%)
  between operations  13.8 us (1%)
    while x40, other arithmetic  393 us
    psum x1, waiting for transfers between devices, body(): weight_grad = lax.psum(partial_w, ('row', 'col'))  138 us
    dot_general x8, matrix products, backward_step(): jnp.einsum('gk,gif->kif', onehot, prod, precision=lax.Precision.HIGHEST)  113 us
    reduce_scatter x1, waiting for transfers between devices, body(): lax.psum_scatter(col_partial, 'row', scatter_dimension=0, tiled=True)  85.7 us
    dot_general x8, matrix products, forward_step(): jnp.einsum('gk,gif->kif', onehot, prod, precision=lax.Precision.HIGHEST)  80 us
    convert_element_type x8, local copies, waits for them, and re-layouts, tile_mats(): return flat.reshape(group, 256, 256).astype(jnp.bfloat16)  56.9 us
    dot_general x8, matrix products, forward_step(): jnp.einsum('gij,gjf->gif', mats, picked, preferred_element_type=jnp.float32)  44.4 us
    dot_general x8, matrix products, backward_step(): jnp.einsum('gij,gif->gjf', mats, picked, preferred_element_type=jnp.float32)  43.7 us
  transfers between devices with their start and end apart: 5, of which 4 were waited for; matrix products, arithmetic and copies ran while one was open for 45% of the time, Pallas kernels for 0%

commit v1 on v0

v1 whole, which is shorter than its diff:
```python
import functools

import jax
import jax.numpy as jnp
import numpy as np
from jax import lax
from jax.experimental import pallas as pl
from jax.experimental.pallas import tpu as pltpu
from jax.sharding import PartitionSpec as P

BF = jnp.bfloat16
F32 = jnp.float32
UNROLL = 8
EDGES = (0, 20, 44, 60, 64)


def row_id(y, x):
    return (y % 4) * 4 + x % 4


def col_id(z, k):
    return (z % 4) * 2 + k


def shift(a, axis, step):
    if axis == "z":
        pairs = [(col_id(z, k), col_id(z + step, k)) for z in range(4) for k in range(2)]
        return lax.ppermute(a, "col", pairs)
    dy, dx = (step, 0) if axis == "y" else (0, step)
    pairs = [(row_id(y, x), row_id(y + dy, x + dx)) for y in range(4) for x in range(4)]
    return lax.ppermute(a, "row", pairs)


def swap_cores(a):
    return lax.ppermute(a, "col", [(col_id(z, k), col_id(z, 1 - k)) for z in range(4) for k in range(2)])


def slot_table():
    table = np.zeros((4, 4, 4), np.int32)
    at = 0
    order = [
        (0, 0, range(4)), (0, 3, range(4)), (0, 1, range(4)), (3, 0, range(4)), (1, 0, range(4)),
        (0, 2, (0, 1)), (1, 3, range(4)), (0, 2, (2, 3)), (3, 1, range(4)),
        (2, 0, (0, 1)), (3, 3, range(4)), (2, 0, (2, 3)), (1, 1, range(4)),
        (2, 3, range(4)), (2, 1, range(4)), (3, 2, range(4)), (1, 2, range(4)),
        (2, 2, range(4)),
    ]
    for dy, dx, pieces in order:
        for piece in pieces:
            table[dy, dx, piece] = at
            at += 1
    return table.reshape(64)


def plan_tiles(rows, cols, counts, y, x, z, k):
    source = cols // 4
    rel = ((source // 4 - y) % 4 * 4 + (source % 4 - x) % 4) * 4 + cols % 4
    slots = jnp.sum(
        jnp.where(rel[:, None] == jnp.arange(64, dtype=jnp.int32)[None, :], slot_table()[None, :], 0), axis=1
    )
    ids = jnp.arange(256, dtype=jnp.int32)
    key = slots * 256 + ids
    rank = jnp.sum((key[None, :] < key[:, None]).astype(jnp.int32), axis=1)
    fields = jnp.stack([ids, rows, slots, counts])
    placed = jnp.sum(jnp.where(rank[None, :, None] == ids[None, None, :], fields[:, :, None], 0), axis=1)
    ends = [jnp.sum((slots < edge).astype(jnp.int32)) for edge in EDGES]
    tail = jnp.stack(ends + [z, k, z, z]).astype(jnp.int32)
    last = jnp.sum(jnp.where(jnp.arange(9)[:, None] == ids[None, :], tail[:, None], 0), axis=0)
    return jnp.concatenate([placed, last[None]], axis=0)


def spmm_kernel(phase, meta, nrow, ncol, value, pieces, *rest):
    first, final = phase == 0, phase == 3
    rest = list(rest)
    if not first:
        rest.pop(0)
    total = rest.pop(0)
    if final:
        keep, give = rest.pop(0), rest.pop(0)
    value32, iota = rest
    value32[...] = value[...].astype(F32)
    iota[...] = lax.broadcasted_iota(jnp.int32, (256, 256), 0).astype(F32).astype(BF)
    if first:
        total[...] = jnp.zeros_like(total)
    lane = lax.broadcasted_iota(jnp.int32, (1, 256), 1)
    low, high = meta[4, phase], meta[4, phase + 1]
    zero = jnp.zeros((256, 256), BF)
    one = jnp.ones((256, 256), BF)

    def step(i, carry):
        at = [low + i * UNROLL + u for u in range(UNROLL)]
        safe = [jnp.minimum(p, high - 1) for p in at]
        tiles = [meta[0, p] for p in safe]
        picked = []
        for u in range(UNROLL):
            columns = ncol[pl.ds(tiles[u], 1), :].astype(F32).astype(BF)
            gather = jnp.where(iota[...] == jnp.broadcast_to(columns, (256, 256)), one, zero)
            piece = pieces[meta[2, safe[u]] - EDGES[phase]]
            picked.append(jnp.dot(piece, gather, preferred_element_type=F32).astype(BF))
        for u in range(UNROLL):
            live = jnp.where(at[u] < high, meta[3, safe[u]], 0)
            weight = jnp.where(lane < live, value32[pl.ds(tiles[u], 1), :], 0.0).astype(BF)
            rows = nrow[pl.ds(tiles[u], 1), :].astype(F32).astype(BF)
            spread = jnp.where(
                iota[...] == jnp.broadcast_to(rows, (256, 256)), jnp.broadcast_to(weight, (256, 256)), zero
            )
            r = meta[1, safe[u]]
            total[r] = total[r] + lax.dot_general(
                picked[u], spread, (((1,), (1,)), ((), ())), preferred_element_type=F32
            )
        return carry

    lax.fori_loop(0, (high - low + UNROLL - 1) // UNROLL, step, 0)
    if final:
        z, k = meta[4, 5], meta[4, 6]
        for dz in range(4):
            zz = lax.rem(z + dz, 4) * 2
            keep[dz] = total[pl.ds((zz + k) * 4, 4)]
            give[dz] = total[pl.ds((zz + 1 - k) * 4, 4)].astype(BF)


def spmm(phase, meta, nrow, ncol, value, pieces, total=None):
    vmem = pl.BlockSpec(memory_space=pltpu.VMEM)
    args = [nrow, ncol, value, pieces] + ([] if total is None else [total])
    out = [jax.ShapeDtypeStruct((32, 128, 256), F32)]
    if phase == 3:
        out += [jax.ShapeDtypeStruct((4, 4, 128, 256), F32), jax.ShapeDtypeStruct((4, 4, 128, 256), BF)]
    share = (EDGES[phase + 1] - EDGES[phase]) / 64
    return pl.pallas_call(
        functools.partial(spmm_kernel, phase),
        out_shape=out,
        in_specs=[pl.BlockSpec(memory_space=pltpu.SMEM)] + [vmem] * len(args),
        out_specs=[vmem] * len(out),
        scratch_shapes=[pltpu.VMEM((256, 256), F32), pltpu.VMEM((256, 256), BF)],
        input_output_aliases={} if total is None else {5: 0},
        compiler_params=pltpu.CompilerParams(vmem_limit_bytes=40 << 20),
        cost_estimate=pl.CostEstimate(flops=int(share * 3.0e10), bytes_accessed=1 << 20, transcendentals=0),
        name=f"spmm_phase{phase}",
    )(meta, *args)


def finish_kernel(hidden, weight, cotangent, node_out, partial):
    h = [hidden[i] for i in range(4)]
    w = weight[...].astype(F32)
    grad = jnp.zeros((128, 128), F32)
    for i in range(4):
        pre_t = lax.dot_general(
            w, h[i], (((0,), (0,)), ((), ())), precision=lax.Precision.HIGHEST, preferred_element_type=F32
        )
        pre = pre_t.T
        sig = 1.0 / (1.0 + jnp.exp(-pre))
        span = pl.ds(i * 256, 256)
        node_out[span, :] = (pre * sig).astype(BF)
        slope = sig * (1.0 + pre * (1.0 - sig))
        pre_grad = (cotangent[span, :].astype(F32) * slope).astype(BF).astype(F32)
        grad = grad + jnp.dot(h[i], pre_grad, precision=lax.Precision.HIGHEST, preferred_element_type=F32)
    partial[...] = grad


def finish(hidden, weight, cotangent):
    vmem = pl.BlockSpec(memory_space=pltpu.VMEM)
    return pl.pallas_call(
        finish_kernel,
        out_shape=[jax.ShapeDtypeStruct((1024, 128), BF), jax.ShapeDtypeStruct((128, 128), F32)],
        in_specs=[vmem] * 3,
        out_specs=[vmem] * 2,
        compiler_params=pltpu.CompilerParams(vmem_limit_bytes=16 << 20),
        name="finish",
    )(hidden, weight, cotangent)


def cat(*parts):
    return jnp.concatenate(parts, axis=0)


def add(a, b):
    return a.astype(F32) + b.astype(F32)


def sum_ring(v, axis):
    return (v + shift(v, axis, 2)) + (shift(v, axis, 1) + shift(v, axis, -1))


def body(features, weight, cotangent, tile_row, tile_col, nnz_row, nnz_col, edge_value, tile_count):
    row, col = lax.axis_index("row"), lax.axis_index("col")
    meta = plan_tiles(
        tile_row.reshape(256), tile_col.reshape(256), tile_count.reshape(256),
        row // 4, row % 4, col // 2, col % 2,
    )
    slots = (meta, nnz_row.reshape(256, 256), nnz_col.reshape(256, 256), edge_value.reshape(256, 256))

    own = jnp.transpose(features.reshape(4, 256, 128), (0, 2, 1))
    r1, l1 = shift(own, "x", 1), shift(own, "x", -1)
    d1, u1 = shift(own, "y", 1), shift(own, "y", -1)
    r2, l2 = shift(cat(r1[:2], u1), "x", 1), shift(cat(l1[2:], d1), "x", -1)
    d2, u2 = shift(cat(d1[:2], r1), "y", 1), shift(cat(u1[2:], l1), "y", -1)
    (total,) = spmm(0, *slots, cat(own, r1, l1, d1, u1))
    across, along = cat(r2[:2], l2[:2]), cat(d2[:2], u2[:2])
    r3, l3 = shift(along, "x", 1), shift(along, "x", -1)
    d3, u3 = shift(across, "y", 1), shift(across, "y", -1)
    (total,) = spmm(1, *slots, cat(r2, l2, d2, u2), total)
    r4, l4 = shift(r3[0:1], "x", 1), shift(l3[1:2], "x", -1)
    d4, u4 = shift(d3[2:3], "y", 1), shift(u3[3:4], "y", -1)
    (total,) = spmm(2, *slots, cat(r3, l3, d3, u3), total)
    total, keep, give = spmm(3, *slots, cat(r4, l4, d4, u4), total)

    got = swap_cores(give)
    mine = add(keep[0], got[0])
    far = add(keep[2], got[2]).astype(BF)
    up32, down32 = add(keep[1], got[1]), add(keep[3], got[3])
    far_up = shift(far[:2], "z", 1)
    far_down = shift(far[2:], "z", -1)
    near_up = shift(up32[2:].astype(BF), "z", 1)
    near_down = shift(down32[:2].astype(BF), "z", -1)
    sum_up = shift(add(up32[:2], far_up).astype(BF), "z", 1)
    sum_down = shift(add(down32[2:], far_down).astype(BF), "z", -1)
    hidden = mine + cat(add(sum_up, near_down), add(near_up, sum_down))

    node_out, partial = finish(hidden, weight, cotangent)
    grad = partial + swap_cores(partial)
    for axis in ("z", "x", "y"):
        grad = sum_ring(grad, axis)
    return node_out, grad


def solution(mesh):
    placed = (
        P(("col", "row"), None),
        P(),
        P(("row", "col"), None),
        P("row", "col", None),
        P("row", "col", None),
        P("row", "col", None, None),
        P("row", "col", None, None),
        P("row", "col", None, None),
        P("row", "col", None),
    )
    return jax.shard_map(
        body, mesh=mesh, in_specs=placed, out_specs=(P(("row", "col"), None), P()), check_vma=False
    )
```

time: 1200 us -> 117 us (0.10)
  other arithmetic: 447 us -> 5.28 us
  matrix products: 285 us -> 0 us
  waiting for transfers between devices: 288 us -> 26.9 us
  local copies, waits for them, and re-layouts: 161 us -> 4.61 us
  starting transfers between devices: 0.2 us -> 49.9 us
  Pallas kernels: 0 us -> 28.2 us
  between operations: 13.8 us -> 1.2 us
    while x40 -> x0, other arithmetic: 393 us -> none
    dot_general x34 -> x0, matrix products: 285 us -> none  [the longest x8 113 us: backward_step(): jnp.einsum('gk,gif->kif', onehot, prod, precision=lax.Precision.HIGHEST)]
    psum x1 -> x0, waiting for transfers between devices: 138 us -> none  [body(): weight_grad = lax.psum(partial_w, ('row', 'col'))]
    reduce_scatter x2 -> x0, waiting for transfers between devices: 127 us -> none  [the longest x1 85.7 us: body(): lax.psum_scatter(col_partial, 'row', scatter_dimension=0, tiled=True)]
    convert_element_type x8 -> x2, local copies, waits for them, and re-layouts: 56.9 us -> 0.03 us  [the longest x1 0.02 us: body(): near_down = shift(down32[:2].astype(BF), 'z', -1)]
    ppermute x0 -> x33, starting transfers between devices: none -> 49.9 us  [the longest x22 33.9 us: shift(): return lax.ppermute(a, 'row', pairs)]
    gather x16 -> x0, local copies, waits for them, and re-layouts: 45.4 us -> none  [the longest x8 25.1 us: forward_step(): picked = jnp.take(blocks, col_ids, axis=0)]
    convert_element_type x9 -> x2, other arithmetic: 43.3 us -> 0.07 us  [the longest x1 0.03 us: body(): sum_down = shift(add(down32[2:], far_down).astype(BF), 'z', -1)]
  transfers between devices with their start and end apart: 5 -> 33, of which waited for: 4 -> 12; matrix products, arithmetic and copies ran while one was open for 45% -> 7% of each run, Pallas kernels for 0% -> 20%
where the time goes in v1:
time: 117 us; the launch traced here: 116 us
  starting transfers between devices  49.9 us (43%)
  Pallas kernels  28.2 us (24%)
  waiting for transfers between devices  26.9 us (23%)
  other arithmetic  5.28 us (5%)
  local copies, waits for them, and re-layouts  4.61 us (4%)
  between operations  1.2 us (1%)
    ppermute x22, starting transfers between devices, shift(): return lax.ppermute(a, 'row', pairs)  33.9 us
    pallas_call x4, Pallas kernels, spmm(): pl.pallas_call(functools.partial(spmm_kernel, phase), out_shape=out, in_s...  26.1 us
    ppermute x9, starting transfers between devices, shift(): return lax.ppermute(a, 'col', pairs)  16 us
    ppermute x9, waiting for transfers between devices, shift(): return lax.ppermute(a, 'col', pairs)  12 us
    ppermute x22, waiting for transfers between devices, shift(): return lax.ppermute(a, 'row', pairs)  11.1 us
    ppermute x2, waiting for transfers between devices, swap_cores(): lax.ppermute(a, 'col', [(col_id(z, k), col_id(z, 1 - k)) for z in range(4...  3.9 us
    another operation x1, local copies, waits for them, and re-layouts, plan_tiles(): tail = jnp.stack(ends + [z, k, z, z]).astype(jnp.int32)  3.24 us
  transfers between devices with their start and end apart: 33, of which 12 were waited for; matrix products, arithmetic and copies ran while one was open for 7% of the time, Pallas kernels for 20%

profile of v1, /device:TPU:0, one launch (start us, length us, event | category | flops | bytes accessed | tf_op | source)
XLA Modules:
  0.0 116.1 jit_solution(16490193723669135140)
XLA Ops:
  1.7 2.9 %collective-permute-start.4 = (bf16[4,128,256]{2,1,0:T(8,128)(2,1)S(1)}, bf16[4,128,256]{2,1,0:T(8,128)(2,1)S(1)}, u32[]{:S(2)}, u32[]{:S(2)}) collective-permute-start(bf16[4,128,256]{2,1,0:T(8,128)(2,1)S(1)} %bitcast.52), channel_id=1, source_target_pairs={{0,24},{8,0},{16,8},{24,16},{32,56},{40,32},{48,40},{56,48},{64,88... | collective-permute-start | bytes 786440 | tf_op jit(solution)/shard_map/ppermute | solution.py:31
  4.6 3.0 %collective-permute-start.3 = (bf16[4,128,256]{2,1,0:T(8,128)(2,1)S(1)}, bf16[4,128,256]{2,1,0:T(8,128)(2,1)S(1)}, u32[]{:S(2)}, u32[]{:S(2)}) collective-permute-start(bf16[4,128,256]{2,1,0:T(8,128)(2,1)S(1)} %bitcast.53), channel_id=1, source_target_pairs={{0,96},{8,104},{16,112},{24,120},{32,0},{40,8},{48,16},{56,24},{64... | collective-permute-start | bytes 786440 | tf_op jit(solution)/shard_map/ppermute | solution.py:31
  11.2 3.2 %stack.39 = s32[9]{0:T(128)S(1)} concatenate(s32[1]{0:T(128)} %bitcast.4, s32[1]{0:T(128)} %bitcast.5, s32[1]{0:T(128)} %bitcast.6, s32[1]{0:T(128)} %bitcast.7, s32[1]{0:T(128)} %bitcast.8, s32[1]{0:T(128)} %bitcast.9, s32[1]{0:T(128)} %bitcast.10, s32[1]{0:T(128)} %bitcast.9, s32[1]{0:T(128)} %bitcast.9), dimensions={0} | concatenate | bytes 72 | tf_op jit(solution)/shard_map/stack | solution.py:67
  16.4 3.0 %collective-permute-start.11 = (bf16[6,128,256]{2,1,0:T(8,128)(2,1)S(1)}, bf16[6,128,256]{2,1,0:T(8,128)(2,1)S(1)}, u32[]{:S(2)}, u32[]{:S(2)}) collective-permute-start(bf16[6,128,256]{2,1,0:T(8,128)(2,1)S(1)} %pad_maximum_fusion.5), channel_id=1, source_target_pairs={{0,24},{8,0},{16,8},{24,16},{32,56},{40,32},{48,40},{56,48},{64,88... | collective-permute-start | bytes 1179656 | tf_op jit(solution)/shard_map/ppermute | solution.py:31
  19.8 3.3 %collective-permute-start.5 = (bf16[6,128,256]{2,1,0:T(8,128)(2,1)S(1)}, bf16[6,128,256]{2,1,0:T(8,128)(2,1)S(1)}, u32[]{:S(2)}, u32[]{:S(2)}) collective-permute-start(bf16[6,128,256]{2,1,0:T(8,128)(2,1)S(1)} %pad_maximum_fusion.3), channel_id=1, source_target_pairs={{0,96},{8,104},{16,112},{24,120},{32,0},{40,8},{48,16},{56,24},{64... | collective-permute-start | bytes 1179656 | tf_op jit(solution)/shard_map/ppermute | solution.py:31
  23.2 7.1 %spmm_phase0.1.rest_0_ = f32[32,128,256]{2,1,0:T(8,128)S(1)} custom-call(s32[5,256]{1,0:T(8,128)S(1)} %pad_add_fusion.meta, s32[256,256]{1,0:T(8,128)S(1)} %bitcast.40, s32[256,256]{1,0:T(8,128)S(1)} %bitcast.44, bf16[256,256]{1,0:T(8,128)(2,1)S(1)} %bitcast.48, bf16[20,128,256]{2,1,0:T(8,128)(2,1)S(1)} %constant_dynamic-update-slice_fusion.pieces), custom_call_target="tpu_custom_call" | custom-call | flops 9374999552 | bytes 1048576 | tf_op jit(solution)/shard_map/spmm_phase0/pallas_call | solution.py:129
  30.5 2.3 %collective-permute-start.14 = (bf16[4,128,256]{2,1,0:T(8,128)(2,1)S(1)}, bf16[4,128,256]{2,1,0:T(8,128)(2,1)S(1)}, u32[]{:S(2)}, u32[]{:S(2)}) collective-permute-start(bf16[4,128,256]{2,1,0:T(8,128)(2,1)S(1)} %pad_maximum_fusion.7), channel_id=1, source_target_pairs={{0,96},{8,104},{16,112},{24,120},{32,0},{40,8},{48,16},{56,24},{64... | collective-permute-start | bytes 786440 | tf_op jit(solution)/shard_map/ppermute | solution.py:31
  32.9 3.8 %collective-permute-start.8 = (bf16[4,128,256]{2,1,0:T(8,128)(2,1)S(1)}, bf16[4,128,256]{2,1,0:T(8,128)(2,1)S(1)}, u32[]{:S(2)}, u32[]{:S(2)}) collective-permute-start(bf16[4,128,256]{2,1,0:T(8,128)(2,1)S(1)} %pad_maximum_fusion.6), channel_id=1, source_target_pairs={{0,24},{8,0},{16,8},{24,16},{32,56},{40,32},{48,40},{56,48},{64,88... | collective-permute-start | bytes 786440 | tf_op jit(solution)/shard_map/ppermute | solution.py:31
  36.9 9.0 %spmm_phase1.1.rest_0_ = f32[32,128,256]{2,1,0:T(8,128)S(1)} custom-call(s32[5,256]{1,0:T(8,128)S(1)} %pad_add_fusion.meta, s32[256,256]{1,0:T(8,128)S(1)} %bitcast.41, s32[256,256]{1,0:T(8,128)S(1)} %bitcast.45, bf16[256,256]{1,0:T(8,128)(2,1)S(1)} %bitcast.49, bf16[24,128,256]{2,1,0:T(8,128)(2,1)S(1)} %pad_maximum_fusion.pieces, ...), custom_call_target="tpu_custom_call", output_to_operand_aliasing={{}: (5, {})} | custom-call | flops 11249999872 | bytes 1048576 | tf_op jit(solution)/shard_map/spmm_phase1/pallas_call | solution.py:129
  48.1 4.4 %collective-permute-start.9 = (bf16[1,128,256]{2,1,0:T(8,128)(2,1)S(1)}, bf16[1,128,256]{2,1,0:T(8,128)(2,1)S(1)}, u32[]{:S(2)}, u32[]{:S(2)}) collective-permute-start(bf16[1,128,256]{2,1,0:T(8,128)(2,1)S(1)} %slice.129), channel_id=1, source_target_pairs={{0,24},{8,0},{16,8},{24,16},{32,56},{40,32},{48,40},{56,48},{64,88... | collective-permute-start | bytes 196616 | tf_op jit(solution)/shard_map/ppermute | solution.py:31
  52.7 6.9 %spmm_phase2.1.rest_0_ = f32[32,128,256]{2,1,0:T(8,128)S(1)} custom-call(s32[5,256]{1,0:T(8,128)S(1)} %pad_add_fusion.meta, s32[256,256]{1,0:T(8,128)S(1)} %bitcast.42, s32[256,256]{1,0:T(8,128)S(1)} %bitcast.46, bf16[256,256]{1,0:T(8,128)(2,1)S(1)} %bitcast.50, bf16[16,128,256]{2,1,0:T(8,128)(2,1)S(1)} %pad_maximum_fusion.1.pieces, ...), custom_call_target="tpu_custom_call", output_to_operand_aliasing={{}: (5, {})} | custom-call | flops 7500000256 | bytes 1048576 | tf_op jit(solution)/shard_map/spmm_phase2/pallas_call | solution.py:129
  59.7 3.0 %spmm_phase3.1 = (f32[32,128,256]{2,1,0:T(8,128)S(1)}, f32[4,4,128,256]{3,2,1,0:T(8,128)S(1)}, bf16[4,4,128,256]{3,2,1,0:T(8,128)(2,1)S(1)}) custom-call(s32[5,256]{1,0:T(8,128)S(1)} %pad_add_fusion.meta, s32[256,256]{1,0:T(8,128)S(1)} %bitcast.43, s32[256,256]{1,0:T(8,128)S(1)} %bitcast.47, ...), custom_call_target="tpu_custom_call", output_to_operand_aliasing={{0}: (5, {})} | custom-call | flops 1875000064 | bytes 1048576 | tf_op jit(solution)/shard_map/spmm_phase3/pallas_call | solution.py:129
  62.8 2.6 %collective-permute-done.16 = bf16[4,4,128,256]{3,2,1,0:T(8,128)(2,1)S(1)} collective-permute-done((bf16[4,4,128,256]{3,2,1,0:T(8,128)(2,1)S(1)}, bf16[4,4,128,256]{3,2,1,0:T(8,128)(2,1)S(1)}, u32[]{:S(2)}, u32[]{:S(2)}) %collective-permute-start.16) | collective-permute-done | bytes 1048608 | tf_op jit(solution)/shard_map/ppermute | solution.py:35
  65.7 4.3 %collective-permute-start.19 = (bf16[2,128,256]{2,1,0:T(8,128)(2,1)S(1)}, bf16[2,128,256]{2,1,0:T(8,128)(2,1)S(1)}, u32[]{:S(2)}, u32[]{:S(2)}) collective-permute-start(bf16[2,128,256]{2,1,0:T(8,128)(2,1)S(1)} %fusion.4), channel_id=1, source_target_pairs={{0,6},{1,7},{2,0},{3,1},{4,2},{5,3},{6,4},{7,5},{8,14},{9,15},{10,... | collective-permute-start | bytes 393224 | tf_op jit(solution)/shard_map/ppermute | solution.py:28
  70.2 3.3 %collective-permute-start.21 = (bf16[2,128,256]{2,1,0:T(8,128)(2,1)S(1)}, bf16[2,128,256]{2,1,0:T(8,128)(2,1)S(1)}, u32[]{:S(2)}, u32[]{:S(2)}) collective-permute-start(bf16[2,128,256]{2,1,0:T(8,128)(2,1)S(1)} %get-tuple-element.19), channel_id=1, source_target_pairs={{0,6},{1,7},{2,0},{3,1},{4,2},{5,3},{6,4},{7,5},{8,14},{9,15},{10,... | collective-permute-start | bytes 393224 | tf_op jit(solution)/shard_map/ppermute | solution.py:28
  73.5 4.2 %collective-permute-done.17 = bf16[2,128,256]{2,1,0:T(8,128)(2,1)S(1)} collective-permute-done((bf16[2,128,256]{2,1,0:T(8,128)(2,1)S(1)}, bf16[2,128,256]{2,1,0:T(8,128)(2,1)S(1)}, u32[]{:S(2)}, u32[]{:S(2)}) %collective-permute-start.17) | collective-permute-done | bytes 131104 | tf_op jit(solution)/shard_map/ppermute | solution.py:28
  77.8 3.3 %collective-permute-start.22 = (bf16[2,128,256]{2,1,0:T(8,128)(2,1)S(1)}, bf16[2,128,256]{2,1,0:T(8,128)(2,1)S(1)}, u32[]{:S(2)}, u32[]{:S(2)}) collective-permute-start(bf16[2,128,256]{2,1,0:T(8,128)(2,1)S(1)} %fusion.1), channel_id=1, source_target_pairs={{0,6},{1,7},{2,0},{3,1},{4,2},{5,3},{6,4},{7,5},{8,14},{9,15},{10,... | collective-permute-start | bytes 393224 | tf_op jit(solution)/shard_map/ppermute | solution.py:28
  81.1 2.8 %collective-permute-done.18 = bf16[2,128,256]{2,1,0:T(8,128)(2,1)S(1)} collective-permute-done((bf16[2,128,256]{2,1,0:T(8,128)(2,1)S(1)}, bf16[2,128,256]{2,1,0:T(8,128)(2,1)S(1)}, u32[]{:S(2)}, u32[]{:S(2)}) %collective-permute-start.18) | collective-permute-done | bytes 131104 | tf_op jit(solution)/shard_map/ppermute | solution.py:28
  84.2 2.1 %finish.1 = (bf16[1024,128]{1,0:T(8,128)(2,1)}, f32[128,128]{1,0:T(8,128)S(1)}) custom-call(f32[4,128,256]{2,1,0:T(8,128)S(1)} %maximum_add_fusion.hidden, bf16[128,128]{1,0:T(8,128)(2,1)S(1)} %copy-done.1, bf16[1024,128]{1,0:T(8,128)(2,1)S(1)} %copy-done), custom_call_target="tpu_custom_call" | custom-call | tf_op jit(solution)/shard_map/finish/pallas_call | solution.py:162
  87.5 3.4 %collective-permute-start.26 = (f32[128,128]{1,0:T(8,128)S(1)}, f32[128,128]{1,0:T(8,128)S(1)}, u32[]{:S(2)}, u32[]{:S(2)}) collective-permute-start(f32[128,128]{1,0:T(8,128)S(1)} %add.160), channel_id=1, source_target_pairs={{0,6},{1,7},{2,0},{3,1},{4,2},{5,3},{6,4},{7,5},{8,14},{9,15},{10,... | collective-permute-start | bytes 196616 | tf_op jit(solution)/shard_map/ppermute | solution.py:28
  92.8 4.6 %collective-permute-done.25 = f32[128,128]{1,0:T(8,128)S(1)} collective-permute-done((f32[128,128]{1,0:T(8,128)S(1)}, f32[128,128]{1,0:T(8,128)S(1)}, u32[]{:S(2)}, u32[]{:S(2)}) %collective-permute-start.25) | collective-permute-done | bytes 65568 | tf_op jit(solution)/shard_map/ppermute | solution.py:28
  97.4 4.0 %collective-permute-start.29 = (f32[128,128]{1,0:T(8,128)S(1)}, f32[128,128]{1,0:T(8,128)S(1)}, u32[]{:S(2)}, u32[]{:S(2)}) collective-permute-start(f32[128,128]{1,0:T(8,128)S(1)} %add_add_fusion.2), channel_id=1, source_target_pairs={{0,24},{8,0},{16,8},{24,16},{32,56},{40,32},{48,40},{56,48},{64,88... | collective-permute-start | bytes 196616 | tf_op jit(solution)/shard_map/ppermute | solution.py:31
  103.3 4.3 %collective-permute-done.28 = f32[128,128]{1,0:T(8,128)S(1)} collective-permute-done((f32[128,128]{1,0:T(8,128)S(1)}, f32[128,128]{1,0:T(8,128)S(1)}, u32[]{:S(2)}, u32[]{:S(2)}) %collective-permute-start.28) | collective-permute-done | bytes 65568 | tf_op jit(solution)/shard_map/ppermute | solution.py:31
  112.2 2.6 %collective-permute-done.31 = f32[128,128]{1,0:T(8,128)S(1)} collective-permute-done((f32[128,128]{1,0:T(8,128)S(1)}, f32[128,128]{1,0:T(8,128)S(1)}, u32[]{:S(2)}, u32[]{:S(2)}) %collective-permute-start.31) | collective-permute-done | bytes 65568 | tf_op jit(solution)/shard_map/ppermute | solution.py:31
  (108 shorter events, 21.5 us)
Async XLA Ops:
  1.7 12.8 %collective-permute-start.4 = (bf16[4,128,256]{2,1,0:T(8,128)(2,1)S(1)}, bf16[4,128,256]{2,1,0:T(8,128)(2,1)S(1)}, u32[]{:S(2)}, u32[]{:S(2)}) collective-permute-start(bf16[4,128,256]{2,1,0:T(8,128)(2,1)S(1)} %bitcast.52), channel_id=1, source_target_pairs={{0,24},{8,0},{16,8},{24,16},{32,56},{40,32},{48,40},{56,48},{64,88... | collective-permute-start | bytes 786440 | tf_op jit(solution)/shard_map/ppermute | solution.py:31
  4.6 14.9 %collective-permute-start.3 = (bf16[4,128,256]{2,1,0:T(8,128)(2,1)S(1)}, bf16[4,128,256]{2,1,0:T(8,128)(2,1)S(1)}, u32[]{:S(2)}, u32[]{:S(2)}) collective-permute-start(bf16[4,128,256]{2,1,0:T(8,128)(2,1)S(1)} %bitcast.53), channel_id=1, source_target_pairs={{0,96},{8,104},{16,112},{24,120},{32,0},{40,8},{48,16},{56,24},{64... | collective-permute-start | bytes 786440 | tf_op jit(solution)/shard_map/ppermute | solution.py:31
  7.6 11.8 %collective-permute-start.1 = (bf16[4,128,256]{2,1,0:T(8,128)(2,1)S(1)}, bf16[4,128,256]{2,1,0:T(8,128)(2,1)S(1)}, u32[]{:S(2)}, u32[]{:S(2)}) collective-permute-start(bf16[4,128,256]{2,1,0:T(8,128)(2,1)S(1)} %bitcast.54), channel_id=1, source_target_pairs={{0,8},{8,16},{16,24},{24,0},{32,40},{40,48},{48,56},{56,32},{64,72... | collective-permute-start | bytes 786440 | tf_op jit(solution)/shard_map/ppermute | solution.py:31
  7.7 8.7 %collective-permute-start = (bf16[4,128,256]{2,1,0:T(8,128)(2,1)S(1)}, bf16[4,128,256]{2,1,0:T(8,128)(2,1)S(1)}, u32[]{:S(2)}, u32[]{:S(2)}) collective-permute-start(bf16[4,128,256]{2,1,0:T(8,128)(2,1)S(1)} %bitcast.55), channel_id=1, source_target_pairs={{0,32},{8,40},{16,48},{24,56},{32,64},{40,72},{48,80},{56,88},{64,... | collective-permute-start | bytes 786440 | tf_op jit(solution)/shard_map/ppermute | solution.py:31
  16.4 14.0 %collective-permute-start.11 = (bf16[6,128,256]{2,1,0:T(8,128)(2,1)S(1)}, bf16[6,128,256]{2,1,0:T(8,128)(2,1)S(1)}, u32[]{:S(2)}, u32[]{:S(2)}) collective-permute-start(bf16[6,128,256]{2,1,0:T(8,128)(2,1)S(1)} %pad_maximum_fusion.5), channel_id=1, source_target_pairs={{0,24},{8,0},{16,8},{24,16},{32,56},{40,32},{48,40},{56,48},{64,88... | collective-permute-start | bytes 1179656 | tf_op jit(solution)/shard_map/ppermute | solution.py:31
  19.5 13.3 %collective-permute-start.2 = (bf16[6,128,256]{2,1,0:T(8,128)(2,1)S(1)}, bf16[6,128,256]{2,1,0:T(8,128)(2,1)S(1)}, u32[]{:S(2)}, u32[]{:S(2)}) collective-permute-start(bf16[6,128,256]{2,1,0:T(8,128)(2,1)S(1)} %pad_maximum_fusion.2), channel_id=1, source_target_pairs={{0,32},{8,40},{16,48},{24,56},{32,64},{40,72},{48,80},{56,88},{64,... | collective-permute-start | bytes 1179656 | tf_op jit(solution)/shard_map/ppermute | solution.py:31
  19.7 10.7 %collective-permute-start.10 = (bf16[6,128,256]{2,1,0:T(8,128)(2,1)S(1)}, bf16[6,128,256]{2,1,0:T(8,128)(2,1)S(1)}, u32[]{:S(2)}, u32[]{:S(2)}) collective-permute-start(bf16[6,128,256]{2,1,0:T(8,128)(2,1)S(1)} %pad_maximum_fusion.4), channel_id=1, source_target_pairs={{0,8},{8,16},{16,24},{24,0},{32,40},{40,48},{48,56},{56,32},{64,72... | collective-permute-start | bytes 1179656 | tf_op jit(solution)/shard_map/ppermute | solution.py:31
  19.8 13.0 %collective-permute-start.5 = (bf16[6,128,256]{2,1,0:T(8,128)(2,1)S(1)}, bf16[6,128,256]{2,1,0:T(8,128)(2,1)S(1)}, u32[]{:S(2)}, u32[]{:S(2)}) collective-permute-start(bf16[6,128,256]{2,1,0:T(8,128)(2,1)S(1)} %pad_maximum_fusion.3), channel_id=1, source_target_pairs={{0,96},{8,104},{16,112},{24,120},{32,0},{40,8},{48,16},{56,24},{64... | collective-permute-start | bytes 1179656 | tf_op jit(solution)/shard_map/ppermute | solution.py:31
  30.5 15.4 %collective-permute-start.14 = (bf16[4,128,256]{2,1,0:T(8,128)(2,1)S(1)}, bf16[4,128,256]{2,1,0:T(8,128)(2,1)S(1)}, u32[]{:S(2)}, u32[]{:S(2)}) collective-permute-start(bf16[4,128,256]{2,1,0:T(8,128)(2,1)S(1)} %pad_maximum_fusion.7), channel_id=1, source_target_pairs={{0,96},{8,104},{16,112},{24,120},{32,0},{40,8},{48,16},{56,24},{64... | collective-permute-start | bytes 786440 | tf_op jit(solution)/shard_map/ppermute | solution.py:31
  32.8 14.8 %collective-permute-start.12 = (bf16[4,128,256]{2,1,0:T(8,128)(2,1)S(1)}, bf16[4,128,256]{2,1,0:T(8,128)(2,1)S(1)}, u32[]{:S(2)}, u32[]{:S(2)}) collective-permute-start(bf16[4,128,256]{2,1,0:T(8,128)(2,1)S(1)} %pad_maximum_fusion.7), channel_id=1, source_target_pairs={{0,32},{8,40},{16,48},{24,56},{32,64},{40,72},{48,80},{56,88},{64,... | collective-permute-start | bytes 786440 | tf_op jit(solution)/shard_map/ppermute | solution.py:31
  32.9 15.2 %collective-permute-start.8 = (bf16[4,128,256]{2,1,0:T(8,128)(2,1)S(1)}, bf16[4,128,256]{2,1,0:T(8,128)(2,1)S(1)}, u32[]{:S(2)}, u32[]{:S(2)}) collective-permute-start(bf16[4,128,256]{2,1,0:T(8,128)(2,1)S(1)} %pad_maximum_fusion.6), channel_id=1, source_target_pairs={{0,24},{8,0},{16,8},{24,16},{32,56},{40,32},{48,40},{56,48},{64,88... | collective-permute-start | bytes 786440 | tf_op jit(solution)/shard_map/ppermute | solution.py:31
  36.7 15.8 %collective-permute-start.6 = (bf16[4,128,256]{2,1,0:T(8,128)(2,1)S(1)}, bf16[4,128,256]{2,1,0:T(8,128)(2,1)S(1)}, u32[]{:S(2)}, u32[]{:S(2)}) collective-permute-start(bf16[4,128,256]{2,1,0:T(8,128)(2,1)S(1)} %pad_maximum_fusion.6), channel_id=1, source_target_pairs={{0,8},{8,16},{16,24},{24,0},{32,40},{40,48},{48,56},{56,32},{64,72... | collective-permute-start | bytes 786440 | tf_op jit(solution)/shard_map/ppermute | solution.py:31
  45.9 13.7 %collective-permute-start.15 = (bf16[1,128,256]{2,1,0:T(8,128)(2,1)S(1)}, bf16[1,128,256]{2,1,0:T(8,128)(2,1)S(1)}, u32[]{:S(2)}, u32[]{:S(2)}) collective-permute-start(bf16[1,128,256]{2,1,0:T(8,128)(2,1)S(1)} %slice.135), channel_id=1, source_target_pairs={{0,96},{8,104},{16,112},{24,120},{32,0},{40,8},{48,16},{56,24},{64... | collective-permute-start | bytes 196616 | tf_op jit(solution)/shard_map/ppermute | solution.py:31
  47.6 12.0 %collective-permute-start.13 = (bf16[1,128,256]{2,1,0:T(8,128)(2,1)S(1)}, bf16[1,128,256]{2,1,0:T(8,128)(2,1)S(1)}, u32[]{:S(2)}, u32[]{:S(2)}) collective-permute-start(bf16[1,128,256]{2,1,0:T(8,128)(2,1)S(1)} %slice.134), channel_id=1, source_target_pairs={{0,32},{8,40},{16,48},{24,56},{32,64},{40,72},{48,80},{56,88},{64,... | collective-permute-start | bytes 196616 | tf_op jit(solution)/shard_map/ppermute | solution.py:31
  48.1 11.6 %collective-permute-start.9 = (bf16[1,128,256]{2,1,0:T(8,128)(2,1)S(1)}, bf16[1,128,256]{2,1,0:T(8,128)(2,1)S(1)}, u32[]{:S(2)}, u32[]{:S(2)}) collective-permute-start(bf16[1,128,256]{2,1,0:T(8,128)(2,1)S(1)} %slice.129), channel_id=1, source_target_pairs={{0,24},{8,0},{16,8},{24,16},{32,56},{40,32},{48,40},{56,48},{64,88... | collective-permute-start | bytes 196616 | tf_op jit(solution)/shard_map/ppermute | solution.py:31
  52.5 7.2 %collective-permute-start.7 = (bf16[1,128,256]{2,1,0:T(8,128)(2,1)S(1)}, bf16[1,128,256]{2,1,0:T(8,128)(2,1)S(1)}, u32[]{:S(2)}, u32[]{:S(2)}) collective-permute-start(bf16[1,128,256]{2,1,0:T(8,128)(2,1)S(1)} %slice.128), channel_id=1, source_target_pairs={{0,8},{8,16},{16,24},{24,0},{32,40},{40,48},{48,56},{56,32},{64,72... | collective-permute-start | bytes 196616 | tf_op jit(solution)/shard_map/ppermute | solution.py:31
  65.7 15.4 %collective-permute-start.19 = (bf16[2,128,256]{2,1,0:T(8,128)(2,1)S(1)}, bf16[2,128,256]{2,1,0:T(8,128)(2,1)S(1)}, u32[]{:S(2)}, u32[]{:S(2)}) collective-permute-start(bf16[2,128,256]{2,1,0:T(8,128)(2,1)S(1)} %fusion.4), channel_id=1, source_target_pairs={{0,6},{1,7},{2,0},{3,1},{4,2},{5,3},{6,4},{7,5},{8,14},{9,15},{10,... | collective-permute-start | bytes 393224 | tf_op jit(solution)/shard_map/ppermute | solution.py:28
  70.0 7.6 %collective-permute-start.17 = (bf16[2,128,256]{2,1,0:T(8,128)(2,1)S(1)}, bf16[2,128,256]{2,1,0:T(8,128)(2,1)S(1)}, u32[]{:S(2)}, u32[]{:S(2)}) collective-permute-start(bf16[2,128,256]{2,1,0:T(8,128)(2,1)S(1)} %get-tuple-element.18), channel_id=1, source_target_pairs={{0,2},{1,3},{2,4},{3,5},{4,6},{5,7},{6,0},{7,1},{8,10},{9,11},{10,... | collective-permute-start | bytes 393224 | tf_op jit(solution)/shard_map/ppermute | solution.py:28
  70.1 13.9 %collective-permute-start.20 = (bf16[2,128,256]{2,1,0:T(8,128)(2,1)S(1)}, bf16[2,128,256]{2,1,0:T(8,128)(2,1)S(1)}, u32[]{:S(2)}, u32[]{:S(2)}) collective-permute-start(bf16[2,128,256]{2,1,0:T(8,128)(2,1)S(1)} %fusion.5), channel_id=1, source_target_pairs={{0,2},{1,3},{2,4},{3,5},{4,6},{5,7},{6,0},{7,1},{8,10},{9,11},{10,... | collective-permute-start | bytes 393224 | tf_op jit(solution)/shard_map/ppermute | solution.py:28
  70.2 7.6 %collective-permute-start.21 = (bf16[2,128,256]{2,1,0:T(8,128)(2,1)S(1)}, bf16[2,128,256]{2,1,0:T(8,128)(2,1)S(1)}, u32[]{:S(2)}, u32[]{:S(2)}) collective-permute-start(bf16[2,128,256]{2,1,0:T(8,128)(2,1)S(1)} %get-tuple-element.19), channel_id=1, source_target_pairs={{0,6},{1,7},{2,0},{3,1},{4,2},{5,3},{6,4},{7,5},{8,14},{9,15},{10,... | collective-permute-start | bytes 393224 | tf_op jit(solution)/shard_map/ppermute | solution.py:28
  77.7 6.2 %collective-permute-start.18 = (bf16[2,128,256]{2,1,0:T(8,128)(2,1)S(1)}, bf16[2,128,256]{2,1,0:T(8,128)(2,1)S(1)}, u32[]{:S(2)}, u32[]{:S(2)}) collective-permute-start(bf16[2,128,256]{2,1,0:T(8,128)(2,1)S(1)} %fusion.3), channel_id=1, source_target_pairs={{0,2},{1,3},{2,4},{3,5},{4,6},{5,7},{6,0},{7,1},{8,10},{9,11},{10,... | collective-permute-start | bytes 393224 | tf_op jit(solution)/shard_map/ppermute | solution.py:28
  90.9 6.5 %collective-permute-start.25 = (f32[128,128]{1,0:T(8,128)S(1)}, f32[128,128]{1,0:T(8,128)S(1)}, u32[]{:S(2)}, u32[]{:S(2)}) collective-permute-start(f32[128,128]{1,0:T(8,128)S(1)} %add.160), channel_id=1, source_target_pairs={{0,2},{1,3},{2,4},{3,5},{4,6},{5,7},{6,0},{7,1},{8,10},{9,11},{10,... | collective-permute-start | bytes 196616 | tf_op jit(solution)/shard_map/ppermute | solution.py:28
  90.9 6.5 %collective-permute-start.24 = (f32[128,128]{1,0:T(8,128)S(1)}, f32[128,128]{1,0:T(8,128)S(1)}, u32[]{:S(2)}, u32[]{:S(2)}) collective-permute-start(f32[128,128]{1,0:T(8,128)S(1)} %add.160), channel_id=1, source_target_pairs={{0,4},{1,5},{2,6},{3,7},{4,0},{5,1},{6,2},{7,3},{8,12},{9,13},{10,... | collective-permute-start | bytes 196616 | tf_op jit(solution)/shard_map/ppermute | solution.py:28
  101.4 6.2 %collective-permute-start.28 = (f32[128,128]{1,0:T(8,128)S(1)}, f32[128,128]{1,0:T(8,128)S(1)}, u32[]{:S(2)}, u32[]{:S(2)}) collective-permute-start(f32[128,128]{1,0:T(8,128)S(1)} %add_add_fusion.2), channel_id=1, source_target_pairs={{0,8},{8,16},{16,24},{24,0},{32,40},{40,48},{48,56},{56,32},{64,72... | collective-permute-start | bytes 196616 | tf_op jit(solution)/shard_map/ppermute | solution.py:31
  (14 other events, 66.7 us)

commit v2 on v1

--- a/solution.py
+++ b/solution.py
@@ -11,7 +11,8 @@
 BF = jnp.bfloat16
 F32 = jnp.float32
 UNROLL = 8
-EDGES = (0, 20, 44, 60, 64)
+FIRST = (0, 20, 44, 44)
+WIDTH = (20, 24, 20, 20)
 
 
 def row_id(y, x):
@@ -26,7 +27,7 @@
     if axis == "z":
         pairs = [(col_id(z, k), col_id(z + step, k)) for z in range(4) for k in range(2)]
         return lax.ppermute(a, "col", pairs)
-    dy, dx = (step, 0) if axis == "y" else (0, step)
+    dy, dx = {"y": (step, 0), "x": (0, step), "yx": (step, step)}[axis]
     pairs = [(row_id(y, x), row_id(y + dy, x + dx)) for y in range(4) for x in range(4)]
     return lax.ppermute(a, "row", pairs)
 
@@ -59,23 +60,24 @@
         jnp.where(rel[:, None] == jnp.arange(64, dtype=jnp.int32)[None, :], slot_table()[None, :], 0), axis=1
     )
     ids = jnp.arange(256, dtype=jnp.int32)
-    key = slots * 256 + ids
+    near = (rows // 8 != (z + 2) % 4).astype(jnp.int32)
+    phase = jnp.where(slots < FIRST[1], 0, jnp.where(slots < FIRST[2], 1, 2 + near))
+    key = phase * 256 + ids
     rank = jnp.sum((key[None, :] < key[:, None]).astype(jnp.int32), axis=1)
     fields = jnp.stack([ids, rows, slots, counts])
     placed = jnp.sum(jnp.where(rank[None, :, None] == ids[None, None, :], fields[:, :, None], 0), axis=1)
-    ends = [jnp.sum((slots < edge).astype(jnp.int32)) for edge in EDGES]
-    tail = jnp.stack(ends + [z, k, z, z]).astype(jnp.int32)
-    last = jnp.sum(jnp.where(jnp.arange(9)[:, None] == ids[None, :], tail[:, None], 0), axis=0)
+    starts = jnp.sum((phase[None, :] < ids[:, None]).astype(jnp.int32), axis=1)
+    last = jnp.where(ids < 5, starts, jnp.where(ids == 5, z, k))
     return jnp.concatenate([placed, last[None]], axis=0)
 
 
 def spmm_kernel(phase, meta, nrow, ncol, value, pieces, *rest):
-    first, final = phase == 0, phase == 3
+    first = phase == 0
     rest = list(rest)
     if not first:
         rest.pop(0)
     total = rest.pop(0)
-    if final:
+    if phase >= 2:
         keep, give = rest.pop(0), rest.pop(0)
     value32, iota = rest
     value32[...] = value[...].astype(F32)
@@ -95,7 +97,7 @@
         for u in range(UNROLL):
             columns = ncol[pl.ds(tiles[u], 1), :].astype(F32).astype(BF)
             gather = jnp.where(iota[...] == jnp.broadcast_to(columns, (256, 256)), one, zero)
-            piece = pieces[meta[2, safe[u]] - EDGES[phase]]
+            piece = pieces[meta[2, safe[u]] - FIRST[phase]]
             picked.append(jnp.dot(piece, gather, preferred_element_type=F32).astype(BF))
         for u in range(UNROLL):
             live = jnp.where(at[u] < high, meta[3, safe[u]], 0)
@@ -111,21 +113,22 @@
         return carry
 
     lax.fori_loop(0, (high - low + UNROLL - 1) // UNROLL, step, 0)
-    if final:
+    if phase >= 2:
         z, k = meta[4, 5], meta[4, 6]
-        for dz in range(4):
+        for i, dz in enumerate(((2,), (0, 1, 3))[phase - 2]):
             zz = lax.rem(z + dz, 4) * 2
-            keep[dz] = total[pl.ds((zz + k) * 4, 4)]
-            give[dz] = total[pl.ds((zz + 1 - k) * 4, 4)].astype(BF)
+            keep[i] = total[pl.ds((zz + k) * 4, 4)]
+            give[i] = total[pl.ds((zz + 1 - k) * 4, 4)].astype(BF)
 
 
 def spmm(phase, meta, nrow, ncol, value, pieces, total=None):
     vmem = pl.BlockSpec(memory_space=pltpu.VMEM)
     args = [nrow, ncol, value, pieces] + ([] if total is None else [total])
     out = [jax.ShapeDtypeStruct((32, 128, 256), F32)]
-    if phase == 3:
-        out += [jax.ShapeDtypeStruct((4, 4, 128, 256), F32), jax.ShapeDtypeStruct((4, 4, 128, 256), BF)]
-    share = (EDGES[phase + 1] - EDGES[phase]) / 64
+    if phase >= 2:
+        blocks = (1, 3)[phase - 2]
+        out += [jax.ShapeDtypeStruct((blocks, 4, 128, 256), F32), jax.ShapeDtypeStruct((blocks, 4, 128, 256), BF)]
+    share = WIDTH[phase] / 64 * (1.0, 1.0, 0.25, 0.75)[phase]
     return pl.pallas_call(
         functools.partial(spmm_kernel, phase),
         out_shape=out,
@@ -139,7 +142,7 @@
     )(meta, *args)
 
 
-def finish_kernel(hidden, weight, cotangent, node_out, partial):
+def finish_kernel(col, hidden, weight, cotangent, node_out, keep, give):
     h = [hidden[i] for i in range(4)]
     w = weight[...].astype(F32)
     grad = jnp.zeros((128, 128), F32)
@@ -154,19 +157,21 @@
         slope = sig * (1.0 + pre * (1.0 - sig))
         pre_grad = (cotangent[span, :].astype(F32) * slope).astype(BF).astype(F32)
         grad = grad + jnp.dot(h[i], pre_grad, precision=lax.Precision.HIGHEST, preferred_element_type=F32)
-    partial[...] = grad
-
-
-def finish(hidden, weight, cotangent):
+    low = lax.rem(col[0], 2) == 0
+    keep[...] = jnp.where(low, grad[:64], grad[64:])
+    give[...] = jnp.where(low, grad[64:], grad[:64])
+
+
+def finish(col, hidden, weight, cotangent):
     vmem = pl.BlockSpec(memory_space=pltpu.VMEM)
     return pl.pallas_call(
         finish_kernel,
-        out_shape=[jax.ShapeDtypeStruct((1024, 128), BF), jax.ShapeDtypeStruct((128, 128), F32)],
-        in_specs=[vmem] * 3,
-        out_specs=[vmem] * 2,
+        out_shape=[jax.ShapeDtypeStruct((1024, 128), BF)] + [jax.ShapeDtypeStruct((64, 128), F32)] * 2,
+        in_specs=[pl.BlockSpec(memory_space=pltpu.SMEM)] + [vmem] * 3,
+        out_specs=[vmem] * 3,
         compiler_params=pltpu.CompilerParams(vmem_limit_bytes=16 << 20),
         name="finish",
-    )(hidden, weight, cotangent)
+    )(col.reshape(1), hidden, weight, cotangent)
 
 
 def cat(*parts):
@@ -199,27 +204,25 @@
     r3, l3 = shift(along, "x", 1), shift(along, "x", -1)
     d3, u3 = shift(across, "y", 1), shift(across, "y", -1)
     (total,) = spmm(1, *slots, cat(r2, l2, d2, u2), total)
-    r4, l4 = shift(r3[0:1], "x", 1), shift(l3[1:2], "x", -1)
-    d4, u4 = shift(d3[2:3], "y", 1), shift(u3[3:4], "y", -1)
-    (total,) = spmm(2, *slots, cat(r3, l3, d3, u3), total)
-    total, keep, give = spmm(3, *slots, cat(r4, l4, d4, u4), total)
-
+    a3, b3 = shift(d2[2:4], "yx", 1), shift(u2[4:6], "yx", -1)
+    last = cat(r3, l3, d3, u3, a3, b3)
+
+    total, keep, give = spmm(2, *slots, last, total)
+    far = add(keep[0], swap_cores(give)[0]).astype(BF)
+    far_up, far_down = shift(far[:2], "z", 1), shift(far[2:], "z", -1)
+    total, keep, give = spmm(3, *slots, last, total)
     got = swap_cores(give)
-    mine = add(keep[0], got[0])
-    far = add(keep[2], got[2]).astype(BF)
-    up32, down32 = add(keep[1], got[1]), add(keep[3], got[3])
-    far_up = shift(far[:2], "z", 1)
-    far_down = shift(far[2:], "z", -1)
-    near_up = shift(up32[2:].astype(BF), "z", 1)
-    near_down = shift(down32[:2].astype(BF), "z", -1)
-    sum_up = shift(add(up32[:2], far_up).astype(BF), "z", 1)
-    sum_down = shift(add(down32[2:], far_down).astype(BF), "z", -1)
-    hidden = mine + cat(add(sum_up, near_down), add(near_up, sum_down))
-
-    node_out, partial = finish(hidden, weight, cotangent)
-    grad = partial + swap_cores(partial)
+    mine, up, down = add(keep[0], got[0]), add(keep[1], got[1]), add(keep[2], got[2])
+    up = shift(cat(add(up[:2], far_up), up[2:]).astype(BF), "z", 1)
+    down = shift(cat(down[:2], add(down[2:], far_down)).astype(BF), "z", -1)
+    hidden = mine + add(up, down)
+
+    node_out, grad, other = finish(col, hidden, weight, cotangent)
+    grad = grad + swap_cores(other)
     for axis in ("z", "x", "y"):
         grad = sum_ring(grad, axis)
+    other = swap_cores(grad)
+    grad = jnp.where(col % 2 == 0, cat(grad, other), cat(other, grad))
     return node_out, grad
 
 

time: 117 us -> 118 us (level)
  waiting for transfers between devices: 26.9 us -> 36.3 us
  starting transfers between devices: 49.9 us -> 43.3 us
  local copies, waits for them, and re-layouts: 4.61 us -> 1.46 us
    ppermute x9 -> x7, starting transfers between devices: 16 us -> 10.2 us  [shift(): return lax.ppermute(a, 'col', pairs)]
    ppermute x9 -> x7, waiting for transfers between devices: 12 us -> 17.5 us  [shift(): return lax.ppermute(a, 'col', pairs)]
    another operation x1 -> x0, local copies, waits for them, and re-layouts: 3.24 us -> none  [plan_tiles(): tail = jnp.stack(ends + [z, k, z, z]).astype(jnp.int32)]
    ppermute x22 -> x20, waiting for transfers between devices: 11.1 us -> 14.3 us  [shift(): return lax.ppermute(a, 'row', pairs)]
    ppermute x22 -> x20, starting transfers between devices: 33.9 us -> 32.5 us  [shift(): return lax.ppermute(a, 'row', pairs)]
    ppermute x2 -> x4, waiting for transfers between devices: 3.9 us -> 4.55 us  [swap_cores(): lax.ppermute(a, 'col', [(col_id(z, k), col_id(z, 1 - k)) for z in range(4...]
  transfers between devices with their start and end apart: 33 -> 31, of which waited for: 12 -> 15; matrix products, arithmetic and copies ran while one was open for 7% -> 4% of each run, Pallas kernels for 20% -> 16%
where the time goes in v2:
time: 118 us; the launch traced here: 116 us
  starting transfers between devices  43.3 us (37%)
  waiting for transfers between devices  36.3 us (31%)
  Pallas kernels  28.9 us (24%)
  other arithmetic  4.96 us (4%)
  local copies, waits for them, and re-layouts  1.46 us (1%)
  between operations  1.22 us (1%)
    ppermute x20, starting transfers between devices, shift(): return lax.ppermute(a, 'row', pairs)  32.5 us
    pallas_call x4, Pallas kernels, spmm(): pl.pallas_call(functools.partial(spmm_kernel, phase), out_shape=out, in_s...  26.8 us
    ppermute x7, waiting for transfers between devices, shift(): return lax.ppermute(a, 'col', pairs)  17.5 us
    ppermute x20, waiting for transfers between devices, shift(): return lax.ppermute(a, 'row', pairs)  14.3 us
    ppermute x7, starting transfers between devices, shift(): return lax.ppermute(a, 'col', pairs)  10.2 us
    ppermute x4, waiting for transfers between devices, swap_cores(): lax.ppermute(a, 'col', [(col_id(z, k), col_id(z, 1 - k)) for z in range(4...  4.55 us
  transfers between devices with their start and end apart: 31, of which 15 were waited for; matrix products, arithmetic and copies ran while one was open for 4% of the time, Pallas kernels for 16%

profile of v2, /device:TPU:0, one launch (start us, length us, event | category | flops | bytes accessed | tf_op | source)
XLA Modules:
  0.0 116.2 jit_solution(14774818949606532177)
XLA Ops:
  1.7 2.9 %collective-permute-start.4 = (bf16[4,128,256]{2,1,0:T(8,128)(2,1)S(1)}, bf16[4,128,256]{2,1,0:T(8,128)(2,1)S(1)}, u32[]{:S(2)}, u32[]{:S(2)}) collective-permute-start(bf16[4,128,256]{2,1,0:T(8,128)(2,1)S(1)} %bitcast.47), channel_id=1, source_target_pairs={{0,24},{8,0},{16,8},{24,16},{32,56},{40,32},{48,40},{56,48},{64,88... | collective-permute-start | bytes 786440 | tf_op jit(solution)/shard_map/ppermute | solution.py:32
  4.6 3.0 %collective-permute-start.3 = (bf16[4,128,256]{2,1,0:T(8,128)(2,1)S(1)}, bf16[4,128,256]{2,1,0:T(8,128)(2,1)S(1)}, u32[]{:S(2)}, u32[]{:S(2)}) collective-permute-start(bf16[4,128,256]{2,1,0:T(8,128)(2,1)S(1)} %bitcast.48), channel_id=1, source_target_pairs={{0,96},{8,104},{16,112},{24,120},{32,0},{40,8},{48,16},{56,24},{64... | collective-permute-start | bytes 786440 | tf_op jit(solution)/shard_map/ppermute | solution.py:32
  11.2 5.2 %collective-permute-done = bf16[4,128,256]{2,1,0:T(8,128)(2,1)S(1)} collective-permute-done((bf16[4,128,256]{2,1,0:T(8,128)(2,1)S(1)}, bf16[4,128,256]{2,1,0:T(8,128)(2,1)S(1)}, u32[]{:S(2)}, u32[]{:S(2)}) %collective-permute-start) | collective-permute-done | bytes 262176 | tf_op jit(solution)/shard_map/ppermute | solution.py:32
  16.4 3.0 %collective-permute-start.9 = (bf16[6,128,256]{2,1,0:T(8,128)(2,1)S(1)}, bf16[6,128,256]{2,1,0:T(8,128)(2,1)S(1)}, u32[]{:S(2)}, u32[]{:S(2)}) collective-permute-start(bf16[6,128,256]{2,1,0:T(8,128)(2,1)S(1)} %pad_maximum_fusion.4), channel_id=1, source_target_pairs={{0,24},{8,0},{16,8},{24,16},{32,56},{40,32},{48,40},{56,48},{64,88... | collective-permute-start | bytes 1179656 | tf_op jit(solution)/shard_map/ppermute | solution.py:32
  19.8 3.3 %collective-permute-start.5 = (bf16[6,128,256]{2,1,0:T(8,128)(2,1)S(1)}, bf16[6,128,256]{2,1,0:T(8,128)(2,1)S(1)}, u32[]{:S(2)}, u32[]{:S(2)}) collective-permute-start(bf16[6,128,256]{2,1,0:T(8,128)(2,1)S(1)} %pad_maximum_fusion.2), channel_id=1, source_target_pairs={{0,96},{8,104},{16,112},{24,120},{32,0},{40,8},{48,16},{56,24},{64... | collective-permute-start | bytes 1179656 | tf_op jit(solution)/shard_map/ppermute | solution.py:32
  23.2 8.5 %spmm_phase0.1.rest_0_ = f32[32,128,256]{2,1,0:T(8,128)S(1)} custom-call(s32[5,256]{1,0:T(8,128)S(1)} %pad_add_fusion.meta, s32[256,256]{1,0:T(8,128)S(1)} %bitcast.35, s32[256,256]{1,0:T(8,128)S(1)} %bitcast.39, bf16[256,256]{1,0:T(8,128)(2,1)S(1)} %bitcast.43, bf16[20,128,256]{2,1,0:T(8,128)(2,1)S(1)} %constant_dynamic-update-slice_fusion.6.pieces), custom_call_target="tpu_custom_call" | custom-call | flops 9374999552 | bytes 1048576 | tf_op jit(solution)/shard_map/spmm_phase0/pallas_call | solution.py:132
  34.1 2.6 %collective-permute-start.7 = (bf16[4,128,256]{2,1,0:T(8,128)(2,1)S(1)}, bf16[4,128,256]{2,1,0:T(8,128)(2,1)S(1)}, u32[]{:S(2)}, u32[]{:S(2)}) collective-permute-start(bf16[4,128,256]{2,1,0:T(8,128)(2,1)S(1)} %pad_maximum_fusion.5), channel_id=1, source_target_pairs={{0,24},{8,0},{16,8},{24,16},{32,56},{40,32},{48,40},{56,48},{64,88... | collective-permute-start | bytes 786440 | tf_op jit(solution)/shard_map/ppermute | solution.py:32
  36.9 9.7 %spmm_phase1.1.rest_0_ = f32[32,128,256]{2,1,0:T(8,128)S(1)} custom-call(s32[5,256]{1,0:T(8,128)S(1)} %pad_add_fusion.meta, s32[256,256]{1,0:T(8,128)S(1)} %bitcast.36, s32[256,256]{1,0:T(8,128)S(1)} %bitcast.40, bf16[256,256]{1,0:T(8,128)(2,1)S(1)} %bitcast.44, bf16[24,128,256]{2,1,0:T(8,128)(2,1)S(1)} %pad_maximum_fusion.pieces, ...), custom_call_target="tpu_custom_call", output_to_operand_aliasing={{}: (5, {})} | custom-call | flops 11249999872 | bytes 1048576 | tf_op jit(solution)/shard_map/spmm_phase1/pallas_call | solution.py:132
  46.6 4.7 %collective-permute-start.13 = (bf16[2,128,256]{2,1,0:T(8,128)(2,1)S(1)}, bf16[2,128,256]{2,1,0:T(8,128)(2,1)S(1)}, u32[]{:S(2)}, u32[]{:S(2)}) collective-permute-start(bf16[2,128,256]{2,1,0:T(8,128)(2,1)S(1)} %get-tuple-element.22), channel_id=1, source_target_pairs={{0,120},{8,96},{16,104},{24,112},{32,24},{40,0},{48,8},{56,16},{64... | collective-permute-start | bytes 393224 | tf_op jit(solution)/shard_map/ppermute | solution.py:32
  51.5 2.4 %collective-permute-done.13 = bf16[2,128,256]{2,1,0:T(8,128)(2,1)S(1)} collective-permute-done((bf16[2,128,256]{2,1,0:T(8,128)(2,1)S(1)}, bf16[2,128,256]{2,1,0:T(8,128)(2,1)S(1)}, u32[]{:S(2)}, u32[]{:S(2)}) %collective-permute-start.13) | collective-permute-done | bytes 131104 | tf_op jit(solution)/shard_map/ppermute | solution.py:32
  53.8 2.2 %spmm_phase2.1 = (f32[32,128,256]{2,1,0:T(8,128)S(1)}, f32[1,4,128,256]{3,2,1,0:T(8,128)S(1)}, bf16[1,4,128,256]{3,2,1,0:T(8,128)(2,1)S(1)}) custom-call(s32[5,256]{1,0:T(8,128)S(1)} %pad_add_fusion.meta, s32[256,256]{1,0:T(8,128)S(1)} %bitcast.37, s32[256,256]{1,0:T(8,128)S(1)} %bitcast.41, ...), custom_call_target="tpu_custom_call", output_to_operand_aliasing={{0}: (5, {})} | custom-call | flops 2343749888 | bytes 1048576 | tf_op jit(solution)/shard_map/spmm_phase2/pallas_call | solution.py:132
  56.0 6.4 %spmm_phase3.1 = (f32[32,128,256]{2,1,0:T(8,128)S(1)}, f32[3,4,128,256]{3,2,1,0:T(8,128)S(1)}, bf16[3,4,128,256]{3,2,1,0:T(8,128)(2,1)S(1)}) custom-call(s32[5,256]{1,0:T(8,128)S(1)} %pad_add_fusion.meta, s32[256,256]{1,0:T(8,128)S(1)} %bitcast.38, s32[256,256]{1,0:T(8,128)S(1)} %bitcast.42, ...), custom_call_target="tpu_custom_call", output_to_operand_aliasing={{0}: (5, {})} | custom-call | flops 7031249920 | bytes 1048576 | tf_op jit(solution)/shard_map/spmm_phase3/pallas_call | solution.py:132
  63.0 2.1 %collective-permute-done.15 = bf16[1,4,128,256]{3,2,1,0:T(8,128)(2,1)S(1)} collective-permute-done((bf16[1,4,128,256]{3,2,1,0:T(8,128)(2,1)S(1)}, bf16[1,4,128,256]{3,2,1,0:T(8,128)(2,1)S(1)}, u32[]{:S(2)}, u32[]{:S(2)}) %collective-permute-start.15) | collective-permute-done | bytes 262176 | tf_op jit(solution)/shard_map/ppermute | solution.py:36
  65.3 3.4 %collective-permute-start.16 = (bf16[2,128,256]{2,1,0:T(8,128)(2,1)S(1)}, bf16[2,128,256]{2,1,0:T(8,128)(2,1)S(1)}, u32[]{:S(2)}, u32[]{:S(2)}) collective-permute-start(bf16[2,128,256]{2,1,0:T(8,128)(2,1)S(1)} %get-tuple-element.26), channel_id=1, source_target_pairs={{0,2},{1,3},{2,4},{3,5},{4,6},{5,7},{6,0},{7,1},{8,10},{9,11},{10,... | collective-permute-start | bytes 393224 | tf_op jit(solution)/shard_map/ppermute | solution.py:29
  70.3 3.6 %collective-permute-done.18 = bf16[2,128,256]{2,1,0:T(8,128)(2,1)S(1)} collective-permute-done((bf16[2,128,256]{2,1,0:T(8,128)(2,1)S(1)}, bf16[2,128,256]{2,1,0:T(8,128)(2,1)S(1)}, u32[]{:S(2)}, u32[]{:S(2)}) %collective-permute-start.18) | collective-permute-done | bytes 131104 | tf_op jit(solution)/shard_map/ppermute | solution.py:29
  74.0 3.2 %collective-permute-start.19 = (bf16[4,128,256]{2,1,0:T(8,128)(2,1)S(1)}, bf16[4,128,256]{2,1,0:T(8,128)(2,1)S(1)}, u32[]{:S(2)}, u32[]{:S(2)}) collective-permute-start(bf16[4,128,256]{2,1,0:T(8,128)(2,1)S(1)} %pad_maximum_fusion.8), channel_id=1, source_target_pairs={{0,6},{1,7},{2,0},{3,1},{4,2},{5,3},{6,4},{7,5},{8,14},{9,15},{10,... | collective-permute-start | bytes 786440 | tf_op jit(solution)/shard_map/ppermute | solution.py:29
  77.4 4.8 %collective-permute-done.19 = bf16[4,128,256]{2,1,0:T(8,128)(2,1)S(1)} collective-permute-done((bf16[4,128,256]{2,1,0:T(8,128)(2,1)S(1)}, bf16[4,128,256]{2,1,0:T(8,128)(2,1)S(1)}, u32[]{:S(2)}, u32[]{:S(2)}) %collective-permute-start.19) | collective-permute-done | bytes 262176 | tf_op jit(solution)/shard_map/ppermute | solution.py:29
  82.2 3.6 %collective-permute-done.17 = bf16[4,128,256]{2,1,0:T(8,128)(2,1)S(1)} collective-permute-done((bf16[4,128,256]{2,1,0:T(8,128)(2,1)S(1)}, bf16[4,128,256]{2,1,0:T(8,128)(2,1)S(1)}, u32[]{:S(2)}, u32[]{:S(2)}) %collective-permute-start.17) | collective-permute-done | bytes 262176 | tf_op jit(solution)/shard_map/ppermute | solution.py:29
  94.5 2.2 %collective-permute-done.21 = f32[64,128]{1,0:T(8,128)S(1)} collective-permute-done((f32[64,128]{1,0:T(8,128)S(1)}, f32[64,128]{1,0:T(8,128)S(1)}, u32[]{:S(2)}, u32[]{:S(2)}) %collective-permute-start.21) | collective-permute-done | bytes 32800 | tf_op jit(solution)/shard_map/ppermute | solution.py:29
  96.8 3.9 %collective-permute-start.26 = (f32[64,128]{1,0:T(8,128)S(1)}, f32[64,128]{1,0:T(8,128)S(1)}, u32[]{:S(2)}, u32[]{:S(2)}) collective-permute-start(f32[64,128]{1,0:T(8,128)S(1)} %add_add_fusion.2), channel_id=1, source_target_pairs={{0,24},{8,0},{16,8},{24,16},{32,56},{40,32},{48,40},{56,48},{64,88... | collective-permute-start | bytes 98312 | tf_op jit(solution)/shard_map/ppermute | solution.py:32
  100.7 2.4 %collective-permute-start.24 = (f32[64,128]{1,0:T(8,128)S(1)}, f32[64,128]{1,0:T(8,128)S(1)}, u32[]{:S(2)}, u32[]{:S(2)}) collective-permute-start(f32[64,128]{1,0:T(8,128)S(1)} %add_add_fusion.2), channel_id=1, source_target_pairs={{0,16},{8,24},{16,0},{24,8},{32,48},{40,56},{48,32},{56,40},{64,80... | collective-permute-start | bytes 98312 | tf_op jit(solution)/shard_map/ppermute | solution.py:32
  103.1 2.7 %collective-permute-done.25 = f32[64,128]{1,0:T(8,128)S(1)} collective-permute-done((f32[64,128]{1,0:T(8,128)S(1)}, f32[64,128]{1,0:T(8,128)S(1)}, u32[]{:S(2)}, u32[]{:S(2)}) %collective-permute-start.25) | collective-permute-done | bytes 32800 | tf_op jit(solution)/shard_map/ppermute | solution.py:32
  106.2 2.6 %collective-permute-start.29 = (f32[64,128]{1,0:T(8,128)S(1)}, f32[64,128]{1,0:T(8,128)S(1)}, u32[]{:S(2)}, u32[]{:S(2)}) collective-permute-start(f32[64,128]{1,0:T(8,128)S(1)} %add_add_fusion.1), channel_id=1, source_target_pairs={{0,96},{8,104},{16,112},{24,120},{32,0},{40,8},{48,16},{56,24},{64... | collective-permute-start | bytes 98312 | tf_op jit(solution)/shard_map/ppermute | solution.py:32
  110.5 3.4 %collective-permute-done.28 = f32[64,128]{1,0:T(8,128)S(1)} collective-permute-done((f32[64,128]{1,0:T(8,128)S(1)}, f32[64,128]{1,0:T(8,128)S(1)}, u32[]{:S(2)}, u32[]{:S(2)}) %collective-permute-start.28) | collective-permute-done | bytes 32800 | tf_op jit(solution)/shard_map/ppermute | solution.py:32
  (105 shorter events, 23.1 us)
Async XLA Ops:
  1.7 9.4 %collective-permute-start.4 = (bf16[4,128,256]{2,1,0:T(8,128)(2,1)S(1)}, bf16[4,128,256]{2,1,0:T(8,128)(2,1)S(1)}, u32[]{:S(2)}, u32[]{:S(2)}) collective-permute-start(bf16[4,128,256]{2,1,0:T(8,128)(2,1)S(1)} %bitcast.47), channel_id=1, source_target_pairs={{0,24},{8,0},{16,8},{24,16},{32,56},{40,32},{48,40},{56,48},{64,88... | collective-permute-start | bytes 786440 | tf_op jit(solution)/shard_map/ppermute | solution.py:32
  4.6 14.9 %collective-permute-start.3 = (bf16[4,128,256]{2,1,0:T(8,128)(2,1)S(1)}, bf16[4,128,256]{2,1,0:T(8,128)(2,1)S(1)}, u32[]{:S(2)}, u32[]{:S(2)}) collective-permute-start(bf16[4,128,256]{2,1,0:T(8,128)(2,1)S(1)} %bitcast.48), channel_id=1, source_target_pairs={{0,96},{8,104},{16,112},{24,120},{32,0},{40,8},{48,16},{56,24},{64... | collective-permute-start | bytes 786440 | tf_op jit(solution)/shard_map/ppermute | solution.py:32
  7.6 11.8 %collective-permute-start.1 = (bf16[4,128,256]{2,1,0:T(8,128)(2,1)S(1)}, bf16[4,128,256]{2,1,0:T(8,128)(2,1)S(1)}, u32[]{:S(2)}, u32[]{:S(2)}) collective-permute-start(bf16[4,128,256]{2,1,0:T(8,128)(2,1)S(1)} %bitcast.49), channel_id=1, source_target_pairs={{0,8},{8,16},{16,24},{24,0},{32,40},{40,48},{48,56},{56,32},{64,72... | collective-permute-start | bytes 786440 | tf_op jit(solution)/shard_map/ppermute | solution.py:32
  7.7 8.7 %collective-permute-start = (bf16[4,128,256]{2,1,0:T(8,128)(2,1)S(1)}, bf16[4,128,256]{2,1,0:T(8,128)(2,1)S(1)}, u32[]{:S(2)}, u32[]{:S(2)}) collective-permute-start(bf16[4,128,256]{2,1,0:T(8,128)(2,1)S(1)} %bitcast.50), channel_id=1, source_target_pairs={{0,32},{8,40},{16,48},{24,56},{32,64},{40,72},{48,80},{56,88},{64,... | collective-permute-start | bytes 786440 | tf_op jit(solution)/shard_map/ppermute | solution.py:32
  16.4 15.4 %collective-permute-start.9 = (bf16[6,128,256]{2,1,0:T(8,128)(2,1)S(1)}, bf16[6,128,256]{2,1,0:T(8,128)(2,1)S(1)}, u32[]{:S(2)}, u32[]{:S(2)}) collective-permute-start(bf16[6,128,256]{2,1,0:T(8,128)(2,1)S(1)} %pad_maximum_fusion.4), channel_id=1, source_target_pairs={{0,24},{8,0},{16,8},{24,16},{32,56},{40,32},{48,40},{56,48},{64,88... | collective-permute-start | bytes 1179656 | tf_op jit(solution)/shard_map/ppermute | solution.py:32
  19.5 14.5 %collective-permute-start.2 = (bf16[6,128,256]{2,1,0:T(8,128)(2,1)S(1)}, bf16[6,128,256]{2,1,0:T(8,128)(2,1)S(1)}, u32[]{:S(2)}, u32[]{:S(2)}) collective-permute-start(bf16[6,128,256]{2,1,0:T(8,128)(2,1)S(1)} %pad_maximum_fusion.1), channel_id=1, source_target_pairs={{0,32},{8,40},{16,48},{24,56},{32,64},{40,72},{48,80},{56,88},{64,... | collective-permute-start | bytes 1179656 | tf_op jit(solution)/shard_map/ppermute | solution.py:32
  19.6 12.2 %collective-permute-start.8 = (bf16[6,128,256]{2,1,0:T(8,128)(2,1)S(1)}, bf16[6,128,256]{2,1,0:T(8,128)(2,1)S(1)}, u32[]{:S(2)}, u32[]{:S(2)}) collective-permute-start(bf16[6,128,256]{2,1,0:T(8,128)(2,1)S(1)} %pad_maximum_fusion.3), channel_id=1, source_target_pairs={{0,8},{8,16},{16,24},{24,0},{32,40},{40,48},{48,56},{56,32},{64,72... | collective-permute-start | bytes 1179656 | tf_op jit(solution)/shard_map/ppermute | solution.py:32
  19.8 14.2 %collective-permute-start.5 = (bf16[6,128,256]{2,1,0:T(8,128)(2,1)S(1)}, bf16[6,128,256]{2,1,0:T(8,128)(2,1)S(1)}, u32[]{:S(2)}, u32[]{:S(2)}) collective-permute-start(bf16[6,128,256]{2,1,0:T(8,128)(2,1)S(1)} %pad_maximum_fusion.2), channel_id=1, source_target_pairs={{0,96},{8,104},{16,112},{24,120},{32,0},{40,8},{48,16},{56,24},{64... | collective-permute-start | bytes 1179656 | tf_op jit(solution)/shard_map/ppermute | solution.py:32
  31.9 19.5 %collective-permute-start.11 = (bf16[4,128,256]{2,1,0:T(8,128)(2,1)S(1)}, bf16[4,128,256]{2,1,0:T(8,128)(2,1)S(1)}, u32[]{:S(2)}, u32[]{:S(2)}) collective-permute-start(bf16[4,128,256]{2,1,0:T(8,128)(2,1)S(1)} %pad_maximum_fusion.6), channel_id=1, source_target_pairs={{0,96},{8,104},{16,112},{24,120},{32,0},{40,8},{48,16},{56,24},{64... | collective-permute-start | bytes 786440 | tf_op jit(solution)/shard_map/ppermute | solution.py:32
  32.8 18.6 %collective-permute-start.10 = (bf16[4,128,256]{2,1,0:T(8,128)(2,1)S(1)}, bf16[4,128,256]{2,1,0:T(8,128)(2,1)S(1)}, u32[]{:S(2)}, u32[]{:S(2)}) collective-permute-start(bf16[4,128,256]{2,1,0:T(8,128)(2,1)S(1)} %pad_maximum_fusion.6), channel_id=1, source_target_pairs={{0,32},{8,40},{16,48},{24,56},{32,64},{40,72},{48,80},{56,88},{64,... | collective-permute-start | bytes 786440 | tf_op jit(solution)/shard_map/ppermute | solution.py:32
  34.1 17.3 %collective-permute-start.7 = (bf16[4,128,256]{2,1,0:T(8,128)(2,1)S(1)}, bf16[4,128,256]{2,1,0:T(8,128)(2,1)S(1)}, u32[]{:S(2)}, u32[]{:S(2)}) collective-permute-start(bf16[4,128,256]{2,1,0:T(8,128)(2,1)S(1)} %pad_maximum_fusion.5), channel_id=1, source_target_pairs={{0,24},{8,0},{16,8},{24,16},{32,56},{40,32},{48,40},{56,48},{64,88... | collective-permute-start | bytes 786440 | tf_op jit(solution)/shard_map/ppermute | solution.py:32
  36.7 9.9 %collective-permute-start.6 = (bf16[4,128,256]{2,1,0:T(8,128)(2,1)S(1)}, bf16[4,128,256]{2,1,0:T(8,128)(2,1)S(1)}, u32[]{:S(2)}, u32[]{:S(2)}) collective-permute-start(bf16[4,128,256]{2,1,0:T(8,128)(2,1)S(1)} %pad_maximum_fusion.5), channel_id=1, source_target_pairs={{0,8},{8,16},{16,24},{24,0},{32,40},{40,48},{48,56},{56,32},{64,72... | collective-permute-start | bytes 786440 | tf_op jit(solution)/shard_map/ppermute | solution.py:32
  36.7 14.8 %collective-permute-start.12 = (bf16[2,128,256]{2,1,0:T(8,128)(2,1)S(1)}, bf16[2,128,256]{2,1,0:T(8,128)(2,1)S(1)}, u32[]{:S(2)}, u32[]{:S(2)}) collective-permute-start(bf16[2,128,256]{2,1,0:T(8,128)(2,1)S(1)} %get-tuple-element.24), channel_id=1, source_target_pairs={{0,40},{8,48},{16,56},{24,32},{32,72},{40,80},{48,88},{56,64},{64,... | collective-permute-start | bytes 393224 | tf_op jit(solution)/shard_map/ppermute | solution.py:32
  46.6 7.3 %collective-permute-start.13 = (bf16[2,128,256]{2,1,0:T(8,128)(2,1)S(1)}, bf16[2,128,256]{2,1,0:T(8,128)(2,1)S(1)}, u32[]{:S(2)}, u32[]{:S(2)}) collective-permute-start(bf16[2,128,256]{2,1,0:T(8,128)(2,1)S(1)} %get-tuple-element.22), channel_id=1, source_target_pairs={{0,120},{8,96},{16,104},{24,112},{32,24},{40,0},{48,8},{56,16},{64... | collective-permute-start | bytes 393224 | tf_op jit(solution)/shard_map/ppermute | solution.py:32
  62.4 7.7 %collective-permute-start.14 = (bf16[3,4,128,256]{3,2,1,0:T(8,128)(2,1)S(1)}, bf16[3,4,128,256]{3,2,1,0:T(8,128)(2,1)S(1)}, u32[]{:S(2)}, u32[]{:S(2)}) collective-permute-start(bf16[3,4,128,256]{3,2,1,0:T(8,128)(2,1)S(1)} %get-tuple-element.12), channel_id=1, source_target_pairs={{0,1},{1,0},{2,3},{3,2},{4,5},{5,4},{6,7},{7,6},{8,9},{9,8},{10,11... | collective-permute-start | bytes 2359304 | tf_op jit(solution)/shard_map/ppermute | solution.py:36
  65.3 11.9 %collective-permute-start.16 = (bf16[2,128,256]{2,1,0:T(8,128)(2,1)S(1)}, bf16[2,128,256]{2,1,0:T(8,128)(2,1)S(1)}, u32[]{:S(2)}, u32[]{:S(2)}) collective-permute-start(bf16[2,128,256]{2,1,0:T(8,128)(2,1)S(1)} %get-tuple-element.26), channel_id=1, source_target_pairs={{0,2},{1,3},{2,4},{3,5},{4,6},{5,7},{6,0},{7,1},{8,10},{9,11},{10,... | collective-permute-start | bytes 393224 | tf_op jit(solution)/shard_map/ppermute | solution.py:29
  68.6 5.3 %collective-permute-start.18 = (bf16[2,128,256]{2,1,0:T(8,128)(2,1)S(1)}, bf16[2,128,256]{2,1,0:T(8,128)(2,1)S(1)}, u32[]{:S(2)}, u32[]{:S(2)}) collective-permute-start(bf16[2,128,256]{2,1,0:T(8,128)(2,1)S(1)} %get-tuple-element.27), channel_id=1, source_target_pairs={{0,6},{1,7},{2,0},{3,1},{4,2},{5,3},{6,4},{7,5},{8,14},{9,15},{10,... | collective-permute-start | bytes 393224 | tf_op jit(solution)/shard_map/ppermute | solution.py:29
  74.0 8.2 %collective-permute-start.19 = (bf16[4,128,256]{2,1,0:T(8,128)(2,1)S(1)}, bf16[4,128,256]{2,1,0:T(8,128)(2,1)S(1)}, u32[]{:S(2)}, u32[]{:S(2)}) collective-permute-start(bf16[4,128,256]{2,1,0:T(8,128)(2,1)S(1)} %pad_maximum_fusion.8), channel_id=1, source_target_pairs={{0,6},{1,7},{2,0},{3,1},{4,2},{5,3},{6,4},{7,5},{8,14},{9,15},{10,... | collective-permute-start | bytes 786440 | tf_op jit(solution)/shard_map/ppermute | solution.py:29
  77.3 8.5 %collective-permute-start.17 = (bf16[4,128,256]{2,1,0:T(8,128)(2,1)S(1)}, bf16[4,128,256]{2,1,0:T(8,128)(2,1)S(1)}, u32[]{:S(2)}, u32[]{:S(2)}) collective-permute-start(bf16[4,128,256]{2,1,0:T(8,128)(2,1)S(1)} %pad_maximum_fusion.7), channel_id=1, source_target_pairs={{0,2},{1,3},{2,4},{3,5},{4,6},{5,7},{6,0},{7,1},{8,10},{9,11},{10,... | collective-permute-start | bytes 786440 | tf_op jit(solution)/shard_map/ppermute | solution.py:29
  91.4 5.4 %collective-permute-start.21 = (f32[64,128]{1,0:T(8,128)S(1)}, f32[64,128]{1,0:T(8,128)S(1)}, u32[]{:S(2)}, u32[]{:S(2)}) collective-permute-start(f32[64,128]{1,0:T(8,128)S(1)} %add.193), channel_id=1, source_target_pairs={{0,4},{1,5},{2,6},{3,7},{4,0},{5,1},{6,2},{7,3},{8,12},{9,13},{10,... | collective-permute-start | bytes 98312 | tf_op jit(solution)/shard_map/ppermute | solution.py:29
  96.8 6.3 %collective-permute-start.26 = (f32[64,128]{1,0:T(8,128)S(1)}, f32[64,128]{1,0:T(8,128)S(1)}, u32[]{:S(2)}, u32[]{:S(2)}) collective-permute-start(f32[64,128]{1,0:T(8,128)S(1)} %add_add_fusion.2), channel_id=1, source_target_pairs={{0,24},{8,0},{16,8},{24,16},{32,56},{40,32},{48,40},{56,48},{64,88... | collective-permute-start | bytes 98312 | tf_op jit(solution)/shard_map/ppermute | solution.py:32
  100.7 5.1 %collective-permute-start.25 = (f32[64,128]{1,0:T(8,128)S(1)}, f32[64,128]{1,0:T(8,128)S(1)}, u32[]{:S(2)}, u32[]{:S(2)}) collective-permute-start(f32[64,128]{1,0:T(8,128)S(1)} %add_add_fusion.2), channel_id=1, source_target_pairs={{0,8},{8,16},{16,24},{24,0},{32,40},{40,48},{48,56},{56,32},{64,72... | collective-permute-start | bytes 98312 | tf_op jit(solution)/shard_map/ppermute | solution.py:32
  100.7 5.5 %collective-permute-start.24 = (f32[64,128]{1,0:T(8,128)S(1)}, f32[64,128]{1,0:T(8,128)S(1)}, u32[]{:S(2)}, u32[]{:S(2)}) collective-permute-start(f32[64,128]{1,0:T(8,128)S(1)} %add_add_fusion.2), channel_id=1, source_target_pairs={{0,16},{8,24},{16,0},{24,8},{32,48},{40,56},{48,32},{56,40},{64,80... | collective-permute-start | bytes 98312 | tf_op jit(solution)/shard_map/ppermute | solution.py:32
  108.7 5.5 %collective-permute-start.27 = (f32[64,128]{1,0:T(8,128)S(1)}, f32[64,128]{1,0:T(8,128)S(1)}, u32[]{:S(2)}, u32[]{:S(2)}) collective-permute-start(f32[64,128]{1,0:T(8,128)S(1)} %add_add_fusion.1), channel_id=1, source_target_pairs={{0,64},{8,72},{16,80},{24,88},{32,96},{40,104},{48,112},{56,120},{... | collective-permute-start | bytes 98312 | tf_op jit(solution)/shard_map/ppermute | solution.py:32
  (12 other events, 51.5 us)

commit v3 on v2

v3 whole, which is shorter than its diff:
```python
import functools

import jax
import jax.numpy as jnp
from jax import lax
from jax.experimental import pallas as pl
from jax.experimental.pallas import tpu as pltpu
from jax.sharding import PartitionSpec as P

BF = jnp.bfloat16
F32 = jnp.float32
UNROLL = 16
FIRST = (0, 16, 40, 40)
PLUS = 6


def permute(a, move):
    pairs = []
    for i in range(128):
        y, x, z, k = i // 32, i // 8 % 4, i // 2 % 4, i % 2
        y, x, z, k = (v % 4 for v in move(y, x, z, k))
        pairs.append((i, y * 32 + x * 8 + z * 2 + k))
    return lax.ppermute(a, ("row", "col"), pairs)


def first_axis(a, step):
    return permute(a, lambda y, x, z, k: (y + step * k, x + step * (1 - k), z, k))


def second_axis(a, step):
    return permute(a, lambda y, x, z, k: (y + step * (1 - k), x + step * k, z, k))


def swap_cores(a):
    return permute(a, lambda y, x, z, k: (y, x, z, 1 - k))


def shift(a, axis, step):
    by = [step * (axis == name) for name in "yxz"]
    return permute(a, lambda y, x, z, k: (y + by[0], x + by[1], z + by[2], k))


def plan_tiles(rows, cols, counts, y, x, z, k):
    source = cols // 4
    dy, dx = (source // 4 - y) % 4, (source % 4 - x) % 4
    near, far = jnp.where(k == 0, dx, dy), jnp.where(k == 0, dy, dx)
    triple = (near - (near == 3)) * 4
    slots = cols % 4 + jnp.where(
        far == 0,
        near * 4,
        jnp.where(
            near == 2,
            jnp.where(far == 3, 40, jnp.where(far == 1, 44, 60)),
            triple + jnp.where(far == 1, 16, jnp.where(far == 3, 28, 48)),
        ),
    )
    ids = jnp.arange(256, dtype=jnp.int32)
    owner, ahead = rows // 4 % 2, (rows // 8) ^ z
    away = (ahead == 2) | (ahead == 1 + 2 * owner)
    phase = jnp.where(slots < 16, 0, jnp.where(slots < 40, 1, jnp.where(away, 2, 3)))
    group = phase * 2 + (counts <= 128).astype(jnp.int32)
    key = group * 256 + ids
    rank = jnp.sum((key[None, :] < key[:, None]).astype(jnp.int32), axis=1)
    fields = jnp.stack([ids, rows, slots, counts])
    placed = jnp.sum(jnp.where(rank[None, :, None] == ids[None, None, :], fields[:, :, None], 0), axis=1)
    starts = jnp.sum((group[None, :] < ids[:, None]).astype(jnp.int32), axis=1)
    last = jnp.where(ids < 9, starts, jnp.where(ids == 9, z, k))
    return jnp.concatenate([placed, last[None]], axis=0)


def spmm_kernel(phase, meta, nrow, ncol, value, pieces, *rest):
    rest = list(rest)
    if phase > 0:
        rest.pop(0)
    total = rest.pop(0)
    if phase >= 2:
        keep, give = rest.pop(0), rest.pop(0)
    value32, iota = rest
    value32[...] = value[...].astype(F32)
    iota[...] = lax.broadcasted_iota(jnp.int32, (256, 256), 0).astype(F32).astype(BF)
    if phase == 0:
        total[...] = jnp.zeros_like(total)
    low, middle, high = meta[4, 2 * phase], meta[4, 2 * phase + 1], meta[4, 2 * phase + 2]

    def run(width, begin, steps):
        lane = lax.broadcasted_iota(jnp.int32, (1, width), 1)
        zero = jnp.zeros((256, width), BF)
        one = jnp.ones((256, width), BF)

        def line(ref, tile):
            return ref[pl.ds(tile, 1), :][:, :width]

        def spread(picture, hot):
            index = jnp.broadcast_to(picture.astype(F32).astype(BF), (256, width))
            return jnp.where(iota[:, :width] == index, hot, zero)

        def step(i, carry):
            at = [begin + i * UNROLL + u for u in range(UNROLL)]
            safe = [jnp.minimum(p, high - 1) for p in at]
            tiles = [meta[0, p] for p in safe]
            picked = []
            for u in range(UNROLL):
                piece = pieces[meta[2, safe[u]] - FIRST[phase]]
                columns = spread(line(ncol, tiles[u]), one)
                picked.append(jnp.dot(piece, columns, preferred_element_type=F32).astype(BF))
            for u in range(UNROLL):
                live = jnp.where(at[u] < high, meta[3, safe[u]], 0)
                weight = jnp.where(lane < live, line(value32, tiles[u]), 0.0).astype(BF)
                rows = spread(line(nrow, tiles[u]), jnp.broadcast_to(weight, (256, width)))
                r = meta[1, safe[u]]
                total[r] = total[r] + lax.dot_general(
                    rows, picked[u], (((1,), (1,)), ((), ())), preferred_element_type=F32
                )
            return carry

        lax.fori_loop(0, steps, step, 0)

    wide = (middle - low + UNROLL - 1) // UNROLL
    run(256, low, wide)
    begin = jnp.minimum(low + wide * UNROLL, high)
    run(128, begin, (high - begin + UNROLL - 1) // UNROLL)
    if phase >= 2:
        z, k = meta[4, 9], meta[4, 10]
        near, other = 1 + 2 * k, 3 - 2 * k
        ahead = ((near, other), (2, 2)) if phase == 2 else ((0, 0), (other, near))
        for i, (e_keep, e_give) in enumerate(ahead):
            keep[i] = total[pl.ds(((z ^ e_keep) * 2 + k) * 4, 4)]
            give[i] = total[pl.ds(((z ^ e_give) * 2 + 1 - k) * 4, 4)].astype(BF)


def spmm(phase, meta, nrow, ncol, value, pieces, total=None):
    vmem = pl.BlockSpec(memory_space=pltpu.VMEM)
    args = [nrow, ncol, value, pieces] + ([] if total is None else [total])
    out = [jax.ShapeDtypeStruct((32, 256, 128), F32)]
    if phase >= 2:
        out += [jax.ShapeDtypeStruct((2, 4, 256, 128), F32), jax.ShapeDtypeStruct((2, 4, 256, 128), BF)]
    share = (16, 24, 12, 12)[phase] / 64
    return pl.pallas_call(
        functools.partial(spmm_kernel, phase),
        out_shape=out,
        in_specs=[pl.BlockSpec(memory_space=pltpu.SMEM)] + [vmem] * len(args),
        out_specs=[vmem] * len(out),
        scratch_shapes=[pltpu.VMEM((256, 256), F32), pltpu.VMEM((256, 256), BF)],
        input_output_aliases={} if total is None else {5: 0},
        compiler_params=pltpu.CompilerParams(vmem_limit_bytes=40 << 20),
        cost_estimate=pl.CostEstimate(flops=int(share * 2.0e10), bytes_accessed=1 << 20, transcendentals=0),
        name=f"spmm_phase{phase}",
    )(meta, *args)


def finish_kernel(col, hidden, weight, cotangent, node_out, keep, give):
    w = weight[...].astype(F32)
    grad = jnp.zeros((128, 128), F32)
    for i in range(4):
        h = hidden[i]
        pre = jnp.dot(h, w, precision=lax.Precision.HIGHEST, preferred_element_type=F32)
        sig = 1.0 / (1.0 + jnp.exp(-pre))
        span = pl.ds(i * 256, 256)
        node_out[span, :] = (pre * sig).astype(BF)
        slope = sig * (1.0 + pre * (1.0 - sig))
        pre_grad = (cotangent[span, :].astype(F32) * slope).astype(BF).astype(F32)
        grad = grad + lax.dot_general(
            h, pre_grad, (((0,), (0,)), ((), ())), precision=lax.Precision.HIGHEST, preferred_element_type=F32
        )
    low = lax.rem(col[0], 2) == 0
    keep[...] = jnp.where(low, grad[:64], grad[64:])
    give[...] = jnp.where(low, grad[64:], grad[:64])


def finish(col, hidden, weight, cotangent):
    vmem = pl.BlockSpec(memory_space=pltpu.VMEM)
    return pl.pallas_call(
        finish_kernel,
        out_shape=[jax.ShapeDtypeStruct((1024, 128), BF)] + [jax.ShapeDtypeStruct((64, 128), F32)] * 2,
        in_specs=[pl.BlockSpec(memory_space=pltpu.SMEM)] + [vmem] * 3,
        out_specs=[vmem] * 3,
        compiler_params=pltpu.CompilerParams(vmem_limit_bytes=16 << 20),
        name="finish",
    )(col.reshape(1), hidden, weight, cotangent)


def transpose_kernel(features, out):
    for i in range(4):
        out[i] = features[pl.ds(i * 256, 256), :].T


def transposed(features):
    vmem = pl.BlockSpec(memory_space=pltpu.VMEM)
    return pl.pallas_call(
        transpose_kernel,
        out_shape=jax.ShapeDtypeStruct((4, 128, 256), BF),
        in_specs=[vmem],
        out_specs=vmem,
        compiler_params=pltpu.CompilerParams(vmem_limit_bytes=8 << 20),
        name="transposed",
    )(features)


def cat(*parts):
    return jnp.concatenate(parts, axis=0)


def add(a, b):
    return a.astype(F32) + b.astype(F32)


def sum_ring(v, axis):
    return (v + shift(v, axis, 2)) + (shift(v, axis, 1) + shift(v, axis, -1))


def body(features, weight, cotangent, tile_row, tile_col, nnz_row, nnz_col, edge_value, tile_count):
    row, col = lax.axis_index("row"), lax.axis_index("col")
    meta = plan_tiles(
        tile_row.reshape(256), tile_col.reshape(256), tile_count.reshape(256),
        row // 4, row % 4, col // 2, col % 2,
    )
    slots = (meta, nnz_row.reshape(256, 256), nnz_col.reshape(256, 256), edge_value.reshape(256, 256))

    own = transposed(features)
    right, left = first_axis(own, 1), first_axis(own, -1)
    opposite = first_axis(own, 2)
    near = cat(own, left, right)
    down, up = second_axis(near, 1), second_axis(near, -1)
    corner = second_axis(opposite, 2)
    (total,) = spmm(0, *slots, cat(own, left, opposite, right))
    plus = second_axis(cat(opposite, down[:PLUS]), 1)
    minus = second_axis(cat(opposite, up[PLUS:]), -1)
    (total,) = spmm(1, *slots, cat(up, down), total)
    rest = cat(plus[:4], minus[:4], plus[4:], minus[4:], corner)
    total, keep, give = spmm(2, *slots, rest, total)

    away = add(keep, swap_cores(give)).astype(BF)
    away, total = lax.optimization_barrier((away, total))
    got = permute(away, lambda y, x, z, k: (y, x, z ^ (1 + 2 * k), k))
    total, keep, give = spmm(3, *slots, rest, total)
    give, got = lax.optimization_barrier((give, got))
    home = add(keep, swap_cores(give))
    mine, pair = add(home[0], got[0]), add(home[1], got[1])
    hidden = add(mine, permute(pair.astype(BF), lambda y, x, z, k: (y, x, z ^ (3 - 2 * k), k)))

    node_out, grad, other = finish(col, hidden, weight, cotangent)
    grad = grad + swap_cores(other)
    for axis in ("z", "x", "y"):
        grad = sum_ring(grad, axis)
    other = swap_cores(grad)
    grad = jnp.where(col % 2 == 0, cat(grad, other), cat(other, grad))
    return node_out, grad


def solution(mesh):
    placed = (
        P(("col", "row"), None),
        P(),
        P(("row", "col"), None),
        P("row", "col", None),
        P("row", "col", None),
        P("row", "col", None, None),
        P("row", "col", None, None),
        P("row", "col", None, None),
        P("row", "col", None),
    )
    return jax.shard_map(
        body, mesh=mesh, in_specs=placed, out_specs=(P(("row", "col"), None), P()), check_vma=False
    )
```

time: 118 us -> 101 us (0.86); the launches traced: 116 us -> 100 us
  starting transfers between devices: 43.3 us -> 33.2 us
  Pallas kernels: 28.9 us -> 21.4 us
  waiting for transfers between devices: 36.3 us -> 38.8 us
    ppermute x31 -> x23, starting transfers between devices: 43.3 us -> 33.2 us  [permute(): return lax.ppermute(a, ('row', 'col'), pairs)]
    pallas_call x4, Pallas kernels: 26.8 us -> 19.3 us  [spmm(): pl.pallas_call(functools.partial(spmm_kernel, phase), out_shape=out, in_s...]
    ppermute x31 -> x23, waiting for transfers between devices: 36.3 us -> 38.8 us  [permute(): return lax.ppermute(a, ('row', 'col'), pairs)]
  transfers between devices with their start and end apart: 31 -> 23, of which waited for: 15 -> 17; matrix products, arithmetic and copies ran while one was open for 4% -> 4% of each run, Pallas kernels for 16% -> 16%
where the time goes in v3:
time: 101 us; the launch traced here: 100 us
  waiting for transfers between devices  38.8 us (38%)
  starting transfers between devices  33.2 us (33%)
  Pallas kernels  21.4 us (21%)
  other arithmetic  4.92 us (5%)
  local copies, waits for them, and re-layouts  1.14 us (1%)
    ppermute x23, waiting for transfers between devices, permute(): return lax.ppermute(a, ('row', 'col'), pairs)  38.8 us
    ppermute x23, starting transfers between devices, permute(): return lax.ppermute(a, ('row', 'col'), pairs)  33.2 us
    pallas_call x4, Pallas kernels, spmm(): pl.pallas_call(functools.partial(spmm_kernel, phase), out_shape=out, in_s...  19.3 us
  transfers between devices with their start and end apart: 23, of which 17 were waited for; matrix products, arithmetic and copies ran while one was open for 4% of the time, Pallas kernels for 16%

profile of v3, /device:TPU:0, one launch (start us, length us, event | category | flops | bytes accessed | tf_op | source)
XLA Modules:
  0.0 100.4 jit_solution(11376628592896026355)
XLA Ops:
  3.3 1.7 %collective-permute-start.1 = (bf16[4,128,256]{2,1,0:T(8,128)(2,1)S(1)}, bf16[4,128,256]{2,1,0:T(8,128)(2,1)S(1)}, u32[]{:S(2)}, u32[]{:S(2)}) collective-permute-start(bf16[4,128,256]{2,1,0:T(8,128)(2,1)S(1)} %transposed.1), channel_id=1, source_target_pairs={{0,24},{1,97},{2,26},{3,99},{4,28},{5,101},{6,30},{7,103},{8,0},{9... | collective-permute-start | bytes 786440 | tf_op jit(solution)/shard_map/ppermute | solution.py:23
  5.0 1.9 %collective-permute-start = (bf16[4,128,256]{2,1,0:T(8,128)(2,1)S(1)}, bf16[4,128,256]{2,1,0:T(8,128)(2,1)S(1)}, u32[]{:S(2)}, u32[]{:S(2)}) collective-permute-start(bf16[4,128,256]{2,1,0:T(8,128)(2,1)S(1)} %transposed.1), channel_id=1, source_target_pairs={{0,16},{1,65},{2,18},{3,67},{4,20},{5,69},{6,22},{7,71},{8,24},{9,... | collective-permute-start | bytes 786440 | tf_op jit(solution)/shard_map/ppermute | solution.py:23
  10.2 4.7 %collective-permute-start.5 = (bf16[12,128,256]{2,1,0:T(8,128)(2,1)S(1)}, bf16[12,128,256]{2,1,0:T(8,128)(2,1)S(1)}, u32[]{:S(2)}, u32[]{:S(2)}) collective-permute-start(bf16[12,128,256]{2,1,0:T(8,128)(2,1)S(1)} %pad_maximum_fusion.2), channel_id=1, source_target_pairs={{0,96},{1,25},{2,98},{3,27},{4,100},{5,29},{6,102},{7,31},{8,104},... | collective-permute-start | bytes 2359304 | tf_op jit(solution)/shard_map/ppermute | solution.py:23
  17.0 5.7 %spmm_phase0.1.rest_0_ = f32[32,256,128]{2,1,0:T(8,128)S(1)} custom-call(s32[5,256]{1,0:T(8,128)S(1)} %pad_add_fusion.meta, s32[256,256]{1,0:T(8,128)S(1)} %bitcast.29, s32[256,256]{1,0:T(8,128)S(1)} %bitcast.33, bf16[256,256]{1,0:T(8,128)(2,1)S(1)} %bitcast.37, bf16[16,128,256]{2,1,0:T(8,128)(2,1)S(1)} %pad_maximum_fusion.1.pieces), custom_call_target="tpu_custom_call" | custom-call | flops 5000000000 | bytes 1048576 | tf_op jit(solution)/shard_map/spmm_phase0/pallas_call | solution.py:138
  22.7 4.6 %collective-permute-done.5 = bf16[12,128,256]{2,1,0:T(8,128)(2,1)S(1)} collective-permute-done((bf16[12,128,256]{2,1,0:T(8,128)(2,1)S(1)}, bf16[12,128,256]{2,1,0:T(8,128)(2,1)S(1)}, u32[]{:S(2)}, u32[]{:S(2)}) %collective-permute-start.5) | collective-permute-done | bytes 786464 | tf_op jit(solution)/shard_map/ppermute | solution.py:23
  27.3 3.7 %collective-permute-done.3 = bf16[12,128,256]{2,1,0:T(8,128)(2,1)S(1)} collective-permute-done((bf16[12,128,256]{2,1,0:T(8,128)(2,1)S(1)}, bf16[12,128,256]{2,1,0:T(8,128)(2,1)S(1)}, u32[]{:S(2)}, u32[]{:S(2)}) %collective-permute-start.3) | collective-permute-done | bytes 786464 | tf_op jit(solution)/shard_map/ppermute | solution.py:23
  31.3 2.0 %collective-permute-start.4 = (bf16[10,128,256]{2,1,0:T(8,128)(2,1)S(1)}, bf16[10,128,256]{2,1,0:T(8,128)(2,1)S(1)}, u32[]{:S(2)}, u32[]{:S(2)}) collective-permute-start(bf16[10,128,256]{2,1,0:T(8,128)(2,1)S(1)} %get-tuple-element.29), channel_id=1, source_target_pairs={{0,32},{1,9},{2,34},{3,11},{4,36},{5,13},{6,38},{7,15},{8,40},{9,1... | collective-permute-start | bytes 1966088 | tf_op jit(solution)/shard_map/ppermute | solution.py:23
  33.4 5.4 %spmm_phase1.1.rest_0_ = f32[32,256,128]{2,1,0:T(8,128)S(1)} custom-call(s32[5,256]{1,0:T(8,128)S(1)} %pad_add_fusion.meta, s32[256,256]{1,0:T(8,128)S(1)} %bitcast.30, s32[256,256]{1,0:T(8,128)S(1)} %bitcast.34, bf16[256,256]{1,0:T(8,128)(2,1)S(1)} %bitcast.38, bf16[24,128,256]{2,1,0:T(8,128)(2,1)S(1)} %pad_maximum_fusion.pieces, ...), custom_call_target="tpu_custom_call", output_to_operand_aliasing={{}: (5, {})} | custom-call | flops 7500000256 | bytes 1048576 | tf_op jit(solution)/shard_map/spmm_phase1/pallas_call | solution.py:138
  38.7 4.3 %collective-permute-done.4 = bf16[10,128,256]{2,1,0:T(8,128)(2,1)S(1)} collective-permute-done((bf16[10,128,256]{2,1,0:T(8,128)(2,1)S(1)}, bf16[10,128,256]{2,1,0:T(8,128)(2,1)S(1)}, u32[]{:S(2)}, u32[]{:S(2)}) %collective-permute-start.4) | collective-permute-done | bytes 655392 | tf_op jit(solution)/shard_map/ppermute | solution.py:23
  43.3 3.7 %spmm_phase2.1 = (f32[32,256,128]{2,1,0:T(8,128)S(1)}, f32[2,4,256,128]{3,2,1,0:T(8,128)S(1)}, bf16[2,4,256,128]{3,2,1,0:T(8,128)(2,1)S(1)}) custom-call(s32[5,256]{1,0:T(8,128)S(1)} %pad_add_fusion.meta, s32[256,256]{1,0:T(8,128)S(1)} %bitcast.31, s32[256,256]{1,0:T(8,128)S(1)} %bitcast.35, ...), custom_call_target="tpu_custom_call", output_to_operand_aliasing={{0}: (5, {})} | custom-call | flops 3750000128 | bytes 1048576 | tf_op jit(solution)/shard_map/spmm_phase2/pallas_call | solution.py:138
  47.0 1.9 %collective-permute-done.8 = bf16[2,4,256,128]{3,2,1,0:T(8,128)(2,1)S(1)} collective-permute-done((bf16[2,4,256,128]{3,2,1,0:T(8,128)(2,1)S(1)}, bf16[2,4,256,128]{3,2,1,0:T(8,128)(2,1)S(1)}, u32[]{:S(2)}, u32[]{:S(2)}) %collective-permute-start.8) | collective-permute-done | bytes 524320 | tf_op jit(solution)/shard_map/ppermute | solution.py:23
  49.1 2.0 %collective-permute-start.9 = (bf16[2,4,256,128]{3,2,1,0:T(8,128)(2,1)S(1)}, bf16[2,4,256,128]{3,2,1,0:T(8,128)(2,1)S(1)}, u32[]{:S(2)}, u32[]{:S(2)}) collective-permute-start(bf16[2,4,256,128]{3,2,1,0:T(8,128)(2,1)S(1)} %add_convert_fusion), channel_id=1, source_target_pairs={{0,2},{1,7},{2,0},{3,5},{4,6},{5,3},{6,4},{7,1},{8,10},{9,15},{10,... | collective-permute-start | bytes 1572872 | tf_op jit(solution)/shard_map/ppermute | solution.py:23
  51.1 4.6 %spmm_phase3.1 = (f32[32,256,128]{2,1,0:T(8,128)S(1)}, f32[2,4,256,128]{3,2,1,0:T(8,128)S(1)}, bf16[2,4,256,128]{3,2,1,0:T(8,128)(2,1)S(1)}) custom-call(s32[5,256]{1,0:T(8,128)S(1)} %pad_add_fusion.meta, s32[256,256]{1,0:T(8,128)S(1)} %bitcast.32, s32[256,256]{1,0:T(8,128)S(1)} %bitcast.36, ...), custom_call_target="tpu_custom_call", output_to_operand_aliasing={{0}: (5, {})} | custom-call | flops 3750000128 | bytes 1048576 | tf_op jit(solution)/shard_map/spmm_phase3/pallas_call | solution.py:138
  55.7 2.6 %collective-permute-done.9 = bf16[2,4,256,128]{3,2,1,0:T(8,128)(2,1)S(1)} collective-permute-done((bf16[2,4,256,128]{3,2,1,0:T(8,128)(2,1)S(1)}, bf16[2,4,256,128]{3,2,1,0:T(8,128)(2,1)S(1)}, u32[]{:S(2)}, u32[]{:S(2)}) %collective-permute-start.9) | collective-permute-done | bytes 524320 | tf_op jit(solution)/shard_map/ppermute | solution.py:23
  61.4 3.2 %collective-permute-start.11 = (bf16[4,256,128]{2,1,0:T(8,128)(2,1)S(1)}, bf16[4,256,128]{2,1,0:T(8,128)(2,1)S(1)}, u32[]{:S(2)}, u32[]{:S(2)}) collective-permute-start(bf16[4,256,128]{2,1,0:T(8,128)(2,1)S(1)} %fusion.3), channel_id=1, source_target_pairs={{0,6},{1,3},{2,4},{3,1},{4,2},{5,7},{6,0},{7,5},{8,14},{9,11},{10,... | collective-permute-start | bytes 786440 | tf_op jit(solution)/shard_map/ppermute | solution.py:23
  64.6 4.5 %collective-permute-done.11 = bf16[4,256,128]{2,1,0:T(8,128)(2,1)S(1)} collective-permute-done((bf16[4,256,128]{2,1,0:T(8,128)(2,1)S(1)}, bf16[4,256,128]{2,1,0:T(8,128)(2,1)S(1)}, u32[]{:S(2)}, u32[]{:S(2)}) %collective-permute-start.11) | collective-permute-done | bytes 262176 | tf_op jit(solution)/shard_map/ppermute | solution.py:23
  69.2 2.0 %finish.1 = (bf16[1024,128]{1,0:T(8,128)(2,1)}, f32[64,128]{1,0:T(8,128)S(1)}, f32[64,128]{1,0:T(8,128)S(1)}) custom-call(s32[1]{0:T(128)} %bitcast.col, f32[4,256,128]{2,1,0:T(8,128)S(1)} %fusion.2.hidden, bf16[128,128]{1,0:T(8,128)(2,1)S(1)} %copy-done.2, bf16[1024,128]{1,0:T(8,128)(2,1)S(1)} %copy-done.1), custom_call_target="tpu_custom_call" | custom-call | tf_op jit(solution)/shard_map/finish/pallas_call | solution.py:172
  72.3 3.1 %collective-permute-start.15 = (f32[64,128]{1,0:T(8,128)S(1)}, f32[64,128]{1,0:T(8,128)S(1)}, u32[]{:S(2)}, u32[]{:S(2)}) collective-permute-start(f32[64,128]{1,0:T(8,128)S(1)} %add.335), channel_id=1, source_target_pairs={{0,6},{1,7},{2,0},{3,1},{4,2},{5,3},{6,4},{7,5},{8,14},{9,15},{10,... | collective-permute-start | bytes 98312 | tf_op jit(solution)/shard_map/ppermute | solution.py:23
  77.1 3.9 %collective-permute-done.14 = f32[64,128]{1,0:T(8,128)S(1)} collective-permute-done((f32[64,128]{1,0:T(8,128)S(1)}, f32[64,128]{1,0:T(8,128)S(1)}, u32[]{:S(2)}, u32[]{:S(2)}) %collective-permute-start.14) | collective-permute-done | bytes 32800 | tf_op jit(solution)/shard_map/ppermute | solution.py:23
  80.9 4.5 %collective-permute-start.18 = (f32[64,128]{1,0:T(8,128)S(1)}, f32[64,128]{1,0:T(8,128)S(1)}, u32[]{:S(2)}, u32[]{:S(2)}) collective-permute-start(f32[64,128]{1,0:T(8,128)S(1)} %add_add_fusion.2), channel_id=1, source_target_pairs={{0,24},{1,25},{2,26},{3,27},{4,28},{5,29},{6,30},{7,31},{8,0},{9,1... | collective-permute-start | bytes 98312 | tf_op jit(solution)/shard_map/ppermute | solution.py:23
  87.0 3.5 %collective-permute-done.17 = f32[64,128]{1,0:T(8,128)S(1)} collective-permute-done((f32[64,128]{1,0:T(8,128)S(1)}, f32[64,128]{1,0:T(8,128)S(1)}, u32[]{:S(2)}, u32[]{:S(2)}) %collective-permute-start.17) | collective-permute-done | bytes 32800 | tf_op jit(solution)/shard_map/ppermute | solution.py:23
  91.0 2.0 %collective-permute-start.20 = (f32[64,128]{1,0:T(8,128)S(1)}, f32[64,128]{1,0:T(8,128)S(1)}, u32[]{:S(2)}, u32[]{:S(2)}) collective-permute-start(f32[64,128]{1,0:T(8,128)S(1)} %add_add_fusion.1), channel_id=1, source_target_pairs={{0,32},{1,33},{2,34},{3,35},{4,36},{5,37},{6,38},{7,39},{8,40},{9,... | collective-permute-start | bytes 98312 | tf_op jit(solution)/shard_map/ppermute | solution.py:23
  93.1 1.9 %collective-permute-done.21 = f32[64,128]{1,0:T(8,128)S(1)} collective-permute-done((f32[64,128]{1,0:T(8,128)S(1)}, f32[64,128]{1,0:T(8,128)S(1)}, u32[]{:S(2)}, u32[]{:S(2)}) %collective-permute-start.21) | collective-permute-done | bytes 32800 | tf_op jit(solution)/shard_map/ppermute | solution.py:23
  96.2 2.2 %collective-permute-done.19 = f32[64,128]{1,0:T(8,128)S(1)} collective-permute-done((f32[64,128]{1,0:T(8,128)S(1)}, f32[64,128]{1,0:T(8,128)S(1)}, u32[]{:S(2)}, u32[]{:S(2)}) %collective-permute-start.19) | collective-permute-done | bytes 32800 | tf_op jit(solution)/shard_map/ppermute | solution.py:23
  (70 shorter events, 19.9 us)
Async XLA Ops:
  1.7 8.4 %collective-permute-start.2 = (bf16[4,128,256]{2,1,0:T(8,128)(2,1)S(1)}, bf16[4,128,256]{2,1,0:T(8,128)(2,1)S(1)}, u32[]{:S(2)}, u32[]{:S(2)}) collective-permute-start(bf16[4,128,256]{2,1,0:T(8,128)(2,1)S(1)} %transposed.1), channel_id=1, source_target_pairs={{0,8},{1,33},{2,10},{3,35},{4,12},{5,37},{6,14},{7,39},{8,16},{9,4... | collective-permute-start | bytes 786440 | tf_op jit(solution)/shard_map/ppermute | solution.py:23
  3.3 6.8 %collective-permute-start.1 = (bf16[4,128,256]{2,1,0:T(8,128)(2,1)S(1)}, bf16[4,128,256]{2,1,0:T(8,128)(2,1)S(1)}, u32[]{:S(2)}, u32[]{:S(2)}) collective-permute-start(bf16[4,128,256]{2,1,0:T(8,128)(2,1)S(1)} %transposed.1), channel_id=1, source_target_pairs={{0,24},{1,97},{2,26},{3,99},{4,28},{5,101},{6,30},{7,103},{8,0},{9... | collective-permute-start | bytes 786440 | tf_op jit(solution)/shard_map/ppermute | solution.py:23
  5.0 10.2 %collective-permute-start = (bf16[4,128,256]{2,1,0:T(8,128)(2,1)S(1)}, bf16[4,128,256]{2,1,0:T(8,128)(2,1)S(1)}, u32[]{:S(2)}, u32[]{:S(2)}) collective-permute-start(bf16[4,128,256]{2,1,0:T(8,128)(2,1)S(1)} %transposed.1), channel_id=1, source_target_pairs={{0,16},{1,65},{2,18},{3,67},{4,20},{5,69},{6,22},{7,71},{8,24},{9,... | collective-permute-start | bytes 786440 | tf_op jit(solution)/shard_map/ppermute | solution.py:23
  10.2 17.1 %collective-permute-start.5 = (bf16[12,128,256]{2,1,0:T(8,128)(2,1)S(1)}, bf16[12,128,256]{2,1,0:T(8,128)(2,1)S(1)}, u32[]{:S(2)}, u32[]{:S(2)}) collective-permute-start(bf16[12,128,256]{2,1,0:T(8,128)(2,1)S(1)} %pad_maximum_fusion.2), channel_id=1, source_target_pairs={{0,96},{1,25},{2,98},{3,27},{4,100},{5,29},{6,102},{7,31},{8,104},... | collective-permute-start | bytes 2359304 | tf_op jit(solution)/shard_map/ppermute | solution.py:23
  15.0 16.0 %collective-permute-start.3 = (bf16[12,128,256]{2,1,0:T(8,128)(2,1)S(1)}, bf16[12,128,256]{2,1,0:T(8,128)(2,1)S(1)}, u32[]{:S(2)}, u32[]{:S(2)}) collective-permute-start(bf16[12,128,256]{2,1,0:T(8,128)(2,1)S(1)} %pad_maximum_fusion.2), channel_id=1, source_target_pairs={{0,32},{1,9},{2,34},{3,11},{4,36},{5,13},{6,38},{7,15},{8,40},{9,1... | collective-permute-start | bytes 2359304 | tf_op jit(solution)/shard_map/ppermute | solution.py:23
  15.2 28.0 %collective-permute-start.7 = (bf16[4,128,256]{2,1,0:T(8,128)(2,1)S(1)}, bf16[4,128,256]{2,1,0:T(8,128)(2,1)S(1)}, u32[]{:S(2)}, u32[]{:S(2)}) collective-permute-start(bf16[4,128,256]{2,1,0:T(8,128)(2,1)S(1)} %collective-permute-done), channel_id=1, source_target_pairs={{0,64},{1,17},{2,66},{3,19},{4,68},{5,21},{6,70},{7,23},{8,72},{9,... | collective-permute-start | bytes 786440 | tf_op jit(solution)/shard_map/ppermute | solution.py:23
  31.1 12.0 %collective-permute-start.6 = (bf16[10,128,256]{2,1,0:T(8,128)(2,1)S(1)}, bf16[10,128,256]{2,1,0:T(8,128)(2,1)S(1)}, u32[]{:S(2)}, u32[]{:S(2)}) collective-permute-start(bf16[10,128,256]{2,1,0:T(8,128)(2,1)S(1)} %get-tuple-element.28), channel_id=1, source_target_pairs={{0,96},{1,25},{2,98},{3,27},{4,100},{5,29},{6,102},{7,31},{8,104},... | collective-permute-start | bytes 1966088 | tf_op jit(solution)/shard_map/ppermute | solution.py:23
  31.3 11.8 %collective-permute-start.4 = (bf16[10,128,256]{2,1,0:T(8,128)(2,1)S(1)}, bf16[10,128,256]{2,1,0:T(8,128)(2,1)S(1)}, u32[]{:S(2)}, u32[]{:S(2)}) collective-permute-start(bf16[10,128,256]{2,1,0:T(8,128)(2,1)S(1)} %get-tuple-element.29), channel_id=1, source_target_pairs={{0,32},{1,9},{2,34},{3,11},{4,36},{5,13},{6,38},{7,15},{8,40},{9,1... | collective-permute-start | bytes 1966088 | tf_op jit(solution)/shard_map/ppermute | solution.py:23
  47.0 2.0 %collective-permute-start.8 = (bf16[2,4,256,128]{3,2,1,0:T(8,128)(2,1)S(1)}, bf16[2,4,256,128]{3,2,1,0:T(8,128)(2,1)S(1)}, u32[]{:S(2)}, u32[]{:S(2)}) collective-permute-start(bf16[2,4,256,128]{3,2,1,0:T(8,128)(2,1)S(1)} %get-tuple-element.15), channel_id=1, source_target_pairs={{0,1},{1,0},{2,3},{3,2},{4,5},{5,4},{6,7},{7,6},{8,9},{9,8},{10,11... | collective-permute-start | bytes 1572872 | tf_op jit(solution)/shard_map/ppermute | solution.py:23
  49.1 9.3 %collective-permute-start.9 = (bf16[2,4,256,128]{3,2,1,0:T(8,128)(2,1)S(1)}, bf16[2,4,256,128]{3,2,1,0:T(8,128)(2,1)S(1)}, u32[]{:S(2)}, u32[]{:S(2)}) collective-permute-start(bf16[2,4,256,128]{3,2,1,0:T(8,128)(2,1)S(1)} %add_convert_fusion), channel_id=1, source_target_pairs={{0,2},{1,7},{2,0},{3,5},{4,6},{5,3},{6,4},{7,1},{8,10},{9,15},{10,... | collective-permute-start | bytes 1572872 | tf_op jit(solution)/shard_map/ppermute | solution.py:23
  58.3 2.8 %collective-permute-start.10 = (bf16[2,4,256,128]{3,2,1,0:T(8,128)(2,1)S(1)}, bf16[2,4,256,128]{3,2,1,0:T(8,128)(2,1)S(1)}, u32[]{:S(2)}, u32[]{:S(2)}) collective-permute-start(bf16[2,4,256,128]{3,2,1,0:T(8,128)(2,1)S(1)} %get-tuple-element.21), channel_id=1, source_target_pairs={{0,1},{1,0},{2,3},{3,2},{4,5},{5,4},{6,7},{7,6},{8,9},{9,8},{10,11... | collective-permute-start | bytes 1572872 | tf_op jit(solution)/shard_map/ppermute | solution.py:23
  61.3 7.9 %copy-start.1 = (bf16[1024,128]{1,0:T(8,128)(2,1)S(1)}, bf16[1024,128]{1,0:T(8,128)(2,1)}, u32[]{:S(2)}) copy-start(bf16[1024,128]{1,0:T(8,128)(2,1)} %cotangent.1) | copy-start | bytes 786436
  61.4 7.7 %collective-permute-start.11 = (bf16[4,256,128]{2,1,0:T(8,128)(2,1)S(1)}, bf16[4,256,128]{2,1,0:T(8,128)(2,1)S(1)}, u32[]{:S(2)}, u32[]{:S(2)}) collective-permute-start(bf16[4,256,128]{2,1,0:T(8,128)(2,1)S(1)} %fusion.3), channel_id=1, source_target_pairs={{0,6},{1,3},{2,4},{3,1},{4,2},{5,7},{6,0},{7,5},{8,14},{9,11},{10,... | collective-permute-start | bytes 786440 | tf_op jit(solution)/shard_map/ppermute | solution.py:23
  71.1 1.2 %collective-permute-start.12 = (f32[64,128]{1,0:T(8,128)S(1)}, f32[64,128]{1,0:T(8,128)S(1)}, u32[]{:S(2)}, u32[]{:S(2)}) collective-permute-start(f32[64,128]{1,0:T(8,128)S(1)} %get-tuple-element.25), channel_id=1, source_target_pairs={{0,1},{1,0},{2,3},{3,2},{4,5},{5,4},{6,7},{7,6},{8,9},{9,8},{10,11... | collective-permute-start | bytes 98312 | tf_op jit(solution)/shard_map/ppermute | solution.py:23
  72.3 4.7 %collective-permute-start.15 = (f32[64,128]{1,0:T(8,128)S(1)}, f32[64,128]{1,0:T(8,128)S(1)}, u32[]{:S(2)}, u32[]{:S(2)}) collective-permute-start(f32[64,128]{1,0:T(8,128)S(1)} %add.335), channel_id=1, source_target_pairs={{0,6},{1,7},{2,0},{3,1},{4,2},{5,3},{6,4},{7,5},{8,14},{9,15},{10,... | collective-permute-start | bytes 98312 | tf_op jit(solution)/shard_map/ppermute | solution.py:23
  75.5 5.5 %collective-permute-start.14 = (f32[64,128]{1,0:T(8,128)S(1)}, f32[64,128]{1,0:T(8,128)S(1)}, u32[]{:S(2)}, u32[]{:S(2)}) collective-permute-start(f32[64,128]{1,0:T(8,128)S(1)} %add.335), channel_id=1, source_target_pairs={{0,2},{1,3},{2,4},{3,5},{4,6},{5,7},{6,0},{7,1},{8,10},{9,11},{10,... | collective-permute-start | bytes 98312 | tf_op jit(solution)/shard_map/ppermute | solution.py:23
  75.5 5.5 %collective-permute-start.13 = (f32[64,128]{1,0:T(8,128)S(1)}, f32[64,128]{1,0:T(8,128)S(1)}, u32[]{:S(2)}, u32[]{:S(2)}) collective-permute-start(f32[64,128]{1,0:T(8,128)S(1)} %add.335), channel_id=1, source_target_pairs={{0,4},{1,5},{2,6},{3,7},{4,0},{5,1},{6,2},{7,3},{8,12},{9,13},{10,... | collective-permute-start | bytes 98312 | tf_op jit(solution)/shard_map/ppermute | solution.py:23
  80.9 6.1 %collective-permute-start.18 = (f32[64,128]{1,0:T(8,128)S(1)}, f32[64,128]{1,0:T(8,128)S(1)}, u32[]{:S(2)}, u32[]{:S(2)}) collective-permute-start(f32[64,128]{1,0:T(8,128)S(1)} %add_add_fusion.2), channel_id=1, source_target_pairs={{0,24},{1,25},{2,26},{3,27},{4,28},{5,29},{6,30},{7,31},{8,0},{9,1... | collective-permute-start | bytes 98312 | tf_op jit(solution)/shard_map/ppermute | solution.py:23
  85.5 5.1 %collective-permute-start.17 = (f32[64,128]{1,0:T(8,128)S(1)}, f32[64,128]{1,0:T(8,128)S(1)}, u32[]{:S(2)}, u32[]{:S(2)}) collective-permute-start(f32[64,128]{1,0:T(8,128)S(1)} %add_add_fusion.2), channel_id=1, source_target_pairs={{0,8},{1,9},{2,10},{3,11},{4,12},{5,13},{6,14},{7,15},{8,16},{9,17... | collective-permute-start | bytes 98312 | tf_op jit(solution)/shard_map/ppermute | solution.py:23
  85.5 5.5 %collective-permute-start.16 = (f32[64,128]{1,0:T(8,128)S(1)}, f32[64,128]{1,0:T(8,128)S(1)}, u32[]{:S(2)}, u32[]{:S(2)}) collective-permute-start(f32[64,128]{1,0:T(8,128)S(1)} %add_add_fusion.2), channel_id=1, source_target_pairs={{0,16},{1,17},{2,18},{3,19},{4,20},{5,21},{6,22},{7,23},{8,24},{9,... | collective-permute-start | bytes 98312 | tf_op jit(solution)/shard_map/ppermute | solution.py:23
  90.9 4.0 %collective-permute-start.21 = (f32[64,128]{1,0:T(8,128)S(1)}, f32[64,128]{1,0:T(8,128)S(1)}, u32[]{:S(2)}, u32[]{:S(2)}) collective-permute-start(f32[64,128]{1,0:T(8,128)S(1)} %add_add_fusion.1), channel_id=1, source_target_pairs={{0,96},{1,97},{2,98},{3,99},{4,100},{5,101},{6,102},{7,103},{8,104... | collective-permute-start | bytes 98312 | tf_op jit(solution)/shard_map/ppermute | solution.py:23
  91.0 5.2 %collective-permute-start.20 = (f32[64,128]{1,0:T(8,128)S(1)}, f32[64,128]{1,0:T(8,128)S(1)}, u32[]{:S(2)}, u32[]{:S(2)}) collective-permute-start(f32[64,128]{1,0:T(8,128)S(1)} %add_add_fusion.1), channel_id=1, source_target_pairs={{0,32},{1,33},{2,34},{3,35},{4,36},{5,37},{6,38},{7,39},{8,40},{9,... | collective-permute-start | bytes 98312 | tf_op jit(solution)/shard_map/ppermute | solution.py:23
  93.0 5.4 %collective-permute-start.19 = (f32[64,128]{1,0:T(8,128)S(1)}, f32[64,128]{1,0:T(8,128)S(1)}, u32[]{:S(2)}, u32[]{:S(2)}) collective-permute-start(f32[64,128]{1,0:T(8,128)S(1)} %add_add_fusion.1), channel_id=1, source_target_pairs={{0,64},{1,65},{2,66},{3,67},{4,68},{5,69},{6,70},{7,71},{8,72},{9,... | collective-permute-start | bytes 98312 | tf_op jit(solution)/shard_map/ppermute | solution.py:23
  98.5 1.3 %collective-permute-start.22 = (f32[64,128]{1,0:T(8,128)S(1)}, f32[64,128]{1,0:T(8,128)S(1)}, u32[]{:S(2)}, u32[]{:S(2)}) collective-permute-start(f32[64,128]{1,0:T(8,128)S(1)} %add_add_fusion), channel_id=1, source_target_pairs={{0,1},{1,0},{2,3},{3,2},{4,5},{5,4},{6,7},{7,6},{8,9},{9,8},{10,11... | collective-permute-start | bytes 98312 | tf_op jit(solution)/shard_map/ppermute | solution.py:23
  (5 other events, 29.5 us)

commit v4 on v3

--- a/solution.py
+++ b/solution.py
@@ -148,7 +148,7 @@
     )(meta, *args)
 
 
-def finish_kernel(col, hidden, weight, cotangent, node_out, keep, give):
+def finish_kernel(hidden, weight, cotangent, node_out, partial):
     w = weight[...].astype(F32)
     grad = jnp.zeros((128, 128), F32)
     for i in range(4):
@@ -162,21 +162,19 @@
         grad = grad + lax.dot_general(
             h, pre_grad, (((0,), (0,)), ((), ())), precision=lax.Precision.HIGHEST, preferred_element_type=F32
         )
-    low = lax.rem(col[0], 2) == 0
-    keep[...] = jnp.where(low, grad[:64], grad[64:])
-    give[...] = jnp.where(low, grad[64:], grad[:64])
-
-
-def finish(col, hidden, weight, cotangent):
+    partial[...] = grad
+
+
+def finish(hidden, weight, cotangent):
     vmem = pl.BlockSpec(memory_space=pltpu.VMEM)
     return pl.pallas_call(
         finish_kernel,
-        out_shape=[jax.ShapeDtypeStruct((1024, 128), BF)] + [jax.ShapeDtypeStruct((64, 128), F32)] * 2,
-        in_specs=[pl.BlockSpec(memory_space=pltpu.SMEM)] + [vmem] * 3,
-        out_specs=[vmem] * 3,
+        out_shape=[jax.ShapeDtypeStruct((1024, 128), BF), jax.ShapeDtypeStruct((128, 128), F32)],
+        in_specs=[vmem] * 3,
+        out_specs=[vmem] * 2,
         compiler_params=pltpu.CompilerParams(vmem_limit_bytes=16 << 20),
         name="finish",
-    )(col.reshape(1), hidden, weight, cotangent)
+    )(hidden, weight, cotangent)
 
 
 def transpose_kernel(features, out):
@@ -205,7 +203,11 @@
 
 
 def sum_ring(v, axis):
-    return (v + shift(v, axis, 2)) + (shift(v, axis, 1) + shift(v, axis, -1))
+    sent = v.astype(BF)
+    beside = permute(sent, lambda y, x, z, k: tuple(
+        c + (1 - 2 * k) * (axis == name) for c, name in ((y, "y"), (x, "x"), (z, "z"))) + (k,))
+    across = shift(sent, axis, 2).astype(F32)
+    return (lax.reduce_precision(v, 8, 7) + across) + add(beside, swap_cores(beside))
 
 
 def body(features, weight, cotangent, tile_row, tile_col, nnz_row, nnz_col, edge_value, tile_count):
@@ -238,12 +240,10 @@
     mine, pair = add(home[0], got[0]), add(home[1], got[1])
     hidden = add(mine, permute(pair.astype(BF), lambda y, x, z, k: (y, x, z ^ (3 - 2 * k), k)))
 
-    node_out, grad, other = finish(col, hidden, weight, cotangent)
-    grad = grad + swap_cores(other)
+    node_out, grad = finish(hidden, weight, cotangent)
+    grad = grad + swap_cores(grad)
     for axis in ("z", "x", "y"):
         grad = sum_ring(grad, axis)
-    other = swap_cores(grad)
-    grad = jnp.where(col % 2 == 0, cat(grad, other), cat(other, grad))
     return node_out, grad
 
 

time: 101 us -> 96.4 us (0.954)
  starting transfers between devices: 33.2 us -> 30 us
  waiting for transfers between devices: 38.8 us -> 36.3 us
    ppermute x23 -> x22, starting transfers between devices: 33.2 us -> 30 us  [permute(): return lax.ppermute(a, ('row', 'col'), pairs)]
    ppermute x23 -> x22, waiting for transfers between devices: 38.8 us -> 36.3 us  [permute(): return lax.ppermute(a, ('row', 'col'), pairs)]
  transfers between devices with their start and end apart: 23 -> 22, of which waited for: 17 -> 14; matrix products, arithmetic and copies ran while one was open for 4% -> 4% of each run, Pallas kernels for 16% -> 16%
where the time goes in v4:
time: 96.4 us; the launch traced here: 95.3 us
  waiting for transfers between devices  36.3 us (38%)
  starting transfers between devices  30 us (31%)
  Pallas kernels  21.9 us (23%)
  other arithmetic  4.95 us (5%)
  local copies, waits for them, and re-layouts  1.14 us (1%)
    ppermute x22, waiting for transfers between devices, permute(): return lax.ppermute(a, ('row', 'col'), pairs)  36.3 us
    ppermute x22, starting transfers between devices, permute(): return lax.ppermute(a, ('row', 'col'), pairs)  30 us
    pallas_call x4, Pallas kernels, spmm(): pl.pallas_call(functools.partial(spmm_kernel, phase), out_shape=out, in_s...  19.8 us
    pallas_call x1, Pallas kernels, finish(): pl.pallas_call(finish_kernel, out_shape=[jax.ShapeDtypeStruct((1024, 128)...  1.95 us
  transfers between devices with their start and end apart: 22, of which 14 were waited for; matrix products, arithmetic and copies ran while one was open for 4% of the time, Pallas kernels for 16%

profile of v4, /device:TPU:0, one launch (start us, length us, event | category | flops | bytes accessed | tf_op | source)
XLA Modules:
  0.0 95.3 jit_solution(13352921098007271660)
XLA Ops:
  1.7 1.6 %collective-permute-start.2 = (bf16[4,128,256]{2,1,0:T(8,128)(2,1)S(1)}, bf16[4,128,256]{2,1,0:T(8,128)(2,1)S(1)}, u32[]{:S(2)}, u32[]{:S(2)}) collective-permute-start(bf16[4,128,256]{2,1,0:T(8,128)(2,1)S(1)} %transposed.1), channel_id=1, source_target_pairs={{0,8},{1,33},{2,10},{3,35},{4,12},{5,37},{6,14},{7,39},{8,16},{9,4... | collective-permute-start | bytes 786440 | tf_op jit(solution)/shard_map/ppermute | solution.py:23
  3.3 1.7 %collective-permute-start.1 = (bf16[4,128,256]{2,1,0:T(8,128)(2,1)S(1)}, bf16[4,128,256]{2,1,0:T(8,128)(2,1)S(1)}, u32[]{:S(2)}, u32[]{:S(2)}) collective-permute-start(bf16[4,128,256]{2,1,0:T(8,128)(2,1)S(1)} %transposed.1), channel_id=1, source_target_pairs={{0,24},{1,97},{2,26},{3,99},{4,28},{5,101},{6,30},{7,103},{8,0},{9... | collective-permute-start | bytes 786440 | tf_op jit(solution)/shard_map/ppermute | solution.py:23
  5.0 1.9 %collective-permute-start = (bf16[4,128,256]{2,1,0:T(8,128)(2,1)S(1)}, bf16[4,128,256]{2,1,0:T(8,128)(2,1)S(1)}, u32[]{:S(2)}, u32[]{:S(2)}) collective-permute-start(bf16[4,128,256]{2,1,0:T(8,128)(2,1)S(1)} %transposed.1), channel_id=1, source_target_pairs={{0,16},{1,65},{2,18},{3,67},{4,20},{5,69},{6,22},{7,71},{8,24},{9,... | collective-permute-start | bytes 786440 | tf_op jit(solution)/shard_map/ppermute | solution.py:23
  10.2 4.7 %collective-permute-start.5 = (bf16[12,128,256]{2,1,0:T(8,128)(2,1)S(1)}, bf16[12,128,256]{2,1,0:T(8,128)(2,1)S(1)}, u32[]{:S(2)}, u32[]{:S(2)}) collective-permute-start(bf16[12,128,256]{2,1,0:T(8,128)(2,1)S(1)} %pad_maximum_fusion.2), channel_id=1, source_target_pairs={{0,96},{1,25},{2,98},{3,27},{4,100},{5,29},{6,102},{7,31},{8,104},... | collective-permute-start | bytes 2359304 | tf_op jit(solution)/shard_map/ppermute | solution.py:23
  15.2 1.6 %collective-permute-start.7 = (bf16[4,128,256]{2,1,0:T(8,128)(2,1)S(1)}, bf16[4,128,256]{2,1,0:T(8,128)(2,1)S(1)}, u32[]{:S(2)}, u32[]{:S(2)}) collective-permute-start(bf16[4,128,256]{2,1,0:T(8,128)(2,1)S(1)} %collective-permute-done), channel_id=1, source_target_pairs={{0,64},{1,17},{2,66},{3,19},{4,68},{5,21},{6,70},{7,23},{8,72},{9,... | collective-permute-start | bytes 786440 | tf_op jit(solution)/shard_map/ppermute | solution.py:23
  17.0 4.6 %spmm_phase0.1.rest_0_ = f32[32,256,128]{2,1,0:T(8,128)S(1)} custom-call(s32[5,256]{1,0:T(8,128)S(1)} %pad_add_fusion.meta, s32[256,256]{1,0:T(8,128)S(1)} %bitcast.28, s32[256,256]{1,0:T(8,128)S(1)} %bitcast.32, bf16[256,256]{1,0:T(8,128)(2,1)S(1)} %bitcast.36, bf16[16,128,256]{2,1,0:T(8,128)(2,1)S(1)} %pad_maximum_fusion.1.pieces), custom_call_target="tpu_custom_call" | custom-call | flops 5000000000 | bytes 1048576 | tf_op jit(solution)/shard_map/spmm_phase0/pallas_call | solution.py:138
  21.6 5.7 %collective-permute-done.5 = bf16[12,128,256]{2,1,0:T(8,128)(2,1)S(1)} collective-permute-done((bf16[12,128,256]{2,1,0:T(8,128)(2,1)S(1)}, bf16[12,128,256]{2,1,0:T(8,128)(2,1)S(1)}, u32[]{:S(2)}, u32[]{:S(2)}) %collective-permute-start.5) | collective-permute-done | bytes 786464 | tf_op jit(solution)/shard_map/ppermute | solution.py:23
  27.3 3.7 %collective-permute-done.3 = bf16[12,128,256]{2,1,0:T(8,128)(2,1)S(1)} collective-permute-done((bf16[12,128,256]{2,1,0:T(8,128)(2,1)S(1)}, bf16[12,128,256]{2,1,0:T(8,128)(2,1)S(1)}, u32[]{:S(2)}, u32[]{:S(2)}) %collective-permute-start.3) | collective-permute-done | bytes 786464 | tf_op jit(solution)/shard_map/ppermute | solution.py:23
  31.3 2.0 %collective-permute-start.4 = (bf16[10,128,256]{2,1,0:T(8,128)(2,1)S(1)}, bf16[10,128,256]{2,1,0:T(8,128)(2,1)S(1)}, u32[]{:S(2)}, u32[]{:S(2)}) collective-permute-start(bf16[10,128,256]{2,1,0:T(8,128)(2,1)S(1)} %get-tuple-element.29), channel_id=1, source_target_pairs={{0,32},{1,9},{2,34},{3,11},{4,36},{5,13},{6,38},{7,15},{8,40},{9,1... | collective-permute-start | bytes 1966088 | tf_op jit(solution)/shard_map/ppermute | solution.py:23
  33.4 6.9 %spmm_phase1.1.rest_0_ = f32[32,256,128]{2,1,0:T(8,128)S(1)} custom-call(s32[5,256]{1,0:T(8,128)S(1)} %pad_add_fusion.meta, s32[256,256]{1,0:T(8,128)S(1)} %bitcast.29, s32[256,256]{1,0:T(8,128)S(1)} %bitcast.33, bf16[256,256]{1,0:T(8,128)(2,1)S(1)} %bitcast.37, bf16[24,128,256]{2,1,0:T(8,128)(2,1)S(1)} %pad_maximum_fusion.pieces, ...), custom_call_target="tpu_custom_call", output_to_operand_aliasing={{}: (5, {})} | custom-call | flops 7500000256 | bytes 1048576 | tf_op jit(solution)/shard_map/spmm_phase1/pallas_call | solution.py:138
  40.3 2.8 %collective-permute-done.4 = bf16[10,128,256]{2,1,0:T(8,128)(2,1)S(1)} collective-permute-done((bf16[10,128,256]{2,1,0:T(8,128)(2,1)S(1)}, bf16[10,128,256]{2,1,0:T(8,128)(2,1)S(1)}, u32[]{:S(2)}, u32[]{:S(2)}) %collective-permute-start.4) | collective-permute-done | bytes 655392 | tf_op jit(solution)/shard_map/ppermute | solution.py:23
  43.3 4.4 %spmm_phase2.1 = (f32[32,256,128]{2,1,0:T(8,128)S(1)}, f32[2,4,256,128]{3,2,1,0:T(8,128)S(1)}, bf16[2,4,256,128]{3,2,1,0:T(8,128)(2,1)S(1)}) custom-call(s32[5,256]{1,0:T(8,128)S(1)} %pad_add_fusion.meta, s32[256,256]{1,0:T(8,128)S(1)} %bitcast.30, s32[256,256]{1,0:T(8,128)S(1)} %bitcast.34, ...), custom_call_target="tpu_custom_call", output_to_operand_aliasing={{0}: (5, {})} | custom-call | flops 3750000128 | bytes 1048576 | tf_op jit(solution)/shard_map/spmm_phase2/pallas_call | solution.py:138
  47.8 1.9 %collective-permute-done.8 = bf16[2,4,256,128]{3,2,1,0:T(8,128)(2,1)S(1)} collective-permute-done((bf16[2,4,256,128]{3,2,1,0:T(8,128)(2,1)S(1)}, bf16[2,4,256,128]{3,2,1,0:T(8,128)(2,1)S(1)}, u32[]{:S(2)}, u32[]{:S(2)}) %collective-permute-start.8) | collective-permute-done | bytes 524320 | tf_op jit(solution)/shard_map/ppermute | solution.py:23
  51.1 3.9 %spmm_phase3.1 = (f32[32,256,128]{2,1,0:T(8,128)S(1)}, f32[2,4,256,128]{3,2,1,0:T(8,128)S(1)}, bf16[2,4,256,128]{3,2,1,0:T(8,128)(2,1)S(1)}) custom-call(s32[5,256]{1,0:T(8,128)S(1)} %pad_add_fusion.meta, s32[256,256]{1,0:T(8,128)S(1)} %bitcast.31, s32[256,256]{1,0:T(8,128)S(1)} %bitcast.35, ...), custom_call_target="tpu_custom_call", output_to_operand_aliasing={{0}: (5, {})} | custom-call | flops 3750000128 | bytes 1048576 | tf_op jit(solution)/shard_map/spmm_phase3/pallas_call | solution.py:138
  55.0 4.2 %collective-permute-done.9 = bf16[2,4,256,128]{3,2,1,0:T(8,128)(2,1)S(1)} collective-permute-done((bf16[2,4,256,128]{3,2,1,0:T(8,128)(2,1)S(1)}, bf16[2,4,256,128]{3,2,1,0:T(8,128)(2,1)S(1)}, u32[]{:S(2)}, u32[]{:S(2)}) %collective-permute-start.9) | collective-permute-done | bytes 524320 | tf_op jit(solution)/shard_map/ppermute | solution.py:23
  59.6 1.5 %collective-permute-done.10 = bf16[2,4,256,128]{3,2,1,0:T(8,128)(2,1)S(1)} collective-permute-done((bf16[2,4,256,128]{3,2,1,0:T(8,128)(2,1)S(1)}, bf16[2,4,256,128]{3,2,1,0:T(8,128)(2,1)S(1)}, u32[]{:S(2)}, u32[]{:S(2)}) %collective-permute-start.10) | collective-permute-done | bytes 524320 | tf_op jit(solution)/shard_map/ppermute | solution.py:23
  61.4 3.2 %collective-permute-start.11 = (bf16[4,256,128]{2,1,0:T(8,128)(2,1)S(1)}, bf16[4,256,128]{2,1,0:T(8,128)(2,1)S(1)}, u32[]{:S(2)}, u32[]{:S(2)}) collective-permute-start(bf16[4,256,128]{2,1,0:T(8,128)(2,1)S(1)} %fusion.3), channel_id=1, source_target_pairs={{0,6},{1,3},{2,4},{3,1},{4,2},{5,7},{6,0},{7,5},{8,14},{9,11},{10,... | collective-permute-start | bytes 786440 | tf_op jit(solution)/shard_map/ppermute | solution.py:23
  64.6 4.5 %collective-permute-done.11 = bf16[4,256,128]{2,1,0:T(8,128)(2,1)S(1)} collective-permute-done((bf16[4,256,128]{2,1,0:T(8,128)(2,1)S(1)}, bf16[4,256,128]{2,1,0:T(8,128)(2,1)S(1)}, u32[]{:S(2)}, u32[]{:S(2)}) %collective-permute-start.11) | collective-permute-done | bytes 262176 | tf_op jit(solution)/shard_map/ppermute | solution.py:23
  69.2 2.0 %finish.1 = (bf16[1024,128]{1,0:T(8,128)(2,1)}, f32[128,128]{1,0:T(8,128)S(1)}) custom-call(f32[4,256,128]{2,1,0:T(8,128)S(1)} %fusion.2.hidden, bf16[128,128]{1,0:T(8,128)(2,1)S(1)} %copy-done.2, bf16[1024,128]{1,0:T(8,128)(2,1)S(1)} %copy-done), custom_call_target="tpu_custom_call" | custom-call | tf_op jit(solution)/shard_map/finish/pallas_call | solution.py:170
  72.5 4.6 %collective-permute-start.13 = (bf16[128,128]{1,0:T(8,128)(2,1)S(1)}, bf16[128,128]{1,0:T(8,128)(2,1)S(1)}, u32[]{:S(2)}, u32[]{:S(2)}) collective-permute-start(bf16[128,128]{1,0:T(8,128)(2,1)S(1)} %add_convert_fusion.1), channel_id=1, source_target_pairs={{0,4},{1,5},{2,6},{3,7},{4,0},{5,1},{6,2},{7,3},{8,12},{9,13},{10,... | collective-permute-start | bytes 98312 | tf_op jit(solution)/shard_map/ppermute | solution.py:23
  77.6 1.7 %collective-permute-done.13 = bf16[128,128]{1,0:T(8,128)(2,1)S(1)} collective-permute-done((bf16[128,128]{1,0:T(8,128)(2,1)S(1)}, bf16[128,128]{1,0:T(8,128)(2,1)S(1)}, u32[]{:S(2)}, u32[]{:S(2)}) %collective-permute-start.13) | collective-permute-done | bytes 32800 | tf_op jit(solution)/shard_map/ppermute | solution.py:23
  79.5 5.8 %collective-permute-start.16 = (bf16[128,128]{1,0:T(8,128)(2,1)S(1)}, bf16[128,128]{1,0:T(8,128)(2,1)S(1)}, u32[]{:S(2)}, u32[]{:S(2)}) collective-permute-start(bf16[128,128]{1,0:T(8,128)(2,1)S(1)} %get-tuple-element.24), channel_id=1, source_target_pairs={{0,16},{1,17},{2,18},{3,19},{4,20},{5,21},{6,22},{7,23},{8,24},{9,... | collective-permute-start | bytes 98312 | tf_op jit(solution)/shard_map/ppermute | solution.py:23
  85.7 1.8 %collective-permute-done.16 = bf16[128,128]{1,0:T(8,128)(2,1)S(1)} collective-permute-done((bf16[128,128]{1,0:T(8,128)(2,1)S(1)}, bf16[128,128]{1,0:T(8,128)(2,1)S(1)}, u32[]{:S(2)}, u32[]{:S(2)}) %collective-permute-start.16) | collective-permute-done | bytes 32800 | tf_op jit(solution)/shard_map/ppermute | solution.py:23
  88.2 5.2 %collective-permute-done.20 = bf16[128,128]{1,0:T(8,128)(2,1)S(1)} collective-permute-done((bf16[128,128]{1,0:T(8,128)(2,1)S(1)}, bf16[128,128]{1,0:T(8,128)(2,1)S(1)}, u32[]{:S(2)}, u32[]{:S(2)}) %collective-permute-start.20) | collective-permute-done | bytes 32800 | tf_op jit(solution)/shard_map/ppermute | solution.py:23
  (67 shorter events, 12.6 us)
Async XLA Ops:
  1.7 8.4 %collective-permute-start.2 = (bf16[4,128,256]{2,1,0:T(8,128)(2,1)S(1)}, bf16[4,128,256]{2,1,0:T(8,128)(2,1)S(1)}, u32[]{:S(2)}, u32[]{:S(2)}) collective-permute-start(bf16[4,128,256]{2,1,0:T(8,128)(2,1)S(1)} %transposed.1), channel_id=1, source_target_pairs={{0,8},{1,33},{2,10},{3,35},{4,12},{5,37},{6,14},{7,39},{8,16},{9,4... | collective-permute-start | bytes 786440 | tf_op jit(solution)/shard_map/ppermute | solution.py:23
  3.3 6.8 %collective-permute-start.1 = (bf16[4,128,256]{2,1,0:T(8,128)(2,1)S(1)}, bf16[4,128,256]{2,1,0:T(8,128)(2,1)S(1)}, u32[]{:S(2)}, u32[]{:S(2)}) collective-permute-start(bf16[4,128,256]{2,1,0:T(8,128)(2,1)S(1)} %transposed.1), channel_id=1, source_target_pairs={{0,24},{1,97},{2,26},{3,99},{4,28},{5,101},{6,30},{7,103},{8,0},{9... | collective-permute-start | bytes 786440 | tf_op jit(solution)/shard_map/ppermute | solution.py:23
  5.0 10.2 %collective-permute-start = (bf16[4,128,256]{2,1,0:T(8,128)(2,1)S(1)}, bf16[4,128,256]{2,1,0:T(8,128)(2,1)S(1)}, u32[]{:S(2)}, u32[]{:S(2)}) collective-permute-start(bf16[4,128,256]{2,1,0:T(8,128)(2,1)S(1)} %transposed.1), channel_id=1, source_target_pairs={{0,16},{1,65},{2,18},{3,67},{4,20},{5,69},{6,22},{7,71},{8,24},{9,... | collective-permute-start | bytes 786440 | tf_op jit(solution)/shard_map/ppermute | solution.py:23
  10.2 17.1 %collective-permute-start.5 = (bf16[12,128,256]{2,1,0:T(8,128)(2,1)S(1)}, bf16[12,128,256]{2,1,0:T(8,128)(2,1)S(1)}, u32[]{:S(2)}, u32[]{:S(2)}) collective-permute-start(bf16[12,128,256]{2,1,0:T(8,128)(2,1)S(1)} %pad_maximum_fusion.2), channel_id=1, source_target_pairs={{0,96},{1,25},{2,98},{3,27},{4,100},{5,29},{6,102},{7,31},{8,104},... | collective-permute-start | bytes 2359304 | tf_op jit(solution)/shard_map/ppermute | solution.py:23
  15.0 16.0 %collective-permute-start.3 = (bf16[12,128,256]{2,1,0:T(8,128)(2,1)S(1)}, bf16[12,128,256]{2,1,0:T(8,128)(2,1)S(1)}, u32[]{:S(2)}, u32[]{:S(2)}) collective-permute-start(bf16[12,128,256]{2,1,0:T(8,128)(2,1)S(1)} %pad_maximum_fusion.2), channel_id=1, source_target_pairs={{0,32},{1,9},{2,34},{3,11},{4,36},{5,13},{6,38},{7,15},{8,40},{9,1... | collective-permute-start | bytes 2359304 | tf_op jit(solution)/shard_map/ppermute | solution.py:23
  15.2 28.0 %collective-permute-start.7 = (bf16[4,128,256]{2,1,0:T(8,128)(2,1)S(1)}, bf16[4,128,256]{2,1,0:T(8,128)(2,1)S(1)}, u32[]{:S(2)}, u32[]{:S(2)}) collective-permute-start(bf16[4,128,256]{2,1,0:T(8,128)(2,1)S(1)} %collective-permute-done), channel_id=1, source_target_pairs={{0,64},{1,17},{2,66},{3,19},{4,68},{5,21},{6,70},{7,23},{8,72},{9,... | collective-permute-start | bytes 786440 | tf_op jit(solution)/shard_map/ppermute | solution.py:23
  31.1 12.0 %collective-permute-start.6 = (bf16[10,128,256]{2,1,0:T(8,128)(2,1)S(1)}, bf16[10,128,256]{2,1,0:T(8,128)(2,1)S(1)}, u32[]{:S(2)}, u32[]{:S(2)}) collective-permute-start(bf16[10,128,256]{2,1,0:T(8,128)(2,1)S(1)} %get-tuple-element.28), channel_id=1, source_target_pairs={{0,96},{1,25},{2,98},{3,27},{4,100},{5,29},{6,102},{7,31},{8,104},... | collective-permute-start | bytes 1966088 | tf_op jit(solution)/shard_map/ppermute | solution.py:23
  31.3 11.8 %collective-permute-start.4 = (bf16[10,128,256]{2,1,0:T(8,128)(2,1)S(1)}, bf16[10,128,256]{2,1,0:T(8,128)(2,1)S(1)}, u32[]{:S(2)}, u32[]{:S(2)}) collective-permute-start(bf16[10,128,256]{2,1,0:T(8,128)(2,1)S(1)} %get-tuple-element.29), channel_id=1, source_target_pairs={{0,32},{1,9},{2,34},{3,11},{4,36},{5,13},{6,38},{7,15},{8,40},{9,1... | collective-permute-start | bytes 1966088 | tf_op jit(solution)/shard_map/ppermute | solution.py:23
  47.7 2.0 %collective-permute-start.8 = (bf16[2,4,256,128]{3,2,1,0:T(8,128)(2,1)S(1)}, bf16[2,4,256,128]{3,2,1,0:T(8,128)(2,1)S(1)}, u32[]{:S(2)}, u32[]{:S(2)}) collective-permute-start(bf16[2,4,256,128]{3,2,1,0:T(8,128)(2,1)S(1)} %get-tuple-element.14), channel_id=1, source_target_pairs={{0,1},{1,0},{2,3},{3,2},{4,5},{5,4},{6,7},{7,6},{8,9},{9,8},{10,11... | collective-permute-start | bytes 1572872 | tf_op jit(solution)/shard_map/ppermute | solution.py:23
  49.8 9.3 %collective-permute-start.9 = (bf16[2,4,256,128]{3,2,1,0:T(8,128)(2,1)S(1)}, bf16[2,4,256,128]{3,2,1,0:T(8,128)(2,1)S(1)}, u32[]{:S(2)}, u32[]{:S(2)}) collective-permute-start(bf16[2,4,256,128]{3,2,1,0:T(8,128)(2,1)S(1)} %add_convert_fusion), channel_id=1, source_target_pairs={{0,2},{1,7},{2,0},{3,5},{4,6},{5,3},{6,4},{7,1},{8,10},{9,15},{10,... | collective-permute-start | bytes 1572872 | tf_op jit(solution)/shard_map/ppermute | solution.py:23
  59.1 2.1 %collective-permute-start.10 = (bf16[2,4,256,128]{3,2,1,0:T(8,128)(2,1)S(1)}, bf16[2,4,256,128]{3,2,1,0:T(8,128)(2,1)S(1)}, u32[]{:S(2)}, u32[]{:S(2)}) collective-permute-start(bf16[2,4,256,128]{3,2,1,0:T(8,128)(2,1)S(1)} %get-tuple-element.20), channel_id=1, source_target_pairs={{0,1},{1,0},{2,3},{3,2},{4,5},{5,4},{6,7},{7,6},{8,9},{9,8},{10,11... | collective-permute-start | bytes 1572872 | tf_op jit(solution)/shard_map/ppermute | solution.py:23
  61.3 7.8 %copy-start = (bf16[1024,128]{1,0:T(8,128)(2,1)S(1)}, bf16[1024,128]{1,0:T(8,128)(2,1)}, u32[]{:S(2)}) copy-start(bf16[1024,128]{1,0:T(8,128)(2,1)} %cotangent.1) | copy-start | bytes 786436
  61.3 7.8 %copy-start.2 = (bf16[128,128]{1,0:T(8,128)(2,1)S(1)}, bf16[128,128]{1,0:T(8,128)(2,1)}, u32[]{:S(2)}) copy-start(bf16[128,128]{1,0:T(8,128)(2,1)} %weight.1) | copy-start | bytes 98308
  61.4 7.7 %collective-permute-start.11 = (bf16[4,256,128]{2,1,0:T(8,128)(2,1)S(1)}, bf16[4,256,128]{2,1,0:T(8,128)(2,1)S(1)}, u32[]{:S(2)}, u32[]{:S(2)}) collective-permute-start(bf16[4,256,128]{2,1,0:T(8,128)(2,1)S(1)} %fusion.3), channel_id=1, source_target_pairs={{0,6},{1,3},{2,4},{3,1},{4,2},{5,7},{6,0},{7,5},{8,14},{9,11},{10,... | collective-permute-start | bytes 786440 | tf_op jit(solution)/shard_map/ppermute | solution.py:23
  71.1 1.3 %collective-permute-start.12 = (f32[128,128]{1,0:T(8,128)S(1)}, f32[128,128]{1,0:T(8,128)S(1)}, u32[]{:S(2)}, u32[]{:S(2)}) collective-permute-start(f32[128,128]{1,0:T(8,128)S(1)} %get-tuple-element.23), channel_id=1, source_target_pairs={{0,1},{1,0},{2,3},{3,2},{4,5},{5,4},{6,7},{7,6},{8,9},{9,8},{10,11... | collective-permute-start | bytes 196616 | tf_op jit(solution)/shard_map/ppermute | solution.py:23
  72.4 5.2 %collective-permute-start.14 = (bf16[128,128]{1,0:T(8,128)(2,1)S(1)}, bf16[128,128]{1,0:T(8,128)(2,1)S(1)}, u32[]{:S(2)}, u32[]{:S(2)}) collective-permute-start(bf16[128,128]{1,0:T(8,128)(2,1)S(1)} %add_convert_fusion.1), channel_id=1, source_target_pairs={{0,2},{1,7},{2,4},{3,1},{4,6},{5,3},{6,0},{7,5},{8,10},{9,15},{10,... | collective-permute-start | bytes 98312 | tf_op jit(solution)/shard_map/ppermute | solution.py:23
  72.5 6.8 %collective-permute-start.13 = (bf16[128,128]{1,0:T(8,128)(2,1)S(1)}, bf16[128,128]{1,0:T(8,128)(2,1)S(1)}, u32[]{:S(2)}, u32[]{:S(2)}) collective-permute-start(bf16[128,128]{1,0:T(8,128)(2,1)S(1)} %add_convert_fusion.1), channel_id=1, source_target_pairs={{0,4},{1,5},{2,6},{3,7},{4,0},{5,1},{6,2},{7,3},{8,12},{9,13},{10,... | collective-permute-start | bytes 98312 | tf_op jit(solution)/shard_map/ppermute | solution.py:23
  77.6 1.7 %collective-permute-start.15 = (bf16[128,128]{1,0:T(8,128)(2,1)S(1)}, bf16[128,128]{1,0:T(8,128)(2,1)S(1)}, u32[]{:S(2)}, u32[]{:S(2)}) collective-permute-start(bf16[128,128]{1,0:T(8,128)(2,1)S(1)} %collective-permute-done.14), channel_id=1, source_target_pairs={{0,1},{1,0},{2,3},{3,2},{4,5},{5,4},{6,7},{7,6},{8,9},{9,8},{10,11... | collective-permute-start | bytes 98312 | tf_op jit(solution)/shard_map/ppermute | solution.py:23
  79.3 6.4 %collective-permute-start.17 = (bf16[128,128]{1,0:T(8,128)(2,1)S(1)}, bf16[128,128]{1,0:T(8,128)(2,1)S(1)}, u32[]{:S(2)}, u32[]{:S(2)}) collective-permute-start(bf16[128,128]{1,0:T(8,128)(2,1)S(1)} %get-tuple-element.24), channel_id=1, source_target_pairs={{0,8},{1,25},{2,10},{3,27},{4,12},{5,29},{6,14},{7,31},{8,16},{9,1... | collective-permute-start | bytes 98312 | tf_op jit(solution)/shard_map/ppermute | solution.py:23
  79.5 8.0 %collective-permute-start.16 = (bf16[128,128]{1,0:T(8,128)(2,1)S(1)}, bf16[128,128]{1,0:T(8,128)(2,1)S(1)}, u32[]{:S(2)}, u32[]{:S(2)}) collective-permute-start(bf16[128,128]{1,0:T(8,128)(2,1)S(1)} %get-tuple-element.24), channel_id=1, source_target_pairs={{0,16},{1,17},{2,18},{3,19},{4,20},{5,21},{6,22},{7,23},{8,24},{9,... | collective-permute-start | bytes 98312 | tf_op jit(solution)/shard_map/ppermute | solution.py:23
  85.7 1.8 %collective-permute-start.18 = (bf16[128,128]{1,0:T(8,128)(2,1)S(1)}, bf16[128,128]{1,0:T(8,128)(2,1)S(1)}, u32[]{:S(2)}, u32[]{:S(2)}) collective-permute-start(bf16[128,128]{1,0:T(8,128)(2,1)S(1)} %collective-permute-done.17), channel_id=1, source_target_pairs={{0,1},{1,0},{2,3},{3,2},{4,5},{5,4},{6,7},{7,6},{8,9},{9,8},{10,11... | collective-permute-start | bytes 98312 | tf_op jit(solution)/shard_map/ppermute | solution.py:23
  87.5 5.9 %collective-permute-start.20 = (bf16[128,128]{1,0:T(8,128)(2,1)S(1)}, bf16[128,128]{1,0:T(8,128)(2,1)S(1)}, u32[]{:S(2)}, u32[]{:S(2)}) collective-permute-start(bf16[128,128]{1,0:T(8,128)(2,1)S(1)} %fusion.23), channel_id=1, source_target_pairs={{0,32},{1,97},{2,34},{3,99},{4,36},{5,101},{6,38},{7,103},{8,40},{... | collective-permute-start | bytes 98312 | tf_op jit(solution)/shard_map/ppermute | solution.py:23
  87.6 5.8 %collective-permute-start.19 = (bf16[128,128]{1,0:T(8,128)(2,1)S(1)}, bf16[128,128]{1,0:T(8,128)(2,1)S(1)}, u32[]{:S(2)}, u32[]{:S(2)}) collective-permute-start(bf16[128,128]{1,0:T(8,128)(2,1)S(1)} %fusion.23), channel_id=1, source_target_pairs={{0,64},{1,65},{2,66},{3,67},{4,68},{5,69},{6,70},{7,71},{8,72},{9,... | collective-permute-start | bytes 98312 | tf_op jit(solution)/shard_map/ppermute | solution.py:23
  93.4 1.2 %collective-permute-start.21 = (bf16[128,128]{1,0:T(8,128)(2,1)S(1)}, bf16[128,128]{1,0:T(8,128)(2,1)S(1)}, u32[]{:S(2)}, u32[]{:S(2)}) collective-permute-start(bf16[128,128]{1,0:T(8,128)(2,1)S(1)} %collective-permute-done.20), channel_id=1, source_target_pairs={{0,1},{1,0},{2,3},{3,2},{4,5},{5,4},{6,7},{7,6},{8,9},{9,8},{10,11... | collective-permute-start | bytes 98312 | tf_op jit(solution)/shard_map/ppermute | solution.py:23
  (4 other events, 21.7 us)

commit v5 on v4

--- a/solution.py
+++ b/solution.py
@@ -233,12 +233,16 @@
 
     away = add(keep, swap_cores(give)).astype(BF)
     away, total = lax.optimization_barrier((away, total))
-    got = permute(away, lambda y, x, z, k: (y, x, z ^ (1 + 2 * k), k))
+
+    def first_chip(a):
+        return permute(a, lambda y, x, z, k: (y, x, z ^ (1 + 2 * k), k))
+
+    got_far, got_near = first_chip(away[1]), first_chip(away[0])
     total, keep, give = spmm(3, *slots, rest, total)
-    give, got = lax.optimization_barrier((give, got))
+    give, got_far = lax.optimization_barrier((give, got_far))
     home = add(keep, swap_cores(give))
-    mine, pair = add(home[0], got[0]), add(home[1], got[1])
-    hidden = add(mine, permute(pair.astype(BF), lambda y, x, z, k: (y, x, z ^ (3 - 2 * k), k)))
+    pair = add(home[1], got_far).astype(BF)
+    hidden = add(add(home[0], got_near), permute(pair, lambda y, x, z, k: (y, x, z ^ (3 - 2 * k), k)))
 
     node_out, grad = finish(hidden, weight, cotangent)
     grad = grad + swap_cores(grad)

time: 96.4 us -> 93.9 us (0.974)
  waiting for transfers between devices: 36.3 us -> 30.4 us
  starting transfers between devices: 30 us -> 33.5 us
    ppermute x22 -> x23, waiting for transfers between devices: 36.3 us -> 30.4 us  [permute(): return lax.ppermute(a, ('row', 'col'), pairs)]
    ppermute x22 -> x23, starting transfers between devices: 30 us -> 33.5 us  [permute(): return lax.ppermute(a, ('row', 'col'), pairs)]
  transfers between devices with their start and end apart: 22 -> 23, of which waited for: 14 -> 16; matrix products, arithmetic and copies ran while one was open for 4% -> 4% of each run, Pallas kernels for 16% -> 17%
where the time goes in v5:
time: 93.9 us; the launch traced here: 92.6 us
  starting transfers between devices  33.5 us (36%)
  waiting for transfers between devices  30.4 us (32%)
  Pallas kernels  21.7 us (23%)
  other arithmetic  4.95 us (5%)
  local copies, waits for them, and re-layouts  1.18 us (1%)
  between operations  0.96 us (1%)
    ppermute x23, starting transfers between devices, permute(): return lax.ppermute(a, ('row', 'col'), pairs)  33.5 us
    ppermute x23, waiting for transfers between devices, permute(): return lax.ppermute(a, ('row', 'col'), pairs)  30.4 us
    pallas_call x4, Pallas kernels, spmm(): pl.pallas_call(functools.partial(spmm_kernel, phase), out_shape=out, in_s...  19.6 us
    pallas_call x1, Pallas kernels, finish(): pl.pallas_call(finish_kernel, out_shape=[jax.ShapeDtypeStruct((1024, 128)...  1.95 us
  transfers between devices with their start and end apart: 23, of which 16 were waited for; matrix products, arithmetic and copies ran while one was open for 4% of the time, Pallas kernels for 17%

profile of v5, /device:TPU:0, one launch (start us, length us, event | category | flops | bytes accessed | tf_op | source)
XLA Modules:
  0.0 92.6 jit_solution(6754744318200946602)
XLA Ops:
  1.7 1.6 %collective-permute-start.2 = (bf16[4,128,256]{2,1,0:T(8,128)(2,1)S(1)}, bf16[4,128,256]{2,1,0:T(8,128)(2,1)S(1)}, u32[]{:S(2)}, u32[]{:S(2)}) collective-permute-start(bf16[4,128,256]{2,1,0:T(8,128)(2,1)S(1)} %transposed.1), channel_id=1, source_target_pairs={{0,8},{1,33},{2,10},{3,35},{4,12},{5,37},{6,14},{7,39},{8,16},{9,4... | collective-permute-start | bytes 786440 | tf_op jit(solution)/shard_map/ppermute | solution.py:23
  3.3 1.7 %collective-permute-start.1 = (bf16[4,128,256]{2,1,0:T(8,128)(2,1)S(1)}, bf16[4,128,256]{2,1,0:T(8,128)(2,1)S(1)}, u32[]{:S(2)}, u32[]{:S(2)}) collective-permute-start(bf16[4,128,256]{2,1,0:T(8,128)(2,1)S(1)} %transposed.1), channel_id=1, source_target_pairs={{0,24},{1,97},{2,26},{3,99},{4,28},{5,101},{6,30},{7,103},{8,0},{9... | collective-permute-start | bytes 786440 | tf_op jit(solution)/shard_map/ppermute | solution.py:23
  5.0 1.9 %collective-permute-start = (bf16[4,128,256]{2,1,0:T(8,128)(2,1)S(1)}, bf16[4,128,256]{2,1,0:T(8,128)(2,1)S(1)}, u32[]{:S(2)}, u32[]{:S(2)}) collective-permute-start(bf16[4,128,256]{2,1,0:T(8,128)(2,1)S(1)} %transposed.1), channel_id=1, source_target_pairs={{0,16},{1,65},{2,18},{3,67},{4,20},{5,69},{6,22},{7,71},{8,24},{9,... | collective-permute-start | bytes 786440 | tf_op jit(solution)/shard_map/ppermute | solution.py:23
  10.2 4.7 %collective-permute-start.5 = (bf16[12,128,256]{2,1,0:T(8,128)(2,1)S(1)}, bf16[12,128,256]{2,1,0:T(8,128)(2,1)S(1)}, u32[]{:S(2)}, u32[]{:S(2)}) collective-permute-start(bf16[12,128,256]{2,1,0:T(8,128)(2,1)S(1)} %pad_maximum_fusion.2), channel_id=1, source_target_pairs={{0,96},{1,25},{2,98},{3,27},{4,100},{5,29},{6,102},{7,31},{8,104},... | collective-permute-start | bytes 2359304 | tf_op jit(solution)/shard_map/ppermute | solution.py:23
  15.2 1.6 %collective-permute-start.7 = (bf16[4,128,256]{2,1,0:T(8,128)(2,1)S(1)}, bf16[4,128,256]{2,1,0:T(8,128)(2,1)S(1)}, u32[]{:S(2)}, u32[]{:S(2)}) collective-permute-start(bf16[4,128,256]{2,1,0:T(8,128)(2,1)S(1)} %collective-permute-done), channel_id=1, source_target_pairs={{0,64},{1,17},{2,66},{3,19},{4,68},{5,21},{6,70},{7,23},{8,72},{9,... | collective-permute-start | bytes 786440 | tf_op jit(solution)/shard_map/ppermute | solution.py:23
  17.0 5.7 %spmm_phase0.1.rest_0_ = f32[32,256,128]{2,1,0:T(8,128)S(1)} custom-call(s32[5,256]{1,0:T(8,128)S(1)} %pad_add_fusion.meta, s32[256,256]{1,0:T(8,128)S(1)} %bitcast.38, s32[256,256]{1,0:T(8,128)S(1)} %bitcast.42, bf16[256,256]{1,0:T(8,128)(2,1)S(1)} %bitcast.46, bf16[16,128,256]{2,1,0:T(8,128)(2,1)S(1)} %pad_maximum_fusion.1.pieces), custom_call_target="tpu_custom_call" | custom-call | flops 5000000000 | bytes 1048576 | tf_op jit(solution)/shard_map/spmm_phase0/pallas_call | solution.py:138
  22.7 4.6 %collective-permute-done.5 = bf16[12,128,256]{2,1,0:T(8,128)(2,1)S(1)} collective-permute-done((bf16[12,128,256]{2,1,0:T(8,128)(2,1)S(1)}, bf16[12,128,256]{2,1,0:T(8,128)(2,1)S(1)}, u32[]{:S(2)}, u32[]{:S(2)}) %collective-permute-start.5) | collective-permute-done | bytes 786464 | tf_op jit(solution)/shard_map/ppermute | solution.py:23
  27.3 3.7 %collective-permute-done.3 = bf16[12,128,256]{2,1,0:T(8,128)(2,1)S(1)} collective-permute-done((bf16[12,128,256]{2,1,0:T(8,128)(2,1)S(1)}, bf16[12,128,256]{2,1,0:T(8,128)(2,1)S(1)}, u32[]{:S(2)}, u32[]{:S(2)}) %collective-permute-start.3) | collective-permute-done | bytes 786464 | tf_op jit(solution)/shard_map/ppermute | solution.py:23
  31.3 2.0 %collective-permute-start.4 = (bf16[10,128,256]{2,1,0:T(8,128)(2,1)S(1)}, bf16[10,128,256]{2,1,0:T(8,128)(2,1)S(1)}, u32[]{:S(2)}, u32[]{:S(2)}) collective-permute-start(bf16[10,128,256]{2,1,0:T(8,128)(2,1)S(1)} %get-tuple-element.31), channel_id=1, source_target_pairs={{0,32},{1,9},{2,34},{3,11},{4,36},{5,13},{6,38},{7,15},{8,40},{9,1... | collective-permute-start | bytes 1966088 | tf_op jit(solution)/shard_map/ppermute | solution.py:23
  33.4 6.4 %spmm_phase1.1.rest_0_ = f32[32,256,128]{2,1,0:T(8,128)S(1)} custom-call(s32[5,256]{1,0:T(8,128)S(1)} %pad_add_fusion.meta, s32[256,256]{1,0:T(8,128)S(1)} %bitcast.39, s32[256,256]{1,0:T(8,128)S(1)} %bitcast.43, bf16[256,256]{1,0:T(8,128)(2,1)S(1)} %bitcast.47, bf16[24,128,256]{2,1,0:T(8,128)(2,1)S(1)} %pad_maximum_fusion.pieces, ...), custom_call_target="tpu_custom_call", output_to_operand_aliasing={{}: (5, {})} | custom-call | flops 7500000256 | bytes 1048576 | tf_op jit(solution)/shard_map/spmm_phase1/pallas_call | solution.py:138
  39.8 3.3 %collective-permute-done.4 = bf16[10,128,256]{2,1,0:T(8,128)(2,1)S(1)} collective-permute-done((bf16[10,128,256]{2,1,0:T(8,128)(2,1)S(1)}, bf16[10,128,256]{2,1,0:T(8,128)(2,1)S(1)}, u32[]{:S(2)}, u32[]{:S(2)}) %collective-permute-start.4) | collective-permute-done | bytes 655392 | tf_op jit(solution)/shard_map/ppermute | solution.py:23
  43.3 3.7 %spmm_phase2.1 = (f32[32,256,128]{2,1,0:T(8,128)S(1)}, f32[2,4,256,128]{3,2,1,0:T(8,128)S(1)}, bf16[2,4,256,128]{3,2,1,0:T(8,128)(2,1)S(1)}) custom-call(s32[5,256]{1,0:T(8,128)S(1)} %pad_add_fusion.meta, s32[256,256]{1,0:T(8,128)S(1)} %bitcast.40, s32[256,256]{1,0:T(8,128)S(1)} %bitcast.44, ...), custom_call_target="tpu_custom_call", output_to_operand_aliasing={{0}: (5, {})} | custom-call | flops 3750000128 | bytes 1048576 | tf_op jit(solution)/shard_map/spmm_phase2/pallas_call | solution.py:138
  47.1 1.9 %collective-permute-done.8 = bf16[2,4,256,128]{3,2,1,0:T(8,128)(2,1)S(1)} collective-permute-done((bf16[2,4,256,128]{3,2,1,0:T(8,128)(2,1)S(1)}, bf16[2,4,256,128]{3,2,1,0:T(8,128)(2,1)S(1)}, u32[]{:S(2)}, u32[]{:S(2)}) %collective-permute-start.8) | collective-permute-done | bytes 524320 | tf_op jit(solution)/shard_map/ppermute | solution.py:23
  49.1 2.8 %collective-permute-start.9 = (bf16[4,256,128]{2,1,0:T(8,128)(2,1)S(1)}, bf16[4,256,128]{2,1,0:T(8,128)(2,1)S(1)}, u32[]{:S(2)}, u32[]{:S(2)}) collective-permute-start(bf16[4,256,128]{2,1,0:T(8,128)(2,1)S(1)} %get-tuple-element.29), channel_id=1, source_target_pairs={{0,2},{1,7},{2,0},{3,5},{4,6},{5,3},{6,4},{7,1},{8,10},{9,15},{10,... | collective-permute-start | bytes 786440 | tf_op jit(solution)/shard_map/ppermute | solution.py:23
  51.9 3.9 %spmm_phase3.1 = (f32[32,256,128]{2,1,0:T(8,128)S(1)}, f32[2,4,256,128]{3,2,1,0:T(8,128)S(1)}, bf16[2,4,256,128]{3,2,1,0:T(8,128)(2,1)S(1)}) custom-call(s32[5,256]{1,0:T(8,128)S(1)} %pad_add_fusion.meta, s32[256,256]{1,0:T(8,128)S(1)} %bitcast.41, s32[256,256]{1,0:T(8,128)S(1)} %bitcast.45, ...), custom_call_target="tpu_custom_call", output_to_operand_aliasing={{0}: (5, {})} | custom-call | flops 3750000128 | bytes 1048576 | tf_op jit(solution)/shard_map/spmm_phase3/pallas_call | solution.py:138
  58.8 3.0 %collective-permute-start.12 = (bf16[4,256,128]{2,1,0:T(8,128)(2,1)S(1)}, bf16[4,256,128]{2,1,0:T(8,128)(2,1)S(1)}, u32[]{:S(2)}, u32[]{:S(2)}) collective-permute-start(bf16[4,256,128]{2,1,0:T(8,128)(2,1)S(1)} %fusion.1), channel_id=1, source_target_pairs={{0,6},{1,3},{2,4},{3,1},{4,2},{5,7},{6,0},{7,5},{8,14},{9,11},{10,... | collective-permute-start | bytes 786440 | tf_op jit(solution)/shard_map/ppermute | solution.py:23
  61.8 2.2 %collective-permute-done.11 = bf16[4,256,128]{2,1,0:T(8,128)(2,1)S(1)} collective-permute-done((bf16[4,256,128]{2,1,0:T(8,128)(2,1)S(1)}, bf16[4,256,128]{2,1,0:T(8,128)(2,1)S(1)}, u32[]{:S(2)}, u32[]{:S(2)}) %collective-permute-start.11) | collective-permute-done | bytes 262176 | tf_op jit(solution)/shard_map/ppermute | solution.py:23
  64.1 2.5 %collective-permute-done.12 = bf16[4,256,128]{2,1,0:T(8,128)(2,1)S(1)} collective-permute-done((bf16[4,256,128]{2,1,0:T(8,128)(2,1)S(1)}, bf16[4,256,128]{2,1,0:T(8,128)(2,1)S(1)}, u32[]{:S(2)}, u32[]{:S(2)}) %collective-permute-start.12) | collective-permute-done | bytes 262176 | tf_op jit(solution)/shard_map/ppermute | solution.py:23
  66.7 1.9 %finish.1 = (bf16[1024,128]{1,0:T(8,128)(2,1)}, f32[128,128]{1,0:T(8,128)S(1)}) custom-call(f32[4,256,128]{2,1,0:T(8,128)S(1)} %fusion.3.hidden, bf16[128,128]{1,0:T(8,128)(2,1)S(1)} %copy-done.2, bf16[1024,128]{1,0:T(8,128)(2,1)S(1)} %copy-done), custom_call_target="tpu_custom_call" | custom-call | tf_op jit(solution)/shard_map/finish/pallas_call | solution.py:170
  70.4 4.0 %collective-permute-start.14 = (bf16[128,128]{1,0:T(8,128)(2,1)S(1)}, bf16[128,128]{1,0:T(8,128)(2,1)S(1)}, u32[]{:S(2)}, u32[]{:S(2)}) collective-permute-start(bf16[128,128]{1,0:T(8,128)(2,1)S(1)} %add_convert_fusion.1), channel_id=1, source_target_pairs={{0,4},{1,5},{2,6},{3,7},{4,0},{5,1},{6,2},{7,3},{8,12},{9,13},{10,... | collective-permute-start | bytes 98312 | tf_op jit(solution)/shard_map/ppermute | solution.py:23
  75.1 1.5 %collective-permute-done.14 = bf16[128,128]{1,0:T(8,128)(2,1)S(1)} collective-permute-done((bf16[128,128]{1,0:T(8,128)(2,1)S(1)}, bf16[128,128]{1,0:T(8,128)(2,1)S(1)}, u32[]{:S(2)}, u32[]{:S(2)}) %collective-permute-start.14) | collective-permute-done | bytes 32800 | tf_op jit(solution)/shard_map/ppermute | solution.py:23
  77.3 5.7 %collective-permute-start.17 = (bf16[128,128]{1,0:T(8,128)(2,1)S(1)}, bf16[128,128]{1,0:T(8,128)(2,1)S(1)}, u32[]{:S(2)}, u32[]{:S(2)}) collective-permute-start(bf16[128,128]{1,0:T(8,128)(2,1)S(1)} %get-tuple-element.24), channel_id=1, source_target_pairs={{0,16},{1,17},{2,18},{3,19},{4,20},{5,21},{6,22},{7,23},{8,24},{9,... | collective-permute-start | bytes 98312 | tf_op jit(solution)/shard_map/ppermute | solution.py:23
  83.5 1.8 %collective-permute-done.17 = bf16[128,128]{1,0:T(8,128)(2,1)S(1)} collective-permute-done((bf16[128,128]{1,0:T(8,128)(2,1)S(1)}, bf16[128,128]{1,0:T(8,128)(2,1)S(1)}, u32[]{:S(2)}, u32[]{:S(2)}) %collective-permute-start.17) | collective-permute-done | bytes 32800 | tf_op jit(solution)/shard_map/ppermute | solution.py:23
  86.4 4.4 %collective-permute-done.21 = bf16[128,128]{1,0:T(8,128)(2,1)S(1)} collective-permute-done((bf16[128,128]{1,0:T(8,128)(2,1)S(1)}, bf16[128,128]{1,0:T(8,128)(2,1)S(1)}, u32[]{:S(2)}, u32[]{:S(2)}) %collective-permute-start.21) | collective-permute-done | bytes 32800 | tf_op jit(solution)/shard_map/ppermute | solution.py:23
  (70 shorter events, 15.1 us)
Async XLA Ops:
  1.7 8.4 %collective-permute-start.2 = (bf16[4,128,256]{2,1,0:T(8,128)(2,1)S(1)}, bf16[4,128,256]{2,1,0:T(8,128)(2,1)S(1)}, u32[]{:S(2)}, u32[]{:S(2)}) collective-permute-start(bf16[4,128,256]{2,1,0:T(8,128)(2,1)S(1)} %transposed.1), channel_id=1, source_target_pairs={{0,8},{1,33},{2,10},{3,35},{4,12},{5,37},{6,14},{7,39},{8,16},{9,4... | collective-permute-start | bytes 786440 | tf_op jit(solution)/shard_map/ppermute | solution.py:23
  3.3 6.8 %collective-permute-start.1 = (bf16[4,128,256]{2,1,0:T(8,128)(2,1)S(1)}, bf16[4,128,256]{2,1,0:T(8,128)(2,1)S(1)}, u32[]{:S(2)}, u32[]{:S(2)}) collective-permute-start(bf16[4,128,256]{2,1,0:T(8,128)(2,1)S(1)} %transposed.1), channel_id=1, source_target_pairs={{0,24},{1,97},{2,26},{3,99},{4,28},{5,101},{6,30},{7,103},{8,0},{9... | collective-permute-start | bytes 786440 | tf_op jit(solution)/shard_map/ppermute | solution.py:23
  5.0 10.2 %collective-permute-start = (bf16[4,128,256]{2,1,0:T(8,128)(2,1)S(1)}, bf16[4,128,256]{2,1,0:T(8,128)(2,1)S(1)}, u32[]{:S(2)}, u32[]{:S(2)}) collective-permute-start(bf16[4,128,256]{2,1,0:T(8,128)(2,1)S(1)} %transposed.1), channel_id=1, source_target_pairs={{0,16},{1,65},{2,18},{3,67},{4,20},{5,69},{6,22},{7,71},{8,24},{9,... | collective-permute-start | bytes 786440 | tf_op jit(solution)/shard_map/ppermute | solution.py:23
  10.2 17.1 %collective-permute-start.5 = (bf16[12,128,256]{2,1,0:T(8,128)(2,1)S(1)}, bf16[12,128,256]{2,1,0:T(8,128)(2,1)S(1)}, u32[]{:S(2)}, u32[]{:S(2)}) collective-permute-start(bf16[12,128,256]{2,1,0:T(8,128)(2,1)S(1)} %pad_maximum_fusion.2), channel_id=1, source_target_pairs={{0,96},{1,25},{2,98},{3,27},{4,100},{5,29},{6,102},{7,31},{8,104},... | collective-permute-start | bytes 2359304 | tf_op jit(solution)/shard_map/ppermute | solution.py:23
  15.0 16.0 %collective-permute-start.3 = (bf16[12,128,256]{2,1,0:T(8,128)(2,1)S(1)}, bf16[12,128,256]{2,1,0:T(8,128)(2,1)S(1)}, u32[]{:S(2)}, u32[]{:S(2)}) collective-permute-start(bf16[12,128,256]{2,1,0:T(8,128)(2,1)S(1)} %pad_maximum_fusion.2), channel_id=1, source_target_pairs={{0,32},{1,9},{2,34},{3,11},{4,36},{5,13},{6,38},{7,15},{8,40},{9,1... | collective-permute-start | bytes 2359304 | tf_op jit(solution)/shard_map/ppermute | solution.py:23
  15.2 28.0 %collective-permute-start.7 = (bf16[4,128,256]{2,1,0:T(8,128)(2,1)S(1)}, bf16[4,128,256]{2,1,0:T(8,128)(2,1)S(1)}, u32[]{:S(2)}, u32[]{:S(2)}) collective-permute-start(bf16[4,128,256]{2,1,0:T(8,128)(2,1)S(1)} %collective-permute-done), channel_id=1, source_target_pairs={{0,64},{1,17},{2,66},{3,19},{4,68},{5,21},{6,70},{7,23},{8,72},{9,... | collective-permute-start | bytes 786440 | tf_op jit(solution)/shard_map/ppermute | solution.py:23
  31.1 12.0 %collective-permute-start.6 = (bf16[10,128,256]{2,1,0:T(8,128)(2,1)S(1)}, bf16[10,128,256]{2,1,0:T(8,128)(2,1)S(1)}, u32[]{:S(2)}, u32[]{:S(2)}) collective-permute-start(bf16[10,128,256]{2,1,0:T(8,128)(2,1)S(1)} %get-tuple-element.30), channel_id=1, source_target_pairs={{0,96},{1,25},{2,98},{3,27},{4,100},{5,29},{6,102},{7,31},{8,104},... | collective-permute-start | bytes 1966088 | tf_op jit(solution)/shard_map/ppermute | solution.py:23
  31.3 11.8 %collective-permute-start.4 = (bf16[10,128,256]{2,1,0:T(8,128)(2,1)S(1)}, bf16[10,128,256]{2,1,0:T(8,128)(2,1)S(1)}, u32[]{:S(2)}, u32[]{:S(2)}) collective-permute-start(bf16[10,128,256]{2,1,0:T(8,128)(2,1)S(1)} %get-tuple-element.31), channel_id=1, source_target_pairs={{0,32},{1,9},{2,34},{3,11},{4,36},{5,13},{6,38},{7,15},{8,40},{9,1... | collective-permute-start | bytes 1966088 | tf_op jit(solution)/shard_map/ppermute | solution.py:23
  47.0 2.0 %collective-permute-start.8 = (bf16[2,4,256,128]{3,2,1,0:T(8,128)(2,1)S(1)}, bf16[2,4,256,128]{3,2,1,0:T(8,128)(2,1)S(1)}, u32[]{:S(2)}, u32[]{:S(2)}) collective-permute-start(bf16[2,4,256,128]{3,2,1,0:T(8,128)(2,1)S(1)} %get-tuple-element.14), channel_id=1, source_target_pairs={{0,1},{1,0},{2,3},{3,2},{4,5},{5,4},{6,7},{7,6},{8,9},{9,8},{10,11... | collective-permute-start | bytes 1572872 | tf_op jit(solution)/shard_map/ppermute | solution.py:23
  49.1 7.1 %collective-permute-start.9 = (bf16[4,256,128]{2,1,0:T(8,128)(2,1)S(1)}, bf16[4,256,128]{2,1,0:T(8,128)(2,1)S(1)}, u32[]{:S(2)}, u32[]{:S(2)}) collective-permute-start(bf16[4,256,128]{2,1,0:T(8,128)(2,1)S(1)} %get-tuple-element.29), channel_id=1, source_target_pairs={{0,2},{1,7},{2,0},{3,5},{4,6},{5,3},{6,4},{7,1},{8,10},{9,15},{10,... | collective-permute-start | bytes 786440 | tf_op jit(solution)/shard_map/ppermute | solution.py:23
  56.2 2.3 %collective-permute-start.10 = (bf16[2,4,256,128]{3,2,1,0:T(8,128)(2,1)S(1)}, bf16[2,4,256,128]{3,2,1,0:T(8,128)(2,1)S(1)}, u32[]{:S(2)}, u32[]{:S(2)}) collective-permute-start(bf16[2,4,256,128]{3,2,1,0:T(8,128)(2,1)S(1)} %get-tuple-element.20), channel_id=1, source_target_pairs={{0,1},{1,0},{2,3},{3,2},{4,5},{5,4},{6,7},{7,6},{8,9},{9,8},{10,11... | collective-permute-start | bytes 1572872 | tf_op jit(solution)/shard_map/ppermute | solution.py:23
  57.1 7.0 %collective-permute-start.11 = (bf16[4,256,128]{2,1,0:T(8,128)(2,1)S(1)}, bf16[4,256,128]{2,1,0:T(8,128)(2,1)S(1)}, u32[]{:S(2)}, u32[]{:S(2)}) collective-permute-start(bf16[4,256,128]{2,1,0:T(8,128)(2,1)S(1)} %get-tuple-element.28), channel_id=1, source_target_pairs={{0,2},{1,7},{2,0},{3,5},{4,6},{5,3},{6,4},{7,1},{8,10},{9,15},{10,... | collective-permute-start | bytes 786440 | tf_op jit(solution)/shard_map/ppermute | solution.py:23
  58.7 8.0 %copy-start = (bf16[1024,128]{1,0:T(8,128)(2,1)S(1)}, bf16[1024,128]{1,0:T(8,128)(2,1)}, u32[]{:S(2)}) copy-start(bf16[1024,128]{1,0:T(8,128)(2,1)} %cotangent.1) | copy-start | bytes 786436
  58.8 7.8 %collective-permute-start.12 = (bf16[4,256,128]{2,1,0:T(8,128)(2,1)S(1)}, bf16[4,256,128]{2,1,0:T(8,128)(2,1)S(1)}, u32[]{:S(2)}, u32[]{:S(2)}) collective-permute-start(bf16[4,256,128]{2,1,0:T(8,128)(2,1)S(1)} %fusion.1), channel_id=1, source_target_pairs={{0,6},{1,3},{2,4},{3,1},{4,2},{5,7},{6,0},{7,5},{8,14},{9,11},{10,... | collective-permute-start | bytes 786440 | tf_op jit(solution)/shard_map/ppermute | solution.py:23
  68.7 1.3 %collective-permute-start.13 = (f32[128,128]{1,0:T(8,128)S(1)}, f32[128,128]{1,0:T(8,128)S(1)}, u32[]{:S(2)}, u32[]{:S(2)}) collective-permute-start(f32[128,128]{1,0:T(8,128)S(1)} %get-tuple-element.23), channel_id=1, source_target_pairs={{0,1},{1,0},{2,3},{3,2},{4,5},{5,4},{6,7},{7,6},{8,9},{9,8},{10,11... | collective-permute-start | bytes 196616 | tf_op jit(solution)/shard_map/ppermute | solution.py:23
  69.9 5.2 %collective-permute-start.15 = (bf16[128,128]{1,0:T(8,128)(2,1)S(1)}, bf16[128,128]{1,0:T(8,128)(2,1)S(1)}, u32[]{:S(2)}, u32[]{:S(2)}) collective-permute-start(bf16[128,128]{1,0:T(8,128)(2,1)S(1)} %add_convert_fusion.1), channel_id=1, source_target_pairs={{0,2},{1,7},{2,4},{3,1},{4,6},{5,3},{6,0},{7,5},{8,10},{9,15},{10,... | collective-permute-start | bytes 98312 | tf_op jit(solution)/shard_map/ppermute | solution.py:23
  70.4 6.3 %collective-permute-start.14 = (bf16[128,128]{1,0:T(8,128)(2,1)S(1)}, bf16[128,128]{1,0:T(8,128)(2,1)S(1)}, u32[]{:S(2)}, u32[]{:S(2)}) collective-permute-start(bf16[128,128]{1,0:T(8,128)(2,1)S(1)} %add_convert_fusion.1), channel_id=1, source_target_pairs={{0,4},{1,5},{2,6},{3,7},{4,0},{5,1},{6,2},{7,3},{8,12},{9,13},{10,... | collective-permute-start | bytes 98312 | tf_op jit(solution)/shard_map/ppermute | solution.py:23
  75.1 1.5 %collective-permute-start.16 = (bf16[128,128]{1,0:T(8,128)(2,1)S(1)}, bf16[128,128]{1,0:T(8,128)(2,1)S(1)}, u32[]{:S(2)}, u32[]{:S(2)}) collective-permute-start(bf16[128,128]{1,0:T(8,128)(2,1)S(1)} %collective-permute-done.15), channel_id=1, source_target_pairs={{0,1},{1,0},{2,3},{3,2},{4,5},{5,4},{6,7},{7,6},{8,9},{9,8},{10,11... | collective-permute-start | bytes 98312 | tf_op jit(solution)/shard_map/ppermute | solution.py:23
  76.7 6.8 %collective-permute-start.18 = (bf16[128,128]{1,0:T(8,128)(2,1)S(1)}, bf16[128,128]{1,0:T(8,128)(2,1)S(1)}, u32[]{:S(2)}, u32[]{:S(2)}) collective-permute-start(bf16[128,128]{1,0:T(8,128)(2,1)S(1)} %get-tuple-element.24), channel_id=1, source_target_pairs={{0,8},{1,25},{2,10},{3,27},{4,12},{5,29},{6,14},{7,31},{8,16},{9,1... | collective-permute-start | bytes 98312 | tf_op jit(solution)/shard_map/ppermute | solution.py:23
  77.3 8.0 %collective-permute-start.17 = (bf16[128,128]{1,0:T(8,128)(2,1)S(1)}, bf16[128,128]{1,0:T(8,128)(2,1)S(1)}, u32[]{:S(2)}, u32[]{:S(2)}) collective-permute-start(bf16[128,128]{1,0:T(8,128)(2,1)S(1)} %get-tuple-element.24), channel_id=1, source_target_pairs={{0,16},{1,17},{2,18},{3,19},{4,20},{5,21},{6,22},{7,23},{8,24},{9,... | collective-permute-start | bytes 98312 | tf_op jit(solution)/shard_map/ppermute | solution.py:23
  83.5 1.8 %collective-permute-start.19 = (bf16[128,128]{1,0:T(8,128)(2,1)S(1)}, bf16[128,128]{1,0:T(8,128)(2,1)S(1)}, u32[]{:S(2)}, u32[]{:S(2)}) collective-permute-start(bf16[128,128]{1,0:T(8,128)(2,1)S(1)} %collective-permute-done.18), channel_id=1, source_target_pairs={{0,1},{1,0},{2,3},{3,2},{4,5},{5,4},{6,7},{7,6},{8,9},{9,8},{10,11... | collective-permute-start | bytes 98312 | tf_op jit(solution)/shard_map/ppermute | solution.py:23
  85.3 5.4 %collective-permute-start.21 = (bf16[128,128]{1,0:T(8,128)(2,1)S(1)}, bf16[128,128]{1,0:T(8,128)(2,1)S(1)}, u32[]{:S(2)}, u32[]{:S(2)}) collective-permute-start(bf16[128,128]{1,0:T(8,128)(2,1)S(1)} %fusion.23), channel_id=1, source_target_pairs={{0,32},{1,97},{2,34},{3,99},{4,36},{5,101},{6,38},{7,103},{8,40},{... | collective-permute-start | bytes 98312 | tf_op jit(solution)/shard_map/ppermute | solution.py:23
  86.1 5.4 %collective-permute-start.20 = (bf16[128,128]{1,0:T(8,128)(2,1)S(1)}, bf16[128,128]{1,0:T(8,128)(2,1)S(1)}, u32[]{:S(2)}, u32[]{:S(2)}) collective-permute-start(bf16[128,128]{1,0:T(8,128)(2,1)S(1)} %fusion.23), channel_id=1, source_target_pairs={{0,64},{1,65},{2,66},{3,67},{4,68},{5,69},{6,70},{7,71},{8,72},{9,... | collective-permute-start | bytes 98312 | tf_op jit(solution)/shard_map/ppermute | solution.py:23
  90.7 1.2 %collective-permute-start.22 = (bf16[128,128]{1,0:T(8,128)(2,1)S(1)}, bf16[128,128]{1,0:T(8,128)(2,1)S(1)}, u32[]{:S(2)}, u32[]{:S(2)}) collective-permute-start(bf16[128,128]{1,0:T(8,128)(2,1)S(1)} %collective-permute-done.21), channel_id=1, source_target_pairs={{0,1},{1,0},{2,3},{3,2},{4,5},{5,4},{6,7},{7,6},{8,9},{9,8},{10,11... | collective-permute-start | bytes 98312 | tf_op jit(solution)/shard_map/ppermute | solution.py:23
  (5 other events, 29.6 us)

commit v6 on v5

--- a/solution.py
+++ b/solution.py
@@ -148,20 +148,24 @@
     )(meta, *args)
 
 
+def two_parts(v):
+    high = v.astype(BF)
+    return high, (v - high.astype(F32)).astype(BF)
+
+
 def finish_kernel(hidden, weight, cotangent, node_out, partial):
-    w = weight[...].astype(F32)
+    w = weight[...]
     grad = jnp.zeros((128, 128), F32)
     for i in range(4):
-        h = hidden[i]
-        pre = jnp.dot(h, w, precision=lax.Precision.HIGHEST, preferred_element_type=F32)
+        parts = two_parts(hidden[i])
+        pre = sum(jnp.dot(part, w, preferred_element_type=F32) for part in parts)
         sig = 1.0 / (1.0 + jnp.exp(-pre))
         span = pl.ds(i * 256, 256)
         node_out[span, :] = (pre * sig).astype(BF)
         slope = sig * (1.0 + pre * (1.0 - sig))
-        pre_grad = (cotangent[span, :].astype(F32) * slope).astype(BF).astype(F32)
-        grad = grad + lax.dot_general(
-            h, pre_grad, (((0,), (0,)), ((), ())), precision=lax.Precision.HIGHEST, preferred_element_type=F32
-        )
+        pre_grad = (cotangent[span, :].astype(F32) * slope).astype(BF)
+        for part in parts:
+            grad = grad + lax.dot_general(part, pre_grad, (((0,), (0,)), ((), ())), preferred_element_type=F32)
     partial[...] = grad
 
 

time: 93.9 us -> 93.3 us (level)
  starting transfers between devices: 33.5 us -> 31.5 us
  waiting for transfers between devices: 30.4 us -> 31.9 us
    ppermute x23, starting transfers between devices: 33.5 us -> 31.5 us  [permute(): return lax.ppermute(a, ('row', 'col'), pairs)]
    ppermute x23, waiting for transfers between devices: 30.4 us -> 31.9 us  [permute(): return lax.ppermute(a, ('row', 'col'), pairs)]
  transfers between devices with their start and end apart: 23 -> 23, of which waited for: 16 -> 15; matrix products, arithmetic and copies ran while one was open for 4% -> 5% of each run, Pallas kernels for 17% -> 17%
where the time goes in v6:
time: 93.3 us; the launch traced here: 92.2 us
  waiting for transfers between devices  31.9 us (34%)
  starting transfers between devices  31.5 us (34%)
  Pallas kernels  21.7 us (23%)
  other arithmetic  4.95 us (5%)
  local copies, waits for them, and re-layouts  1.18 us (1%)
  between operations  0.98 us (1%)
    ppermute x23, waiting for transfers between devices, permute(): return lax.ppermute(a, ('row', 'col'), pairs)  31.9 us
    ppermute x23, starting transfers between devices, permute(): return lax.ppermute(a, ('row', 'col'), pairs)  31.5 us
    pallas_call x4, Pallas kernels, spmm(): pl.pallas_call(functools.partial(spmm_kernel, phase), out_shape=out, in_s...  20.4 us
  transfers between devices with their start and end apart: 23, of which 15 were waited for; matrix products, arithmetic and copies ran while one was open for 5% of the time, Pallas kernels for 17%

profile of v6, /device:TPU:0, one launch (start us, length us, event | category | flops | bytes accessed | tf_op | source)
XLA Modules:
  0.0 92.2 jit_solution(6230328173135559632)
XLA Ops:
  1.7 1.6 %collective-permute-start.2 = (bf16[4,128,256]{2,1,0:T(8,128)(2,1)S(1)}, bf16[4,128,256]{2,1,0:T(8,128)(2,1)S(1)}, u32[]{:S(2)}, u32[]{:S(2)}) collective-permute-start(bf16[4,128,256]{2,1,0:T(8,128)(2,1)S(1)} %transposed.1), channel_id=1, source_target_pairs={{0,8},{1,33},{2,10},{3,35},{4,12},{5,37},{6,14},{7,39},{8,16},{9,4... | collective-permute-start | bytes 786440 | tf_op jit(solution)/shard_map/ppermute | solution.py:23
  3.3 1.7 %collective-permute-start.1 = (bf16[4,128,256]{2,1,0:T(8,128)(2,1)S(1)}, bf16[4,128,256]{2,1,0:T(8,128)(2,1)S(1)}, u32[]{:S(2)}, u32[]{:S(2)}) collective-permute-start(bf16[4,128,256]{2,1,0:T(8,128)(2,1)S(1)} %transposed.1), channel_id=1, source_target_pairs={{0,24},{1,97},{2,26},{3,99},{4,28},{5,101},{6,30},{7,103},{8,0},{9... | collective-permute-start | bytes 786440 | tf_op jit(solution)/shard_map/ppermute | solution.py:23
  5.0 1.9 %collective-permute-start = (bf16[4,128,256]{2,1,0:T(8,128)(2,1)S(1)}, bf16[4,128,256]{2,1,0:T(8,128)(2,1)S(1)}, u32[]{:S(2)}, u32[]{:S(2)}) collective-permute-start(bf16[4,128,256]{2,1,0:T(8,128)(2,1)S(1)} %transposed.1), channel_id=1, source_target_pairs={{0,16},{1,65},{2,18},{3,67},{4,20},{5,69},{6,22},{7,71},{8,24},{9,... | collective-permute-start | bytes 786440 | tf_op jit(solution)/shard_map/ppermute | solution.py:23
  10.2 4.7 %collective-permute-start.5 = (bf16[12,128,256]{2,1,0:T(8,128)(2,1)S(1)}, bf16[12,128,256]{2,1,0:T(8,128)(2,1)S(1)}, u32[]{:S(2)}, u32[]{:S(2)}) collective-permute-start(bf16[12,128,256]{2,1,0:T(8,128)(2,1)S(1)} %pad_maximum_fusion.2), channel_id=1, source_target_pairs={{0,96},{1,25},{2,98},{3,27},{4,100},{5,29},{6,102},{7,31},{8,104},... | collective-permute-start | bytes 2359304 | tf_op jit(solution)/shard_map/ppermute | solution.py:23
  15.2 1.6 %collective-permute-start.7 = (bf16[4,128,256]{2,1,0:T(8,128)(2,1)S(1)}, bf16[4,128,256]{2,1,0:T(8,128)(2,1)S(1)}, u32[]{:S(2)}, u32[]{:S(2)}) collective-permute-start(bf16[4,128,256]{2,1,0:T(8,128)(2,1)S(1)} %collective-permute-done), channel_id=1, source_target_pairs={{0,64},{1,17},{2,66},{3,19},{4,68},{5,21},{6,70},{7,23},{8,72},{9,... | collective-permute-start | bytes 786440 | tf_op jit(solution)/shard_map/ppermute | solution.py:23
  17.0 4.9 %spmm_phase0.1.rest_0_ = f32[32,256,128]{2,1,0:T(8,128)S(1)} custom-call(s32[5,256]{1,0:T(8,128)S(1)} %pad_add_fusion.meta, s32[256,256]{1,0:T(8,128)S(1)} %bitcast.38, s32[256,256]{1,0:T(8,128)S(1)} %bitcast.42, bf16[256,256]{1,0:T(8,128)(2,1)S(1)} %bitcast.46, bf16[16,128,256]{2,1,0:T(8,128)(2,1)S(1)} %pad_maximum_fusion.1.pieces), custom_call_target="tpu_custom_call" | custom-call | flops 5000000000 | bytes 1048576 | tf_op jit(solution)/shard_map/spmm_phase0/pallas_call | solution.py:138
  21.9 5.4 %collective-permute-done.5 = bf16[12,128,256]{2,1,0:T(8,128)(2,1)S(1)} collective-permute-done((bf16[12,128,256]{2,1,0:T(8,128)(2,1)S(1)}, bf16[12,128,256]{2,1,0:T(8,128)(2,1)S(1)}, u32[]{:S(2)}, u32[]{:S(2)}) %collective-permute-start.5) | collective-permute-done | bytes 786464 | tf_op jit(solution)/shard_map/ppermute | solution.py:23
  27.3 3.7 %collective-permute-done.3 = bf16[12,128,256]{2,1,0:T(8,128)(2,1)S(1)} collective-permute-done((bf16[12,128,256]{2,1,0:T(8,128)(2,1)S(1)}, bf16[12,128,256]{2,1,0:T(8,128)(2,1)S(1)}, u32[]{:S(2)}, u32[]{:S(2)}) %collective-permute-start.3) | collective-permute-done | bytes 786464 | tf_op jit(solution)/shard_map/ppermute | solution.py:23
  31.3 2.0 %collective-permute-start.4 = (bf16[10,128,256]{2,1,0:T(8,128)(2,1)S(1)}, bf16[10,128,256]{2,1,0:T(8,128)(2,1)S(1)}, u32[]{:S(2)}, u32[]{:S(2)}) collective-permute-start(bf16[10,128,256]{2,1,0:T(8,128)(2,1)S(1)} %get-tuple-element.31), channel_id=1, source_target_pairs={{0,32},{1,9},{2,34},{3,11},{4,36},{5,13},{6,38},{7,15},{8,40},{9,1... | collective-permute-start | bytes 1966088 | tf_op jit(solution)/shard_map/ppermute | solution.py:23
  33.4 7.2 %spmm_phase1.1.rest_0_ = f32[32,256,128]{2,1,0:T(8,128)S(1)} custom-call(s32[5,256]{1,0:T(8,128)S(1)} %pad_add_fusion.meta, s32[256,256]{1,0:T(8,128)S(1)} %bitcast.39, s32[256,256]{1,0:T(8,128)S(1)} %bitcast.43, bf16[256,256]{1,0:T(8,128)(2,1)S(1)} %bitcast.47, bf16[24,128,256]{2,1,0:T(8,128)(2,1)S(1)} %pad_maximum_fusion.pieces, ...), custom_call_target="tpu_custom_call", output_to_operand_aliasing={{}: (5, {})} | custom-call | flops 7500000256 | bytes 1048576 | tf_op jit(solution)/shard_map/spmm_phase1/pallas_call | solution.py:138
  40.5 2.5 %collective-permute-done.4 = bf16[10,128,256]{2,1,0:T(8,128)(2,1)S(1)} collective-permute-done((bf16[10,128,256]{2,1,0:T(8,128)(2,1)S(1)}, bf16[10,128,256]{2,1,0:T(8,128)(2,1)S(1)}, u32[]{:S(2)}, u32[]{:S(2)}) %collective-permute-start.4) | collective-permute-done | bytes 655392 | tf_op jit(solution)/shard_map/ppermute | solution.py:23
  43.3 4.5 %spmm_phase2.1 = (f32[32,256,128]{2,1,0:T(8,128)S(1)}, f32[2,4,256,128]{3,2,1,0:T(8,128)S(1)}, bf16[2,4,256,128]{3,2,1,0:T(8,128)(2,1)S(1)}) custom-call(s32[5,256]{1,0:T(8,128)S(1)} %pad_add_fusion.meta, s32[256,256]{1,0:T(8,128)S(1)} %bitcast.40, s32[256,256]{1,0:T(8,128)S(1)} %bitcast.44, ...), custom_call_target="tpu_custom_call", output_to_operand_aliasing={{0}: (5, {})} | custom-call | flops 3750000128 | bytes 1048576 | tf_op jit(solution)/shard_map/spmm_phase2/pallas_call | solution.py:138
  47.8 1.9 %collective-permute-done.8 = bf16[2,4,256,128]{3,2,1,0:T(8,128)(2,1)S(1)} collective-permute-done((bf16[2,4,256,128]{3,2,1,0:T(8,128)(2,1)S(1)}, bf16[2,4,256,128]{3,2,1,0:T(8,128)(2,1)S(1)}, u32[]{:S(2)}, u32[]{:S(2)}) %collective-permute-start.8) | collective-permute-done | bytes 524320 | tf_op jit(solution)/shard_map/ppermute | solution.py:23
  51.1 3.9 %spmm_phase3.1 = (f32[32,256,128]{2,1,0:T(8,128)S(1)}, f32[2,4,256,128]{3,2,1,0:T(8,128)S(1)}, bf16[2,4,256,128]{3,2,1,0:T(8,128)(2,1)S(1)}) custom-call(s32[5,256]{1,0:T(8,128)S(1)} %pad_add_fusion.meta, s32[256,256]{1,0:T(8,128)S(1)} %bitcast.41, s32[256,256]{1,0:T(8,128)S(1)} %bitcast.45, ...), custom_call_target="tpu_custom_call", output_to_operand_aliasing={{0}: (5, {})} | custom-call | flops 3750000128 | bytes 1048576 | tf_op jit(solution)/shard_map/spmm_phase3/pallas_call | solution.py:138
  55.0 1.3 %collective-permute-done.9 = bf16[4,256,128]{2,1,0:T(8,128)(2,1)S(1)} collective-permute-done((bf16[4,256,128]{2,1,0:T(8,128)(2,1)S(1)}, bf16[4,256,128]{2,1,0:T(8,128)(2,1)S(1)}, u32[]{:S(2)}, u32[]{:S(2)}) %collective-permute-start.9) | collective-permute-done | bytes 262176 | tf_op jit(solution)/shard_map/ppermute | solution.py:23
  58.8 3.0 %collective-permute-start.12 = (bf16[4,256,128]{2,1,0:T(8,128)(2,1)S(1)}, bf16[4,256,128]{2,1,0:T(8,128)(2,1)S(1)}, u32[]{:S(2)}, u32[]{:S(2)}) collective-permute-start(bf16[4,256,128]{2,1,0:T(8,128)(2,1)S(1)} %fusion.1), channel_id=1, source_target_pairs={{0,6},{1,3},{2,4},{3,1},{4,2},{5,7},{6,0},{7,5},{8,14},{9,11},{10,... | collective-permute-start | bytes 786440 | tf_op jit(solution)/shard_map/ppermute | solution.py:23
  61.8 2.2 %collective-permute-done.11 = bf16[4,256,128]{2,1,0:T(8,128)(2,1)S(1)} collective-permute-done((bf16[4,256,128]{2,1,0:T(8,128)(2,1)S(1)}, bf16[4,256,128]{2,1,0:T(8,128)(2,1)S(1)}, u32[]{:S(2)}, u32[]{:S(2)}) %collective-permute-start.11) | collective-permute-done | bytes 262176 | tf_op jit(solution)/shard_map/ppermute | solution.py:23
  64.1 2.5 %collective-permute-done.12 = bf16[4,256,128]{2,1,0:T(8,128)(2,1)S(1)} collective-permute-done((bf16[4,256,128]{2,1,0:T(8,128)(2,1)S(1)}, bf16[4,256,128]{2,1,0:T(8,128)(2,1)S(1)}, u32[]{:S(2)}, u32[]{:S(2)}) %collective-permute-start.12) | collective-permute-done | bytes 262176 | tf_op jit(solution)/shard_map/ppermute | solution.py:23
  67.9 1.3 %collective-permute-done.13 = f32[128,128]{1,0:T(8,128)S(1)} collective-permute-done((f32[128,128]{1,0:T(8,128)S(1)}, f32[128,128]{1,0:T(8,128)S(1)}, u32[]{:S(2)}, u32[]{:S(2)}) %collective-permute-start.13) | collective-permute-done | bytes 65568 | tf_op jit(solution)/shard_map/ppermute | solution.py:23
  70.1 3.6 %collective-permute-start.14 = (bf16[128,128]{1,0:T(8,128)(2,1)S(1)}, bf16[128,128]{1,0:T(8,128)(2,1)S(1)}, u32[]{:S(2)}, u32[]{:S(2)}) collective-permute-start(bf16[128,128]{1,0:T(8,128)(2,1)S(1)} %add_convert_fusion.1), channel_id=1, source_target_pairs={{0,4},{1,5},{2,6},{3,7},{4,0},{5,1},{6,2},{7,3},{8,12},{9,13},{10,... | collective-permute-start | bytes 98312 | tf_op jit(solution)/shard_map/ppermute | solution.py:23
  74.3 1.5 %collective-permute-done.14 = bf16[128,128]{1,0:T(8,128)(2,1)S(1)} collective-permute-done((bf16[128,128]{1,0:T(8,128)(2,1)S(1)}, bf16[128,128]{1,0:T(8,128)(2,1)S(1)}, u32[]{:S(2)}, u32[]{:S(2)}) %collective-permute-start.14) | collective-permute-done | bytes 32800 | tf_op jit(solution)/shard_map/ppermute | solution.py:23
  76.0 6.3 %collective-permute-start.17 = (bf16[128,128]{1,0:T(8,128)(2,1)S(1)}, bf16[128,128]{1,0:T(8,128)(2,1)S(1)}, u32[]{:S(2)}, u32[]{:S(2)}) collective-permute-start(bf16[128,128]{1,0:T(8,128)(2,1)S(1)} %get-tuple-element.24), channel_id=1, source_target_pairs={{0,16},{1,17},{2,18},{3,19},{4,20},{5,21},{6,22},{7,23},{8,24},{9,... | collective-permute-start | bytes 98312 | tf_op jit(solution)/shard_map/ppermute | solution.py:23
  82.7 1.8 %collective-permute-done.17 = bf16[128,128]{1,0:T(8,128)(2,1)S(1)} collective-permute-done((bf16[128,128]{1,0:T(8,128)(2,1)S(1)}, bf16[128,128]{1,0:T(8,128)(2,1)S(1)}, u32[]{:S(2)}, u32[]{:S(2)}) %collective-permute-start.17) | collective-permute-done | bytes 32800 | tf_op jit(solution)/shard_map/ppermute | solution.py:23
  85.6 4.7 %collective-permute-done.21 = bf16[128,128]{1,0:T(8,128)(2,1)S(1)} collective-permute-done((bf16[128,128]{1,0:T(8,128)(2,1)S(1)}, bf16[128,128]{1,0:T(8,128)(2,1)S(1)}, u32[]{:S(2)}, u32[]{:S(2)}) %collective-permute-start.21) | collective-permute-done | bytes 32800 | tf_op jit(solution)/shard_map/ppermute | solution.py:23
  (70 shorter events, 15.5 us)
Async XLA Ops:
  1.7 8.4 %collective-permute-start.2 = (bf16[4,128,256]{2,1,0:T(8,128)(2,1)S(1)}, bf16[4,128,256]{2,1,0:T(8,128)(2,1)S(1)}, u32[]{:S(2)}, u32[]{:S(2)}) collective-permute-start(bf16[4,128,256]{2,1,0:T(8,128)(2,1)S(1)} %transposed.1), channel_id=1, source_target_pairs={{0,8},{1,33},{2,10},{3,35},{4,12},{5,37},{6,14},{7,39},{8,16},{9,4... | collective-permute-start | bytes 786440 | tf_op jit(solution)/shard_map/ppermute | solution.py:23
  3.3 6.8 %collective-permute-start.1 = (bf16[4,128,256]{2,1,0:T(8,128)(2,1)S(1)}, bf16[4,128,256]{2,1,0:T(8,128)(2,1)S(1)}, u32[]{:S(2)}, u32[]{:S(2)}) collective-permute-start(bf16[4,128,256]{2,1,0:T(8,128)(2,1)S(1)} %transposed.1), channel_id=1, source_target_pairs={{0,24},{1,97},{2,26},{3,99},{4,28},{5,101},{6,30},{7,103},{8,0},{9... | collective-permute-start | bytes 786440 | tf_op jit(solution)/shard_map/ppermute | solution.py:23
  5.0 10.2 %collective-permute-start = (bf16[4,128,256]{2,1,0:T(8,128)(2,1)S(1)}, bf16[4,128,256]{2,1,0:T(8,128)(2,1)S(1)}, u32[]{:S(2)}, u32[]{:S(2)}) collective-permute-start(bf16[4,128,256]{2,1,0:T(8,128)(2,1)S(1)} %transposed.1), channel_id=1, source_target_pairs={{0,16},{1,65},{2,18},{3,67},{4,20},{5,69},{6,22},{7,71},{8,24},{9,... | collective-permute-start | bytes 786440 | tf_op jit(solution)/shard_map/ppermute | solution.py:23
  10.2 17.1 %collective-permute-start.5 = (bf16[12,128,256]{2,1,0:T(8,128)(2,1)S(1)}, bf16[12,128,256]{2,1,0:T(8,128)(2,1)S(1)}, u32[]{:S(2)}, u32[]{:S(2)}) collective-permute-start(bf16[12,128,256]{2,1,0:T(8,128)(2,1)S(1)} %pad_maximum_fusion.2), channel_id=1, source_target_pairs={{0,96},{1,25},{2,98},{3,27},{4,100},{5,29},{6,102},{7,31},{8,104},... | collective-permute-start | bytes 2359304 | tf_op jit(solution)/shard_map/ppermute | solution.py:23
  15.0 16.0 %collective-permute-start.3 = (bf16[12,128,256]{2,1,0:T(8,128)(2,1)S(1)}, bf16[12,128,256]{2,1,0:T(8,128)(2,1)S(1)}, u32[]{:S(2)}, u32[]{:S(2)}) collective-permute-start(bf16[12,128,256]{2,1,0:T(8,128)(2,1)S(1)} %pad_maximum_fusion.2), channel_id=1, source_target_pairs={{0,32},{1,9},{2,34},{3,11},{4,36},{5,13},{6,38},{7,15},{8,40},{9,1... | collective-permute-start | bytes 2359304 | tf_op jit(solution)/shard_map/ppermute | solution.py:23
  15.2 28.0 %collective-permute-start.7 = (bf16[4,128,256]{2,1,0:T(8,128)(2,1)S(1)}, bf16[4,128,256]{2,1,0:T(8,128)(2,1)S(1)}, u32[]{:S(2)}, u32[]{:S(2)}) collective-permute-start(bf16[4,128,256]{2,1,0:T(8,128)(2,1)S(1)} %collective-permute-done), channel_id=1, source_target_pairs={{0,64},{1,17},{2,66},{3,19},{4,68},{5,21},{6,70},{7,23},{8,72},{9,... | collective-permute-start | bytes 786440 | tf_op jit(solution)/shard_map/ppermute | solution.py:23
  31.1 12.0 %collective-permute-start.6 = (bf16[10,128,256]{2,1,0:T(8,128)(2,1)S(1)}, bf16[10,128,256]{2,1,0:T(8,128)(2,1)S(1)}, u32[]{:S(2)}, u32[]{:S(2)}) collective-permute-start(bf16[10,128,256]{2,1,0:T(8,128)(2,1)S(1)} %get-tuple-element.30), channel_id=1, source_target_pairs={{0,96},{1,25},{2,98},{3,27},{4,100},{5,29},{6,102},{7,31},{8,104},... | collective-permute-start | bytes 1966088 | tf_op jit(solution)/shard_map/ppermute | solution.py:23
  31.3 11.8 %collective-permute-start.4 = (bf16[10,128,256]{2,1,0:T(8,128)(2,1)S(1)}, bf16[10,128,256]{2,1,0:T(8,128)(2,1)S(1)}, u32[]{:S(2)}, u32[]{:S(2)}) collective-permute-start(bf16[10,128,256]{2,1,0:T(8,128)(2,1)S(1)} %get-tuple-element.31), channel_id=1, source_target_pairs={{0,32},{1,9},{2,34},{3,11},{4,36},{5,13},{6,38},{7,15},{8,40},{9,1... | collective-permute-start | bytes 1966088 | tf_op jit(solution)/shard_map/ppermute | solution.py:23
  47.7 2.0 %collective-permute-start.8 = (bf16[2,4,256,128]{3,2,1,0:T(8,128)(2,1)S(1)}, bf16[2,4,256,128]{3,2,1,0:T(8,128)(2,1)S(1)}, u32[]{:S(2)}, u32[]{:S(2)}) collective-permute-start(bf16[2,4,256,128]{3,2,1,0:T(8,128)(2,1)S(1)} %get-tuple-element.14), channel_id=1, source_target_pairs={{0,1},{1,0},{2,3},{3,2},{4,5},{5,4},{6,7},{7,6},{8,9},{9,8},{10,11... | collective-permute-start | bytes 1572872 | tf_op jit(solution)/shard_map/ppermute | solution.py:23
  49.9 6.5 %collective-permute-start.9 = (bf16[4,256,128]{2,1,0:T(8,128)(2,1)S(1)}, bf16[4,256,128]{2,1,0:T(8,128)(2,1)S(1)}, u32[]{:S(2)}, u32[]{:S(2)}) collective-permute-start(bf16[4,256,128]{2,1,0:T(8,128)(2,1)S(1)} %get-tuple-element.29), channel_id=1, source_target_pairs={{0,2},{1,7},{2,0},{3,5},{4,6},{5,3},{6,4},{7,1},{8,10},{9,15},{10,... | collective-permute-start | bytes 786440 | tf_op jit(solution)/shard_map/ppermute | solution.py:23
  56.4 2.3 %collective-permute-start.10 = (bf16[2,4,256,128]{3,2,1,0:T(8,128)(2,1)S(1)}, bf16[2,4,256,128]{3,2,1,0:T(8,128)(2,1)S(1)}, u32[]{:S(2)}, u32[]{:S(2)}) collective-permute-start(bf16[2,4,256,128]{3,2,1,0:T(8,128)(2,1)S(1)} %get-tuple-element.20), channel_id=1, source_target_pairs={{0,1},{1,0},{2,3},{3,2},{4,5},{5,4},{6,7},{7,6},{8,9},{9,8},{10,11... | collective-permute-start | bytes 1572872 | tf_op jit(solution)/shard_map/ppermute | solution.py:23
  57.1 7.0 %collective-permute-start.11 = (bf16[4,256,128]{2,1,0:T(8,128)(2,1)S(1)}, bf16[4,256,128]{2,1,0:T(8,128)(2,1)S(1)}, u32[]{:S(2)}, u32[]{:S(2)}) collective-permute-start(bf16[4,256,128]{2,1,0:T(8,128)(2,1)S(1)} %get-tuple-element.28), channel_id=1, source_target_pairs={{0,2},{1,7},{2,0},{3,5},{4,6},{5,3},{6,4},{7,1},{8,10},{9,15},{10,... | collective-permute-start | bytes 786440 | tf_op jit(solution)/shard_map/ppermute | solution.py:23
  58.7 8.0 %copy-start = (bf16[1024,128]{1,0:T(8,128)(2,1)S(1)}, bf16[1024,128]{1,0:T(8,128)(2,1)}, u32[]{:S(2)}) copy-start(bf16[1024,128]{1,0:T(8,128)(2,1)} %cotangent.1) | copy-start | bytes 786436
  58.8 7.8 %collective-permute-start.12 = (bf16[4,256,128]{2,1,0:T(8,128)(2,1)S(1)}, bf16[4,256,128]{2,1,0:T(8,128)(2,1)S(1)}, u32[]{:S(2)}, u32[]{:S(2)}) collective-permute-start(bf16[4,256,128]{2,1,0:T(8,128)(2,1)S(1)} %fusion.1), channel_id=1, source_target_pairs={{0,6},{1,3},{2,4},{3,1},{4,2},{5,7},{6,0},{7,5},{8,14},{9,11},{10,... | collective-permute-start | bytes 786440 | tf_op jit(solution)/shard_map/ppermute | solution.py:23
  67.9 1.3 %collective-permute-start.13 = (f32[128,128]{1,0:T(8,128)S(1)}, f32[128,128]{1,0:T(8,128)S(1)}, u32[]{:S(2)}, u32[]{:S(2)}) collective-permute-start(f32[128,128]{1,0:T(8,128)S(1)} %get-tuple-element.23), channel_id=1, source_target_pairs={{0,1},{1,0},{2,3},{3,2},{4,5},{5,4},{6,7},{7,6},{8,9},{9,8},{10,11... | collective-permute-start | bytes 196616 | tf_op jit(solution)/shard_map/ppermute | solution.py:23
  69.1 5.2 %collective-permute-start.15 = (bf16[128,128]{1,0:T(8,128)(2,1)S(1)}, bf16[128,128]{1,0:T(8,128)(2,1)S(1)}, u32[]{:S(2)}, u32[]{:S(2)}) collective-permute-start(bf16[128,128]{1,0:T(8,128)(2,1)S(1)} %add_convert_fusion.1), channel_id=1, source_target_pairs={{0,2},{1,7},{2,4},{3,1},{4,6},{5,3},{6,0},{7,5},{8,10},{9,15},{10,... | collective-permute-start | bytes 98312 | tf_op jit(solution)/shard_map/ppermute | solution.py:23
  70.1 5.8 %collective-permute-start.14 = (bf16[128,128]{1,0:T(8,128)(2,1)S(1)}, bf16[128,128]{1,0:T(8,128)(2,1)S(1)}, u32[]{:S(2)}, u32[]{:S(2)}) collective-permute-start(bf16[128,128]{1,0:T(8,128)(2,1)S(1)} %add_convert_fusion.1), channel_id=1, source_target_pairs={{0,4},{1,5},{2,6},{3,7},{4,0},{5,1},{6,2},{7,3},{8,12},{9,13},{10,... | collective-permute-start | bytes 98312 | tf_op jit(solution)/shard_map/ppermute | solution.py:23
  74.3 1.5 %collective-permute-start.16 = (bf16[128,128]{1,0:T(8,128)(2,1)S(1)}, bf16[128,128]{1,0:T(8,128)(2,1)S(1)}, u32[]{:S(2)}, u32[]{:S(2)}) collective-permute-start(bf16[128,128]{1,0:T(8,128)(2,1)S(1)} %collective-permute-done.15), channel_id=1, source_target_pairs={{0,1},{1,0},{2,3},{3,2},{4,5},{5,4},{6,7},{7,6},{8,9},{9,8},{10,11... | collective-permute-start | bytes 98312 | tf_op jit(solution)/shard_map/ppermute | solution.py:23
  75.9 6.8 %collective-permute-start.18 = (bf16[128,128]{1,0:T(8,128)(2,1)S(1)}, bf16[128,128]{1,0:T(8,128)(2,1)S(1)}, u32[]{:S(2)}, u32[]{:S(2)}) collective-permute-start(bf16[128,128]{1,0:T(8,128)(2,1)S(1)} %get-tuple-element.24), channel_id=1, source_target_pairs={{0,8},{1,25},{2,10},{3,27},{4,12},{5,29},{6,14},{7,31},{8,16},{9,1... | collective-permute-start | bytes 98312 | tf_op jit(solution)/shard_map/ppermute | solution.py:23
  76.0 8.5 %collective-permute-start.17 = (bf16[128,128]{1,0:T(8,128)(2,1)S(1)}, bf16[128,128]{1,0:T(8,128)(2,1)S(1)}, u32[]{:S(2)}, u32[]{:S(2)}) collective-permute-start(bf16[128,128]{1,0:T(8,128)(2,1)S(1)} %get-tuple-element.24), channel_id=1, source_target_pairs={{0,16},{1,17},{2,18},{3,19},{4,20},{5,21},{6,22},{7,23},{8,24},{9,... | collective-permute-start | bytes 98312 | tf_op jit(solution)/shard_map/ppermute | solution.py:23
  82.7 1.8 %collective-permute-start.19 = (bf16[128,128]{1,0:T(8,128)(2,1)S(1)}, bf16[128,128]{1,0:T(8,128)(2,1)S(1)}, u32[]{:S(2)}, u32[]{:S(2)}) collective-permute-start(bf16[128,128]{1,0:T(8,128)(2,1)S(1)} %collective-permute-done.18), channel_id=1, source_target_pairs={{0,1},{1,0},{2,3},{3,2},{4,5},{5,4},{6,7},{7,6},{8,9},{9,8},{10,11... | collective-permute-start | bytes 98312 | tf_op jit(solution)/shard_map/ppermute | solution.py:23
  84.5 5.8 %collective-permute-start.21 = (bf16[128,128]{1,0:T(8,128)(2,1)S(1)}, bf16[128,128]{1,0:T(8,128)(2,1)S(1)}, u32[]{:S(2)}, u32[]{:S(2)}) collective-permute-start(bf16[128,128]{1,0:T(8,128)(2,1)S(1)} %fusion.23), channel_id=1, source_target_pairs={{0,32},{1,97},{2,34},{3,99},{4,36},{5,101},{6,38},{7,103},{8,40},{... | collective-permute-start | bytes 98312 | tf_op jit(solution)/shard_map/ppermute | solution.py:23
  84.6 5.7 %collective-permute-start.20 = (bf16[128,128]{1,0:T(8,128)(2,1)S(1)}, bf16[128,128]{1,0:T(8,128)(2,1)S(1)}, u32[]{:S(2)}, u32[]{:S(2)}) collective-permute-start(bf16[128,128]{1,0:T(8,128)(2,1)S(1)} %fusion.23), channel_id=1, source_target_pairs={{0,64},{1,65},{2,66},{3,67},{4,68},{5,69},{6,70},{7,71},{8,72},{9,... | collective-permute-start | bytes 98312 | tf_op jit(solution)/shard_map/ppermute | solution.py:23
  90.3 1.2 %collective-permute-start.22 = (bf16[128,128]{1,0:T(8,128)(2,1)S(1)}, bf16[128,128]{1,0:T(8,128)(2,1)S(1)}, u32[]{:S(2)}, u32[]{:S(2)}) collective-permute-start(bf16[128,128]{1,0:T(8,128)(2,1)S(1)} %collective-permute-done.21), channel_id=1, source_target_pairs={{0,1},{1,0},{2,3},{3,2},{4,5},{5,4},{6,7},{7,6},{8,9},{9,8},{10,11... | collective-permute-start | bytes 98312 | tf_op jit(solution)/shard_map/ppermute | solution.py:23
  (5 other events, 29.6 us)
